TPU v7x, 256 devices: a whole 4x4x8 slice. The times are simulated.
256 devices in a mesh: ctx: 64 (over y_hi, z, x), tp: 4 (over y_lo, core).
Axes of the slice: x: 4, y: 4 (y_hi: 2, y_lo: 2; y = y_hi * 2 + y_lo), z: 8, core: 2. Of those that a mesh axis runs over, the one named last changes fastest.
Arguments:
- queries: bfloat16 [8192, 2048], P('ctx', 'tp'), may hold values from -6 to 6
- key_rows: bfloat16 [8192, 512], P('ctx', 'tp'), may hold values from -6 to 6
- value_matrix: bfloat16 [8192, 512], P('ctx', 'tp'), may hold values from -6 to 6
- attention_out: bfloat16 [8192, 2048], P('ctx', 'tp'), may hold values from -6 to 6
- output_grad: bfloat16 [8192, 2048], P('ctx', 'tp'), may hold values from -6 to 6
- w_query: bfloat16 [2048, 2048], P(None, 'tp'), may hold values from -3 to 3
- key_weight: bfloat16 [2048, 512], P(None, 'tp'), may hold values from -3 to 3
- value_weight: bfloat16 [2048, 512], P(None, 'tp'), may hold values from -3 to 3
- span_pos: int32 [128], replicated, may hold values from 0 to 127, as said below
Outputs:
- input_grad: bfloat16 [8192, 2048], P('ctx', 'tp')
Inputs may be any that keep to these rules, and one draw needn't show every extreme that they name: Device d of ctx stores spans 2d and 2d + 1; their positions span_pos[2d] and span_pos[2d + 1] add up to 127, in either order; every position appears once.
All inputs are finite; a program needn't handle non-finite values.
Results may differ from a plain program's by a relative error of at most 0.0056.
Values may be sent and summed in bfloat16 or wider, within the bound.
No kernel may reach another device: no remote copies, remote signals or barrier semaphores. Data moves between devices by JAX's collectives and lax.ppermute only.
A program may use at most 64 MiB of HBM per device.

v0:
```python
import jax
import jax.numpy as jnp
from jax import lax
from jax.sharding import PartitionSpec as P

HEAD_SIZE = 128


def contract_last(left, right):
    return lax.dot_general(
        left, right, (((1,), (1,)), ((), ())), preferred_element_type=jnp.float32
    )


def contract_first(left, right):
    return lax.dot_general(
        left, right, (((0,), (0,)), ((), ())), preferred_element_type=jnp.float32
    )


def block_stats(query, query_pos, key_part, key_pos, running):
    run_max, run_sum = running
    raw_scores = contract_last(query, key_part) * HEAD_SIZE ** (-0.5)
    allowed = key_pos[None, :] <= query_pos[:, None]
    masked = jnp.where(allowed, raw_scores, -jnp.inf)
    new_max = jnp.maximum(run_max, jnp.max(masked, axis=1))
    run_sum = run_sum * jnp.exp(run_max - new_max) + jnp.sum(
        jnp.exp(masked - new_max[:, None]), axis=1
    )
    return (new_max, run_sum)


def block_grads(query, query_pos, grad_rows, log_totals, deltas, key_part, value_part, key_pos):
    score_scale = HEAD_SIZE ** (-0.5)
    raw_scores = contract_last(query, key_part) * score_scale
    allowed = key_pos[None, :] <= query_pos[:, None]
    weights = jnp.where(allowed, jnp.exp(raw_scores - log_totals[:, None]), 0.0)
    probs_low = weights.astype(jnp.bfloat16)
    grad_probs = contract_last(grad_rows, value_part)
    grad_scores = (weights * (grad_probs - deltas[:, None])).astype(jnp.bfloat16)
    part_query = jnp.dot(grad_scores, key_part, preferred_element_type=jnp.float32) * score_scale
    part_key = contract_first(grad_scores, query) * score_scale
    part_value = contract_first(probs_low, grad_rows)
    return (part_query, part_key, part_value)


def local(
    queries,
    key_rows,
    value_matrix,
    attention_out,
    output_grad,
    w_query,
    key_weight,
    value_weight,
    span_pos,
):
    tok_rows = queries.shape[0]
    span_len = tok_rows // 2
    group_width = queries.shape[1] // HEAD_SIZE
    query_count = span_len * group_width
    cycle_size = lax.axis_size("ctx")
    my_index = lax.axis_index("ctx")
    offsets = jnp.arange(span_len, dtype=jnp.int32)
    own_pos = lax.dynamic_slice_in_dim(span_pos, 2 * my_index, 2)
    query_parts, grad_parts, deltas, query_pos = ([], [], [], [])
    for half_index in range(2):
        low = half_index * span_len
        grad_half = output_grad[low : low + span_len].reshape(query_count, HEAD_SIZE)
        out_half = attention_out[low : low + span_len].reshape(query_count, HEAD_SIZE)
        query_parts.append(queries[low : low + span_len].reshape(query_count, HEAD_SIZE))
        grad_parts.append(grad_half)
        deltas.append(jnp.sum(grad_half.astype(jnp.float32) * out_half.astype(jnp.float32), axis=1))
        query_pos.append(jnp.repeat(own_pos[half_index] * span_len + offsets, group_width))
    start_stats = (
        jnp.full((query_count,), -jnp.inf, jnp.float32),
        jnp.zeros((query_count,), jnp.float32),
    )
    zero_rows = jnp.zeros((query_count, HEAD_SIZE), jnp.float32)
    keys_all, values_all = (
        lax.all_gather(key_rows, "ctx", axis=0, tiled=True),
        lax.all_gather(value_matrix, "ctx", axis=0, tiled=True),
    )
    total_rows = keys_all.shape[0]
    span_total = 2 * cycle_size
    span_ids = jnp.arange(span_total, dtype=jnp.int32)
    inverse = jnp.sum(
        jnp.where(span_pos[None, :] == span_ids[:, None], span_ids[None, :], 0), axis=1
    )
    sorted_keys = keys_all.reshape(span_total, span_len, HEAD_SIZE)[inverse].reshape(
        total_rows, HEAD_SIZE
    )
    sorted_values = values_all.reshape(span_total, span_len, HEAD_SIZE)[inverse].reshape(
        total_rows, HEAD_SIZE
    )
    key_block = min(1024, total_rows)
    block_offsets = jnp.arange(key_block, dtype=jnp.int32)
    log_totals = []
    block_counts = []
    for half_index in range(2):
        block_count = (own_pos[half_index] * span_len + span_len - 1) // key_block + 1
        block_counts.append(block_count)

        def sorted_stats(block_index, running):
            first_row = block_index * key_block
            key_part = lax.dynamic_slice_in_dim(sorted_keys, first_row, key_block, 0)
            return block_stats(
                query_parts[half_index],
                query_pos[half_index],
                key_part,
                first_row + block_offsets,
                running,
            )

        run_max, run_sum = lax.fori_loop(0, block_count, sorted_stats, start_stats)
        log_totals.append(run_max + jnp.log(run_sum))
    key_acc = jnp.zeros((total_rows, HEAD_SIZE), jnp.float32)
    value_acc = jnp.zeros((total_rows, HEAD_SIZE), jnp.float32)
    query_accs = []
    for half_index in range(2):

        def sorted_grads(block_index, loop_state):
            query_acc, key_acc, value_acc = loop_state
            first_row = block_index * key_block
            key_part = lax.dynamic_slice_in_dim(sorted_keys, first_row, key_block, 0)
            value_part = lax.dynamic_slice_in_dim(sorted_values, first_row, key_block, 0)
            part_query, part_key, part_value = block_grads(
                query_parts[half_index],
                query_pos[half_index],
                grad_parts[half_index],
                log_totals[half_index],
                deltas[half_index],
                key_part,
                value_part,
                first_row + block_offsets,
            )
            key_acc = lax.dynamic_update_slice_in_dim(
                key_acc,
                lax.dynamic_slice_in_dim(key_acc, first_row, key_block, 0) + part_key,
                first_row,
                0,
            )
            value_acc = lax.dynamic_update_slice_in_dim(
                value_acc,
                lax.dynamic_slice_in_dim(value_acc, first_row, key_block, 0) + part_value,
                first_row,
                0,
            )
            return (query_acc + part_query, key_acc, value_acc)

        query_acc, key_acc, value_acc = lax.fori_loop(
            0, block_counts[half_index], sorted_grads, (zero_rows, key_acc, value_acc)
        )
        query_accs.append(query_acc)
    key_stored = key_acc.reshape(span_total, span_len, HEAD_SIZE)[span_pos].reshape(
        total_rows, HEAD_SIZE
    )
    value_stored = value_acc.reshape(span_total, span_len, HEAD_SIZE)[span_pos].reshape(
        total_rows, HEAD_SIZE
    )
    key_grad, value_grad = (
        lax.psum_scatter(key_stored, "ctx", scatter_dimension=0, tiled=True),
        lax.psum_scatter(value_stored, "ctx", scatter_dimension=0, tiled=True),
    )
    grad_query = jnp.concatenate(
        [acc_part.reshape(span_len, group_width * HEAD_SIZE) for acc_part in query_accs], axis=0
    ).astype(jnp.bfloat16)
    grad_key = key_grad.astype(jnp.bfloat16)
    grad_value = value_grad.astype(jnp.bfloat16)
    partial_sum = (
        contract_last(grad_query, w_query)
        + contract_last(grad_key, key_weight)
        + contract_last(grad_value, value_weight)
    )
    return lax.psum_scatter(partial_sum, "tp", scatter_dimension=1, tiled=True).astype(jnp.bfloat16)


def solution(mesh):
    in_specs = (
        P("ctx", "tp"),
        P("ctx", "tp"),
        P("ctx", "tp"),
        P("ctx", "tp"),
        P("ctx", "tp"),
        P(None, "tp"),
        P(None, "tp"),
        P(None, "tp"),
        P(),
    )
    out_specs = P("ctx", "tp")
    return jax.shard_map(local, mesh=mesh, in_specs=in_specs, out_specs=out_specs, check_vma=False)
```

profile of v0, /device:TPU:1, one launch (start us, length us, event | category | flops | bytes accessed | tf_op | source)
XLA Modules:
  0.0 1110.8 jit_solution(376547123927577358)
XLA Ops:
  15.4 113.5 %all-gather.3.cloned.1.call-done = bf16[8192,128]{1,0:T(8,128)(2,1)} async-done(((bf16[128,128]{1,0:T(8,128)(2,1)}), bf16[8192,128]{1,0:T(8,128)(2,1)}) %all-gather.3.cloned.1.call-update) | async-done | bytes 2097168 | tf_op jit(solution)/shard_map/all_gather | solution.py:81
  128.9 3.8 gather_fusion
  132.7 5.3 while.56
  138.0 108.7 %all-gather.5.cloned.1.call-done = bf16[8192,128]{1,0:T(8,128)(2,1)} async-done(((bf16[128,128]{1,0:T(8,128)(2,1)}), bf16[8192,128]{1,0:T(8,128)(2,1)}) %all-gather.5.cloned.1.call-update) | async-done | bytes 2097168 | tf_op jit(solution)/shard_map/all_gather | solution.py:82
  246.7 3.7 gather_fusion.1
  250.4 2.2 broadcast.88
  252.6 2.2 broadcast.88.clone
  254.9 25.3 %while.57 = (s32[]{:T(128)}, f32[256,128]{1,0:T(8,128)S(1)}, f32[8192,128]{1,0:T(8,128)}, f32[8192,128]{1,0:T(8,128)}, s32[]{:T(128)}, /*index=5*/bf16[8192,128]...) while((s32[]{:T(128)}, f32[256,128]{1,0:T(8,128)S(1)}, ...), condition=%wide.region_7.8_spmd.clone, body=%wide.region_6.7_spmd.clone.sunk | while | flops 338101248 | bytes 8141275 | solution.py:151
  257.7 2.1 fusion.139
  266.1 2.2 fusion.139
  268.3 2.2 fusion.140
  274.5 2.2 fusion.139
  276.7 2.1 fusion.140
  280.2 10.7 while.58
  290.9 50.5 %while.59 = (s32[]{:T(128)}, f32[256,128]{1,0:T(8,128)S(1)}, f32[8192,128]{1,0:T(8,128)}, f32[8192,128]{1,0:T(8,128)}, s32[]{:T(128)}, /*index=5*/bf16[8192,128]...) while((s32[]{:T(128)}, f32[256,128]{1,0:T(8,128)S(1)}, ...), condition=%wide.region_14.15_spmd.clone, body=%wide.region_13.14_spmd.clone.sunk | while | flops 338101248 | bytes 8141275 | solution.py:151
  302.1 2.2 fusion.156
  304.3 2.2 fusion.157
  310.6 2.2 fusion.156
  312.7 2.1 fusion.157
  319.0 2.2 fusion.156
  321.1 2.2 fusion.157
  327.4 2.1 fusion.156
  329.6 2.1 fusion.157
  335.8 2.2 fusion.156
  338.0 2.2 fusion.157
  341.5 5.0 gather_fusion.2
  346.5 4.9 gather_fusion.3
  352.5 316.8 %reduce-scatter.4.cloned.1.call-done = f32[128,128]{1,0:T(8,128)} async-done(((f32[8192,128]{1,0:T(8,128)}), f32[128,128]{1,0:T(8,128)}) %reduce-scatter.4.cloned.1.call-update) | async-done | bytes 65552 | tf_op jit(solution)/shard_map/reduce_scatter | solution.py:162
  669.3 2.4 convolution_add_fusion.3
  671.6 362.4 %reduce-scatter.6.cloned.1.call-done = f32[128,128]{1,0:T(8,128)} async-done(((f32[8192,128]{1,0:T(8,128)}), f32[128,128]{1,0:T(8,128)}) %reduce-scatter.6.cloned.1.call-update) | async-done | bytes 65552 | tf_op jit(solution)/shard_map/reduce_scatter | solution.py:163
  1034.0 2.7 convolution_add_fusion.2
  1036.7 65.9 %reduce-scatter.8.cloned.1.call-done = f32[128,512]{1,0:T(8,128)} async-done(((f32[128,2048]{1,0:T(8,128)}), f32[128,512]{1,0:T(8,128)}) %reduce-scatter.8.cloned.1.call-update) | async-done | bytes 262160 | tf_op jit(solution)/shard_map/reduce_scatter | solution.py:175
  (175 shorter events, 68.7 us)
Async XLA Ops:
  6.5 345.1 %copy-start = (bf16[2048,512]{1,0:T(8,128)(2,1)S(1)}, bf16[2048,512]{1,0:T(8,128)(2,1)}, u32[]{:S(2)}) copy-start(bf16[2048,512]{1,0:T(8,128)(2,1)} %param.22) | copy-start | bytes 6291460
  6.5 122.3 %all-gather.3.cloned.1.call-start = ((), (), s32[]{:S(2)}) async-start(), calls=%async_computation.3 | async-start | bytes 2129920 | tf_op jit(solution)/shard_map/all_gather | solution.py:81
  7.3 239.5 %all-gather.5.cloned.1.call-start = ((), (), s32[]{:S(2)}) async-start(), calls=%async_computation.4 | async-start | bytes 2129920 | tf_op jit(solution)/shard_map/all_gather | solution.py:82
  8.0 661.2 %reduce-scatter.4.cloned.1.call-start = ((), (), s32[]{:S(2)}) async-start(), calls=%async_computation.5 | async-start | bytes 4259840 | tf_op jit(solution)/shard_map/reduce_scatter | solution.py:162
  346.5 687.6 %reduce-scatter.6.cloned.1.call-start = ((), (), s32[]{:S(2)}) async-start(), calls=%async_computation.6 | async-start | bytes 4259840 | tf_op jit(solution)/shard_map/reduce_scatter | solution.py:163
  351.5 751.1 %reduce-scatter.8.cloned.1.call-start = ((), (), s32[]{:S(2)}) async-start(), calls=%async_computation.7 | async-start | bytes 1310720 | tf_op jit(solution)/shard_map/reduce_scatter | solution.py:175
Sparse Core Ops, SparseCore 0:
  10.8 117.9 all-gather.2
  132.3 114.3 all-gather.4
  346.6 322.6 reduce-scatter.3
  671.8 362.1 reduce-scatter.5
  1036.9 65.7 reduce-scatter.7
where the time goes:
time: 1110 us
  waiting for transfers between devices  969 us (87%)
  matrix products  91.3 us (8%)
  local copies, waits for them, and re-layouts  28.6 us (3%)
  between operations  14.7 us (1%)
    reduce_scatter x1, waiting for transfers between devices, local(): lax.psum_scatter(value_stored, 'ctx', scatter_dimension=0, tiled=True)  362 us
    reduce_scatter x1, waiting for transfers between devices, local(): lax.psum_scatter(key_stored, 'ctx', scatter_dimension=0, tiled=True)  317 us
    all_gather x1, waiting for transfers between devices, local(): lax.all_gather(key_rows, 'ctx', axis=0, tiled=True)  113 us
    all_gather x1, waiting for transfers between devices, local(): lax.all_gather(value_matrix, 'ctx', axis=0, tiled=True)  109 us
    reduce_scatter x1, waiting for transfers between devices, local(): lax.psum_scatter(partial_sum, 'tp', scatter_dimension=1, tiled=True)  65.9 us
    dot_general x30, matrix products, contract_last(): lax.dot_general(left, right, (((1,), (1,)), ((), ())), preferred_element_...  40.9 us
    dot_general x18, matrix products, contract_first(): lax.dot_general(left, right, (((0,), (0,)), ((), ())), preferred_element_...  38.7 us
  transfers between devices with their start and end apart: 5, of which 5 were waited for; matrix products, arithmetic and copies ran while one was open for 2% of the time, Pallas kernels for 0%

commit v1 on v0

v1 whole, which is shorter than its diff:
```python
import functools
import math

import jax
import jax.numpy as jnp
from jax import lax
from jax.experimental import pallas as pl
from jax.experimental.pallas import tpu as pltpu
from jax.sharding import PartitionSpec as P

HEAD = 128
SPAN = 64
GROUP = 4
QUERY_SHARE = 4
SUBS = 4
BLOCK = SUBS * SPAN
COLS = GROUP * SPAN
SCALE = HEAD ** (-0.5)
SCALE2 = SCALE * math.log2(math.e)
LOG2E = math.log2(math.e)
NEG = -1e30
F32 = jnp.float32
BF16 = jnp.bfloat16


def dot(left, right, left_dim, right_dim):
    return lax.dot_general(
        left, right, (((left_dim,), (right_dim,)), ((), ())), preferred_element_type=F32
    )


def pack_kernel(q_ref, g_ref, o_ref, out_ref):
    width = GROUP * HEAD
    out_ref[:, :width] = q_ref[...]
    out_ref[:, width : 2 * width] = g_ref[...]
    lane = lax.broadcasted_iota(jnp.int32, (q_ref.shape[0], HEAD), 1)
    extra = jnp.zeros((q_ref.shape[0], HEAD), F32)
    for head in range(GROUP):
        cols = slice(head * HEAD, (head + 1) * HEAD)
        products = g_ref[:, cols].astype(F32) * o_ref[:, cols].astype(F32)
        rest = jnp.sum(products, axis=1, keepdims=True)
        for term in range(3):
            part = rest.astype(BF16).astype(F32)
            extra = jnp.where(lane == term * GROUP + head, part, extra)
            rest = rest - part
    out_ref[:, 2 * width :] = extra.astype(BF16)


def key_row(slot):
    return pl.multiple_of((slot // 2) * (4 * SPAN) + (slot % 2) * SPAN, SPAN)


def stacked(ref, half, first_col):
    rows = slice(half * SPAN, (half + 1) * SPAN)
    return jnp.concatenate(
        [ref[rows, first_col + h * HEAD : first_col + (h + 1) * HEAD] for h in range(GROUP)],
        axis=0,
    )


def mask_pattern():
    row = lax.broadcasted_iota(jnp.int32, (SPAN, COLS), 0)
    col = lax.broadcasted_iota(jnp.int32, (SPAN, COLS), 1)
    return row - col % SPAN


def stats_kernel(spans, meta, kv_ref, p0, p1, p2, p3, out_ref, ks):
    def copy_span(n, carry):
        src = key_row(meta[n])
        ks[pl.ds(pl.multiple_of(n * SPAN, SPAN), SPAN), :] = kv_ref[pl.ds(src, SPAN), :]
        return carry

    lax.fori_loop(0, spans, copy_span, 0)
    pattern = mask_pattern()
    packed = (p0, p1, p2, p3)
    for i in range(2 * QUERY_SHARE):
        query = stacked(packed[i // 2], i % 2, 0)
        query_pos = meta[2 * spans + i]

        def step(block, carry):
            run_max, run_sum = carry
            keys = ks[pl.ds(pl.multiple_of(block * BLOCK, BLOCK), BLOCK), :]
            scores = dot(keys, query, 1, 1) * SCALE2
            parts = []
            new_max = run_max
            for sub in range(SUBS):
                gap = (query_pos - meta[spans + block * SUBS + sub]) * SPAN
                part = jnp.where(pattern <= gap, scores[sub * SPAN : (sub + 1) * SPAN], NEG)
                part = part.reshape(SPAN // 8, 8, COLS)
                new_max = jnp.maximum(new_max, jnp.max(part, axis=0))
                parts.append(part)
            run_sum = run_sum * jnp.exp2(run_max - new_max)
            for part in parts:
                run_sum = run_sum + jnp.sum(jnp.exp2(part - new_max[None]), axis=0)
            return new_max, run_sum

        start = (jnp.full((8, COLS), NEG, F32), jnp.zeros((8, COLS), F32))
        run_max, run_sum = lax.fori_loop(0, meta[2 * spans + 2 * QUERY_SHARE + i], step, start)
        top = jnp.max(run_max, axis=0, keepdims=True)
        out_ref[i : i + 1, :] = top
        total = jnp.sum(run_sum * jnp.exp2(run_max - top), axis=0, keepdims=True)
        out_ref[2 * QUERY_SHARE + i : 2 * QUERY_SHARE + i + 1, :] = total


def grads_kernel(
    spans, meta, kv_ref, p0, p1, p2, p3, s0, s1, s2, s3, dkv_ref, dq0, dq1, dq2, dq3, ks, vs, dka, dva
):
    width = GROUP * HEAD
    minus = jnp.full((SPAN, HEAD), -1.0, BF16)

    def copy_span(n, carry):
        src = key_row(meta[n])
        rows = pl.ds(pl.multiple_of(n * SPAN, SPAN), SPAN)
        ks[rows, :] = kv_ref[pl.ds(src, SPAN), :]
        vs[rows, :HEAD] = kv_ref[pl.ds(pl.multiple_of(src + 2 * SPAN, SPAN), SPAN), :]
        vs[rows, HEAD:] = minus
        return carry

    lax.fori_loop(0, spans, copy_span, 0)
    dka[...] = jnp.zeros_like(dka)
    dva[...] = jnp.zeros_like(dva)
    pattern = mask_pattern()
    lane = lax.broadcasted_iota(jnp.int32, (SPAN, HEAD), 1)
    packed = (p0, p1, p2, p3)
    stats = (s0, s1, s2, s3)
    outs = (dq0, dq1, dq2, dq3)
    for i in range(2 * QUERY_SHARE):
        slot, half = i // 2, i % 2
        query = stacked(packed[slot], half, 0)
        grad = stacked(packed[slot], half, width)
        extra = packed[slot][half * SPAN : (half + 1) * SPAN, 2 * width :].astype(F32)
        extras = jnp.concatenate(
            [
                jnp.where(jnp.logical_and(lane % GROUP == h, lane < 3 * GROUP), extra, 0.0)
                for h in range(GROUP)
            ],
            axis=0,
        ).astype(BF16)
        grad_ext = jnp.concatenate([grad, extras], axis=1)
        query_pos = meta[2 * spans + i]
        tops, sums = [], []
        for shift in range(QUERY_SHARE):
            row = ((slot - shift) % QUERY_SHARE) * 2 + half
            tops.append(stats[shift][row : row + 1, :])
            sums.append(stats[shift][2 * QUERY_SHARE + row : 2 * QUERY_SHARE + row + 1, :])
        top = functools.reduce(jnp.maximum, tops)
        total = sum(s * jnp.exp2(t - top) for s, t in zip(sums, tops))
        log_total = top + jnp.log(total) * LOG2E

        def step(block, query_acc):
            rows = pl.ds(pl.multiple_of(block * BLOCK, BLOCK), BLOCK)
            keys = ks[rows, :]
            scores = dot(keys, query, 1, 1) * SCALE2 - log_total
            weights = []
            for sub in range(SUBS):
                gap = (query_pos - meta[spans + block * SUBS + sub]) * SPAN
                part = jnp.exp2(scores[sub * SPAN : (sub + 1) * SPAN])
                weights.append(jnp.where(pattern <= gap, part, 0.0))
            weights = jnp.concatenate(weights, axis=0)
            grad_probs = dot(vs[rows, :], grad_ext, 1, 1)
            grad_scores = (weights * grad_probs).astype(BF16)
            dva[rows, :] += dot(weights.astype(BF16), grad, 1, 0)
            dka[rows, :] += dot(grad_scores, query, 1, 0)
            return query_acc + dot(grad_scores, keys, 0, 0)

        query_acc = lax.fori_loop(
            0, meta[2 * spans + 2 * QUERY_SHARE + i], step, jnp.zeros((COLS, HEAD), F32)
        )
        for h in range(GROUP):
            outs[slot][half * SPAN : (half + 1) * SPAN, h * HEAD : (h + 1) * HEAD] = (
                query_acc[h * SPAN : (h + 1) * SPAN] * SCALE
            ).astype(outs[slot].dtype)

    def place_span(n, carry):
        dst = key_row(meta[n])
        rows = pl.ds(pl.multiple_of(n * SPAN, SPAN), SPAN)
        dkv_ref[pl.ds(dst, SPAN), :] = (dka[rows, :] * SCALE).astype(BF16)
        dkv_ref[pl.ds(pl.multiple_of(dst + 2 * SPAN, SPAN), SPAN), :] = dva[rows, :].astype(BF16)
        return carry

    lax.fori_loop(0, spans, place_span, 0)


VMEM = pl.BlockSpec(memory_space=pltpu.VMEM)
SMEM = pl.BlockSpec(memory_space=pltpu.SMEM)
PARAMS = pltpu.CompilerParams(vmem_limit_bytes=40 * 1024 * 1024)


def local(q, k, v, o, g, w_query, key_weight, value_weight, span_pos):
    tokens, width = q.shape
    cycle = lax.axis_size("ctx")
    tp_size = lax.axis_size("tp")
    members = cycle // QUERY_SHARE
    spans = 2 * members
    index = lax.axis_index("ctx")
    mine, base = index % QUERY_SHARE, index // QUERY_SHARE * QUERY_SHARE
    key_groups = [[j * QUERY_SHARE + i for j in range(members)] for i in range(QUERY_SHARE)]

    def shifted(array, shift):
        pairs = []
        for device in range(cycle):
            low = device // QUERY_SHARE * QUERY_SHARE
            pairs.append((device, low + (device - low + shift) % QUERY_SHARE))
        return lax.ppermute(array, "ctx", pairs)

    packed = pl.pallas_call(
        pack_kernel,
        out_shape=jax.ShapeDtypeStruct((tokens, 2 * width + HEAD), BF16),
        in_specs=[VMEM] * 3,
        out_specs=VMEM,
        name="pack",
    )(q, g, o)
    packs = [packed] + [shifted(packed, s) for s in range(1, QUERY_SHARE)]
    own_kv = jnp.concatenate([k, v], axis=0)
    copies = jnp.broadcast_to(own_kv[None], (members,) + own_kv.shape).reshape(-1, HEAD)
    kv = lax.all_to_all(copies, "ctx", 0, 0, tiled=True, axis_index_groups=key_groups)

    key_pos = lax.dynamic_slice_in_dim(
        span_pos.reshape(members, QUERY_SHARE, 2), mine, 1, axis=1
    ).reshape(spans)
    ids = jnp.arange(spans, dtype=jnp.int32)
    rank = jnp.sum((key_pos[None, :] < key_pos[:, None]).astype(jnp.int32), axis=1)
    placed = rank[None, :] == ids[:, None]
    order = jnp.sum(jnp.where(placed, ids[None, :], 0), axis=1)
    sorted_pos = jnp.sum(jnp.where(placed, key_pos[None, :], 0), axis=1)
    share_pos = lax.dynamic_slice_in_dim(span_pos, 2 * base, 2 * QUERY_SHARE).reshape(-1, 2)
    turned = (mine - jnp.arange(QUERY_SHARE, dtype=jnp.int32)) % QUERY_SHARE
    query_pos = jnp.sum(
        jnp.where(
            turned[:, None, None] == jnp.arange(QUERY_SHARE, dtype=jnp.int32)[None, :, None],
            share_pos[None],
            0,
        ),
        axis=1,
    ).reshape(-1)
    seen = jnp.sum((key_pos[None, :] <= query_pos[:, None]).astype(jnp.int32), axis=1)
    meta = jnp.concatenate([order, sorted_pos, query_pos, (seen + SUBS - 1) // SUBS])

    stat_rows = 4 * QUERY_SHARE
    stats = pl.pallas_call(
        functools.partial(stats_kernel, spans),
        out_shape=jax.ShapeDtypeStruct((stat_rows, COLS), F32),
        in_specs=[SMEM] + [VMEM] * 5,
        out_specs=VMEM,
        scratch_shapes=[pltpu.VMEM((spans * SPAN, HEAD), BF16)],
        compiler_params=PARAMS,
        name="stats",
    )(meta, kv, *packs)
    all_stats = [stats] + [shifted(stats, s) for s in range(1, QUERY_SHARE)]
    dq_shape = (tokens, width)
    dkv, *dqs = pl.pallas_call(
        functools.partial(grads_kernel, spans),
        out_shape=[jax.ShapeDtypeStruct((2 * spans * SPAN, HEAD), BF16)]
        + [jax.ShapeDtypeStruct(dq_shape, F32)]
        + [jax.ShapeDtypeStruct(dq_shape, BF16)] * (QUERY_SHARE - 1),
        in_specs=[SMEM] + [VMEM] * 9,
        out_specs=[VMEM] * 5,
        scratch_shapes=[
            pltpu.VMEM((spans * SPAN, HEAD), BF16),
            pltpu.VMEM((spans * SPAN, 2 * HEAD), BF16),
            pltpu.VMEM((spans * SPAN, HEAD), F32),
            pltpu.VMEM((spans * SPAN, HEAD), F32),
        ],
        compiler_params=PARAMS,
        name="grads",
    )(meta, kv, *packs, *all_stats)
    dq_parts = [shifted(dqs[s], -s) for s in range(1, QUERY_SHARE)]
    dkv_parts = lax.all_to_all(dkv, "ctx", 0, 0, tiled=True, axis_index_groups=key_groups)
    dq_sum = dqs[0]
    for part in dq_parts:
        dq_sum = dq_sum + part.astype(F32)
    grad_query = dq_sum.astype(BF16)
    dkv_sum = jnp.sum(dkv_parts.reshape(members, 2, tokens, HEAD).astype(F32), axis=0).astype(BF16)
    partial = (
        dot(grad_query, w_query, 1, 1)
        + dot(dkv_sum[0], key_weight, 1, 1)
        + dot(dkv_sum[1], value_weight, 1, 1)
    )
    feats = partial.shape[1] // tp_size
    rank_tp = lax.axis_index("tp")
    total = lax.dynamic_slice_in_dim(partial, rank_tp * feats, feats, 1)
    for s in range(1, tp_size):
        peer = (rank_tp + s) % tp_size
        piece = lax.dynamic_slice_in_dim(partial, peer * feats, feats, 1).astype(BF16)
        pairs = [(d, (d + s) % tp_size) for d in range(tp_size)]
        total = total + lax.ppermute(piece, "tp", pairs).astype(F32)
    return total.astype(BF16)


def solution(mesh):
    row, col = P("ctx", "tp"), P(None, "tp")
    in_specs = (row, row, row, row, row, col, col, col, P())
    return jax.shard_map(local, mesh=mesh, in_specs=in_specs, out_specs=row, check_vma=False)
```

time: 1110 us -> 133 us (0.12)
  waiting for transfers between devices: 969 us -> 46.1 us
  matrix products: 91.3 us -> 3.42 us
  starting transfers between devices: 0.16 us -> 37.8 us
  Pallas kernels: 0 us -> 32.4 us
  local copies, waits for them, and re-layouts: 28.6 us -> 7.49 us
  between operations: 14.7 us -> 0.27 us
    reduce_scatter x3 -> x0, waiting for transfers between devices: 745 us -> none  [the longest x1 362 us: local(): lax.psum_scatter(value_stored, 'ctx', scatter_dimension=0, tiled=True)]
    all_gather x2 -> x0, waiting for transfers between devices: 222 us -> none  [the longest x1 113 us: local(): lax.all_gather(key_rows, 'ctx', axis=0, tiled=True)]
    dot_general x57 -> x3, matrix products: 91.3 us -> 3.42 us  [dot(): lax.dot_general(left, right, (((left_dim,), (right_dim,)), ((), ())), pre...]
    pallas_call x0 -> x3, Pallas kernels: none -> 32.4 us  [the longest x1 20 us: local(): pl.pallas_call(functools.partial(grads_kernel, spans), out_shape=[jax.Sha...]
    all_to_all x0 -> x2, waiting for transfers between devices: none -> 29.4 us  [the longest x1 20.8 us: local(): lax.all_to_all(dkv, 'ctx', 0, 0, tiled=True, axis_index_groups=key_groups)]
    ppermute x0 -> x12, starting transfers between devices: none -> 20.1 us  [the longest x9 13 us: shifted(): return lax.ppermute(array, 'ctx', pairs)]
    all_to_all x0 -> x2, starting transfers between devices: none -> 17.7 us  [the longest x1 11.7 us: local(): lax.all_to_all(copies, 'ctx', 0, 0, tiled=True, axis_index_groups=key_gro...]
    gather x4 -> x0, local copies, waits for them, and re-layouts: 17.4 us -> none  [the longest x1 4.98 us: local(): key_acc.reshape(span_total, span_len, HEAD_SIZE)[span_pos]]
  transfers between devices with their start and end apart: 5 -> 14, of which waited for: 5 -> 7; matrix products, arithmetic and copies ran while one was open for 2% -> 3% of each run, Pallas kernels for 0% -> 1%
where the time goes in v1:
time: 133 us; the launch traced here: 132 us
  waiting for transfers between devices  46.1 us (35%)
  starting transfers between devices  37.8 us (28%)
  Pallas kernels  32.4 us (24%)
  local copies, waits for them, and re-layouts  7.49 us (6%)
  other arithmetic  4.78 us (4%)
  matrix products  3.42 us (3%)
    all_to_all x1, waiting for transfers between devices, local(): lax.all_to_all(dkv, 'ctx', 0, 0, tiled=True, axis_index_groups=key_groups)  20.8 us
    pallas_call x1, Pallas kernels, local(): pl.pallas_call(functools.partial(grads_kernel, spans), out_shape=[jax.Sha...  20 us
    ppermute x9, starting transfers between devices, shifted(): return lax.ppermute(array, 'ctx', pairs)  13 us
    all_to_all x1, starting transfers between devices, local(): lax.all_to_all(copies, 'ctx', 0, 0, tiled=True, axis_index_groups=key_gro...  11.7 us
    ppermute x9, waiting for transfers between devices, shifted(): return lax.ppermute(array, 'ctx', pairs)  11.2 us
    pallas_call x1, Pallas kernels, local(): pl.pallas_call(functools.partial(stats_kernel, spans), out_shape=jax.Shap...  10.4 us
    all_to_all x1, waiting for transfers between devices, local(): lax.all_to_all(copies, 'ctx', 0, 0, tiled=True, axis_index_groups=key_gro...  8.61 us
    ppermute x3, starting transfers between devices, local(): total = total + lax.ppermute(piece, 'tp', pairs).astype(F32)  7.09 us
  transfers between devices with their start and end apart: 14, of which 7 were waited for; matrix products, arithmetic and copies ran while one was open for 3% of the time, Pallas kernels for 1%

profile of v1, /device:TPU:1, one launch (start us, length us, event | category | flops | bytes accessed | tf_op | source)
XLA Modules:
  0.0 132.2 jit_solution(15078788658915291152)
XLA Ops:
  0.0 0.9 pad_maximum_fusion
  0.9 1.2 broadcast_in_dim.55
  2.1 11.7 %all-to-all-start = ((bf16[16,256,128]{2,1,0:T(8,128)(2,1)}), bf16[16,256,128]{2,1,0:T(8,128)(2,1)S(1)}, u32[]{:S(2)}, u32[]{:S(2)}) async-start(bf16[16,256,128]{2,1,0:T(8,128)(2,1)} %broadcast_in_dim.55), calls=%async_computation | async-start | bytes 2097152 | tf_op jit(solution)/shard_map/all_to_all | solution.py:216
  13.9 1.9 %pack.1.p0 = bf16[128,1152]{1,0:T(8,128)(2,1)} custom-call(bf16[128,512]{1,0:T(8,128)(2,1)} %q_ref.1, bf16[128,512]{1,0:T(8,128)(2,1)} %g_ref.1, bf16[128,512]{1,0:T(8,128)(2,1)} %o_ref.1), custom_call_target="tpu_custom_call" | custom-call | tf_op jit(solution)/shard_map/pack/pallas_call | solution.py:206
  15.8 1.2 collective-permute-start
  17.0 2.5 %collective-permute-start.1 = (bf16[128,1152]{1,0:T(8,128)(2,1)}, bf16[128,1152]{1,0:T(8,128)(2,1)}, u32[]{:S(2)}, u32[]{:S(2)}) collective-permute-start(bf16[128,1152]{1,0:T(8,128)(2,1)} %pack.1.p0), channel_id=1, source_target_pairs={{0,8},{4,12},{8,0},{12,4},{16,24},{20,28},{24,16},{28,20},{32,40},... | collective-permute-start | bytes 884744 | tf_op jit(solution)/shard_map/ppermute | solution.py:204
  19.5 1.2 collective-permute-start.2
  22.2 2.6 %collective-permute-done.p1 = bf16[128,1152]{1,0:T(8,128)(2,1)S(1)} collective-permute-done((bf16[128,1152]{1,0:T(8,128)(2,1)}, bf16[128,1152]{1,0:T(8,128)(2,1)S(1)}, u32[]{:S(2)}, u32[]{:S(2)}) %collective-permute-start) | collective-permute-done | bytes 294944 | tf_op jit(solution)/shard_map/ppermute | solution.py:204
  24.8 7.4 %collective-permute-done.1.p2 = bf16[128,1152]{1,0:T(8,128)(2,1)} collective-permute-done((bf16[128,1152]{1,0:T(8,128)(2,1)}, bf16[128,1152]{1,0:T(8,128)(2,1)}, u32[]{:S(2)}, u32[]{:S(2)}) %collective-permute-start.1) | collective-permute-done | bytes 294944 | tf_op jit(solution)/shard_map/ppermute | solution.py:204
  32.2 8.6 %all-to-all-done = bf16[16,256,128]{2,1,0:T(8,128)(2,1)S(1)} async-done(((bf16[16,256,128]{2,1,0:T(8,128)(2,1)}), bf16[16,256,128]{2,1,0:T(8,128)(2,1)S(1)}, u32[]{:S(2)}, u32[]{:S(2)}) %all-to-all-start) | async-done | bytes 1048608 | tf_op jit(solution)/shard_map/all_to_all | solution.py:216
  40.8 1.0 copy-done.1
  41.8 10.4 %stats.1.s0 = f32[16,256]{1,0:T(8,128)S(1)} custom-call(s32[80]{0:T(128)S(1)} %pad_add_fusion.meta, bf16[4096,128]{1,0:T(8,128)(2,1)S(1)} %bitcast.5, bf16[128,1152]{1,0:T(8,128)(2,1)S(1)} %copy-done.1, bf16[128,1152]{1,0:T(8,128)(2,1)S(1)} %collective-permute-done.p1, bf16[128,1152]{1,0:T(8,128)(2,1)} %collective-permute-done.1.p2, ...), custom_call_target="tpu_custom_call" | custom-call | tf_op jit(solution)/shard_map/stats/pallas_call | solution.py:240
  52.2 1.3 collective-permute-start.3
  53.5 2.2 %collective-permute-start.4 = (f32[16,256]{1,0:T(8,128)S(1)}, f32[16,256]{1,0:T(8,128)S(1)}, u32[]{:S(2)}, u32[]{:S(2)}) collective-permute-start(f32[16,256]{1,0:T(8,128)S(1)} %stats.1.s0), channel_id=1, source_target_pairs={{0,8},{4,12},{8,0},{12,4},{16,24},{20,28},{24,16},{28,20},{32,40},... | collective-permute-start | bytes 49160 | tf_op jit(solution)/shard_map/ppermute | solution.py:204
  55.7 1.4 %collective-permute-start.5 = (f32[16,256]{1,0:T(8,128)S(1)}, f32[16,256]{1,0:T(8,128)S(1)}, u32[]{:S(2)}, u32[]{:S(2)}) collective-permute-start(f32[16,256]{1,0:T(8,128)S(1)} %stats.1.s0), channel_id=1, source_target_pairs={{0,12},{4,0},{8,4},{12,8},{16,28},{20,16},{24,20},{28,24},{32,44},... | collective-permute-start | bytes 49160 | tf_op jit(solution)/shard_map/ppermute | solution.py:204
  57.6 0.7 collective-permute-done.5.s3
  58.3 20.0 %grads.1 = (bf16[4096,128]{1,0:T(8,128)(2,1)S(1)}, f32[128,512]{1,0:T(8,128)S(1)}, bf16[128,512]{1,0:T(8,128)(2,1)S(1)}, bf16[128,512]{1,0:T(8,128)(2,1)S(1)}, bf16[128,512]{1,0:T(8,128)(2,1)S(1)}) custom-call(s32[80]{0:T(128)S(1)} %pad_add_fusion.meta, bf16[4096,128]{1,0:T(8,128)(2,1)S(1)} %bitcast.6, bf16[128,1152]{1,0:T(8,128)(2,1)S(1)} %copy-done.2, ...), custom_call_target="tpu_custom_call" | custom-call | tf_op jit(solution)/shard_map/grads/pallas_call | solution.py:251
  78.4 1.0 copy-done.3
  79.3 0.7 copy-done.4
  80.0 0.7 copy-done.6
  82.0 5.9 %all-to-all-start.1 = ((bf16[16,256,128]{2,1,0:T(8,128)(2,1)}), bf16[16,256,128]{2,1,0:T(8,128)(2,1)}, u32[]{:S(2)}, u32[]{:S(2)}) async-start(bf16[16,256,128]{2,1,0:T(8,128)(2,1)} %bitcast.7), calls=%async_computation.1 | async-start | bytes 2097152 | tf_op jit(solution)/shard_map/all_to_all | solution.py:268
  88.0 2.7 %collective-permute-start.6 = (bf16[128,512]{1,0:T(8,128)(2,1)S(1)}, bf16[128,512]{1,0:T(8,128)(2,1)S(1)}, u32[]{:S(2)}, u32[]{:S(2)}) collective-permute-start(bf16[128,512]{1,0:T(8,128)(2,1)S(1)} %copy-done.11), channel_id=1, source_target_pairs={{0,12},{4,0},{8,4},{12,8},{16,28},{20,16},{24,20},{28,24},{32,44},... | collective-permute-start | bytes 393224 | tf_op jit(solution)/shard_map/ppermute | solution.py:204
  90.7 0.7 collective-permute-start.8
  91.4 20.8 %all-to-all-done.1 = bf16[16,256,128]{2,1,0:T(8,128)(2,1)} async-done(((bf16[16,256,128]{2,1,0:T(8,128)(2,1)}), bf16[16,256,128]{2,1,0:T(8,128)(2,1)}, u32[]{:S(2)}, u32[]{:S(2)}) %all-to-all-start.1) | async-done | bytes 1048608 | tf_op jit(solution)/shard_map/all_to_all | solution.py:268
  112.1 1.4 %reduce_sum.62 = bf16[256,128]{1,0:T(8,128)(2,1)S(1)} reduce(bf16[16,256,128]{2,1,0:T(8,128)(2,1)} %all-to-all-done.1, bf16[]{:T(256)} %constant.79.clone.1), dimensions={0}, to_apply=%region_5.6 | reduce | flops 491520 | bytes 1114114 | tf_op jit(solution)/shard_map/reduce_sum | solution.py:273
  113.8 1.3 %fusion.3 = f32[128,2048]{1,0:T(8,128)S(1)} fusion(bf16[2048,128]{1,0:T(8,128)(2,1)} %param.15, bf16[256,128]{1,0:T(8,128)(2,1)S(1)} %reduce_sum.62), kind=kOutput, calls=%fused_computation.10 | convolution fusion | flops 67108864 | bytes 1605632 | tf_op jit(solution)/shard_map/dot_general | solution.py:27
  115.2 1.8 %fusion = f32[128,2048]{1,0:T(8,128)S(1)} fusion(f32[128,2048]{1,0:T(8,128)S(1)} %fusion.1, f32[128,2048]{1,0:T(8,128)S(1)} %fusion.3, bf16[2048,512]{1,0:T(8,128)(2,1)S(1)} %copy-done, bf16[128,512]{1,0:T(8,128)(2,1)} %collective-permute-done.8, bf16[128,512]{1,0:T(8,128)(2,1)} %collective-permute-done.7, f32[128,512]{1,0:T(8,128)S(1)} %copy-done.5, ...), kind=kOutput, calls=%fused_computation.1 | convolution fusion | flops 269418496 | bytes 5898240 | tf_op jit(solution)/shard_map/dot_general | solution.py:27
  117.0 1.0 copy-done.12
  118.5 5.7 %collective-permute-start.11 = (bf16[128,512]{1,0:T(8,128)(2,1)S(1)}, bf16[128,512]{1,0:T(8,128)(2,1)S(1)}, u32[]{:S(2)}, u32[]{:S(2)}) collective-permute-start(bf16[128,512]{1,0:T(8,128)(2,1)S(1)} %get-tuple-element.18), channel_id=1, source_target_pairs={{0,3},{1,0},{2,1},{3,2},{4,7},{5,4},{6,5},{7,6},{8,11},{9,8},{10,9... | collective-permute-start | bytes 393224 | tf_op jit(solution)/shard_map/ppermute | solution.py:286
  124.1 1.0 collective-permute-start.9
  125.1 5.4 %collective-permute-done.11 = bf16[128,512]{1,0:T(8,128)(2,1)S(1)} collective-permute-done((bf16[128,512]{1,0:T(8,128)(2,1)S(1)}, bf16[128,512]{1,0:T(8,128)(2,1)S(1)}, u32[]{:S(2)}, u32[]{:S(2)}) %collective-permute-start.11) | collective-permute-done | bytes 131104 | tf_op jit(solution)/shard_map/ppermute | solution.py:286
  130.6 1.7 %add_convert_fusion = bf16[128,512]{1,0:T(8,128)(2,1)} fusion(bf16[128,512]{1,0:T(8,128)(2,1)S(1)} %collective-permute-done.11, bf16[128,512]{1,0:T(8,128)(2,1)S(1)} %collective-permute-done.10, bf16[128,512]{1,0:T(8,128)(2,1)S(1)} %collective-permute-done.9, f32[128,2048]{1,0:T(8,128)} %copy-done.12, s32[]{:T(128)S(6)} %select_n.76), kind=kLoop, calls=%fused_computation.2 | loop fusion | flops 458752 | bytes 786436 | tf_op jit(solution)/shard_map/convert_element_type | solution.py:287
  (53 shorter events, 4.2 us)
Async XLA Ops:
  0.0 115.2 %copy-start = (bf16[2048,512]{1,0:T(8,128)(2,1)S(1)}, bf16[2048,512]{1,0:T(8,128)(2,1)}, u32[]{:S(2)}) copy-start(bf16[2048,512]{1,0:T(8,128)(2,1)} %param.14) | copy-start | bytes 6291460
  0.0 20.6 %copy-start.14 = (s32[128]{0:T(128)S(1)}, s32[128]{0:T(128)}, u32[]{:S(2)}) copy-start(s32[128]{0:T(128)} %param.17) | copy-start | bytes 1540
  2.1 38.7 %all-to-all-start = ((bf16[16,256,128]{2,1,0:T(8,128)(2,1)}), bf16[16,256,128]{2,1,0:T(8,128)(2,1)S(1)}, u32[]{:S(2)}, u32[]{:S(2)}) async-start(bf16[16,256,128]{2,1,0:T(8,128)(2,1)} %broadcast_in_dim.55), calls=%async_computation | async-start | bytes 2097152 | tf_op jit(solution)/shard_map/all_to_all | solution.py:216
  15.8 9.0 %collective-permute-start = (bf16[128,1152]{1,0:T(8,128)(2,1)}, bf16[128,1152]{1,0:T(8,128)(2,1)S(1)}, u32[]{:S(2)}, u32[]{:S(2)}) collective-permute-start(bf16[128,1152]{1,0:T(8,128)(2,1)} %pack.1.p0), channel_id=1, source_target_pairs={{0,4},{4,8},{8,12},{12,0},{16,20},{20,24},{24,28},{28,16},{32,36},... | collective-permute-start | bytes 884744 | tf_op jit(solution)/shard_map/ppermute | solution.py:204
  17.0 15.2 %collective-permute-start.1 = (bf16[128,1152]{1,0:T(8,128)(2,1)}, bf16[128,1152]{1,0:T(8,128)(2,1)}, u32[]{:S(2)}, u32[]{:S(2)}) collective-permute-start(bf16[128,1152]{1,0:T(8,128)(2,1)} %pack.1.p0), channel_id=1, source_target_pairs={{0,8},{4,12},{8,0},{12,4},{16,24},{20,28},{24,16},{28,20},{32,40},... | collective-permute-start | bytes 884744 | tf_op jit(solution)/shard_map/ppermute | solution.py:204
  19.5 12.7 %collective-permute-start.2 = (bf16[128,1152]{1,0:T(8,128)(2,1)}, bf16[128,1152]{1,0:T(8,128)(2,1)}, u32[]{:S(2)}, u32[]{:S(2)}) collective-permute-start(bf16[128,1152]{1,0:T(8,128)(2,1)} %pack.1.p0), channel_id=1, source_target_pairs={{0,12},{4,0},{8,4},{12,8},{16,28},{20,16},{24,20},{28,24},{32,44},... | collective-permute-start | bytes 884744 | tf_op jit(solution)/shard_map/ppermute | solution.py:204
  40.8 1.0 copy-start.1
  41.8 16.5 %copy-start.2 = (bf16[128,1152]{1,0:T(8,128)(2,1)S(1)}, bf16[128,1152]{1,0:T(8,128)(2,1)}, u32[]{:S(2)}) copy-start(bf16[128,1152]{1,0:T(8,128)(2,1)} %pack.1.p0) | copy-start | bytes 884740
  52.2 4.9 %collective-permute-start.3 = (f32[16,256]{1,0:T(8,128)S(1)}, f32[16,256]{1,0:T(8,128)S(1)}, u32[]{:S(2)}, u32[]{:S(2)}) collective-permute-start(f32[16,256]{1,0:T(8,128)S(1)} %stats.1.s0), channel_id=1, source_target_pairs={{0,4},{4,8},{8,12},{12,0},{16,20},{20,24},{24,28},{28,16},{32,36},... | collective-permute-start | bytes 49160 | tf_op jit(solution)/shard_map/ppermute | solution.py:204
  53.5 4.1 %collective-permute-start.4 = (f32[16,256]{1,0:T(8,128)S(1)}, f32[16,256]{1,0:T(8,128)S(1)}, u32[]{:S(2)}, u32[]{:S(2)}) collective-permute-start(f32[16,256]{1,0:T(8,128)S(1)} %stats.1.s0), channel_id=1, source_target_pairs={{0,8},{4,12},{8,0},{12,4},{16,24},{20,28},{24,16},{28,20},{32,40},... | collective-permute-start | bytes 49160 | tf_op jit(solution)/shard_map/ppermute | solution.py:204
  55.7 2.6 %collective-permute-start.5 = (f32[16,256]{1,0:T(8,128)S(1)}, f32[16,256]{1,0:T(8,128)S(1)}, u32[]{:S(2)}, u32[]{:S(2)}) collective-permute-start(f32[16,256]{1,0:T(8,128)S(1)} %stats.1.s0), channel_id=1, source_target_pairs={{0,12},{4,0},{8,4},{12,8},{16,28},{20,16},{24,20},{28,24},{32,44},... | collective-permute-start | bytes 49160 | tf_op jit(solution)/shard_map/ppermute | solution.py:204
  78.4 1.0 copy-start.3
  79.3 0.7 copy-start.4
  80.0 0.7 copy-start.6
  80.7 0.6 copy-start.8
  81.3 0.6 copy-start.10
  82.0 31.5 %copy-start.13 = (bf16[2048,128]{1,0:T(8,128)(2,1)S(1)}, bf16[2048,128]{1,0:T(8,128)(2,1)}, u32[]{:S(2)}) copy-start(bf16[2048,128]{1,0:T(8,128)(2,1)} %param.16) | copy-start | bytes 1572868
  82.0 6.0 %copy-start.11 = (bf16[128,512]{1,0:T(8,128)(2,1)S(1)}, bf16[128,512]{1,0:T(8,128)(2,1)}, u32[]{:S(2)}) copy-start(bf16[128,512]{1,0:T(8,128)(2,1)} %copy-done.10) | copy-start | bytes 393220
  82.0 8.7 %copy-start.9 = (bf16[128,512]{1,0:T(8,128)(2,1)S(1)}, bf16[128,512]{1,0:T(8,128)(2,1)}, u32[]{:S(2)}) copy-start(bf16[128,512]{1,0:T(8,128)(2,1)} %copy-done.8) | copy-start | bytes 393220
  82.0 8.7 %copy-start.7 = (bf16[128,512]{1,0:T(8,128)(2,1)S(1)}, bf16[128,512]{1,0:T(8,128)(2,1)}, u32[]{:S(2)}) copy-start(bf16[128,512]{1,0:T(8,128)(2,1)} %copy-done.6) | copy-start | bytes 393220
  82.0 30.1 %all-to-all-start.1 = ((bf16[16,256,128]{2,1,0:T(8,128)(2,1)}), bf16[16,256,128]{2,1,0:T(8,128)(2,1)}, u32[]{:S(2)}, u32[]{:S(2)}) async-start(bf16[16,256,128]{2,1,0:T(8,128)(2,1)} %bitcast.7), calls=%async_computation.1 | async-start | bytes 2097152 | tf_op jit(solution)/shard_map/all_to_all | solution.py:268
  88.0 27.2 %collective-permute-start.6 = (bf16[128,512]{1,0:T(8,128)(2,1)S(1)}, bf16[128,512]{1,0:T(8,128)(2,1)S(1)}, u32[]{:S(2)}, u32[]{:S(2)}) collective-permute-start(bf16[128,512]{1,0:T(8,128)(2,1)S(1)} %copy-done.11), channel_id=1, source_target_pairs={{0,12},{4,0},{8,4},{12,8},{16,28},{20,16},{24,20},{28,24},{32,44},... | collective-permute-start | bytes 393224 | tf_op jit(solution)/shard_map/ppermute | solution.py:204
  90.7 24.5 %collective-permute-start.7 = (bf16[128,512]{1,0:T(8,128)(2,1)S(1)}, bf16[128,512]{1,0:T(8,128)(2,1)}, u32[]{:S(2)}, u32[]{:S(2)}) collective-permute-start(bf16[128,512]{1,0:T(8,128)(2,1)S(1)} %copy-done.9), channel_id=1, source_target_pairs={{0,8},{4,12},{8,0},{12,4},{16,24},{20,28},{24,16},{28,20},{32,40},... | collective-permute-start | bytes 393224 | tf_op jit(solution)/shard_map/ppermute | solution.py:204
  90.7 24.5 %copy-start.5 = (f32[128,512]{1,0:T(8,128)S(1)}, f32[128,512]{1,0:T(8,128)}, u32[]{:S(2)}) copy-start(f32[128,512]{1,0:T(8,128)} %copy-done.4) | copy-start | bytes 786436
  90.7 24.5 %collective-permute-start.8 = (bf16[128,512]{1,0:T(8,128)(2,1)S(1)}, bf16[128,512]{1,0:T(8,128)(2,1)}, u32[]{:S(2)}, u32[]{:S(2)}) collective-permute-start(bf16[128,512]{1,0:T(8,128)(2,1)S(1)} %copy-done.7), channel_id=1, source_target_pairs={{0,4},{4,8},{8,12},{12,0},{16,20},{20,24},{24,28},{28,16},{32,36},... | collective-permute-start | bytes 393224 | tf_op jit(solution)/shard_map/ppermute | solution.py:204
  117.0 1.0 copy-start.12
  118.0 7.1 %collective-permute-start.10 = (bf16[128,512]{1,0:T(8,128)(2,1)S(1)}, bf16[128,512]{1,0:T(8,128)(2,1)S(1)}, u32[]{:S(2)}, u32[]{:S(2)}) collective-permute-start(bf16[128,512]{1,0:T(8,128)(2,1)S(1)} %get-tuple-element.19), channel_id=1, source_target_pairs={{0,2},{1,3},{2,0},{3,1},{4,6},{5,7},{6,4},{7,5},{8,10},{9,11},{10,... | collective-permute-start | bytes 393224 | tf_op jit(solution)/shard_map/ppermute | solution.py:286
  118.5 12.1 %collective-permute-start.11 = (bf16[128,512]{1,0:T(8,128)(2,1)S(1)}, bf16[128,512]{1,0:T(8,128)(2,1)S(1)}, u32[]{:S(2)}, u32[]{:S(2)}) collective-permute-start(bf16[128,512]{1,0:T(8,128)(2,1)S(1)} %get-tuple-element.18), channel_id=1, source_target_pairs={{0,3},{1,0},{2,1},{3,2},{4,7},{5,4},{6,5},{7,6},{8,11},{9,8},{10,9... | collective-permute-start | bytes 393224 | tf_op jit(solution)/shard_map/ppermute | solution.py:286
  124.1 6.4 %collective-permute-start.9 = (bf16[128,512]{1,0:T(8,128)(2,1)S(1)}, bf16[128,512]{1,0:T(8,128)(2,1)S(1)}, u32[]{:S(2)}, u32[]{:S(2)}) collective-permute-start(bf16[128,512]{1,0:T(8,128)(2,1)S(1)} %get-tuple-element.17), channel_id=1, source_target_pairs={{0,1},{1,2},{2,3},{3,0},{4,5},{5,6},{6,7},{7,4},{8,9},{9,10},{10,1... | collective-permute-start | bytes 393224 | tf_op jit(solution)/shard_map/ppermute | solution.py:286

commit v2 on v1

v2 whole, which is shorter than its diff:
```python
import functools
import math

import jax
import jax.numpy as jnp
from jax import lax
from jax.experimental import pallas as pl
from jax.experimental.pallas import tpu as pltpu
from jax.sharding import PartitionSpec as P

HEAD = 128
SPAN = 64
GROUP = 4
SHARE = 4
SIDES = 2
SUBS = 4
BLOCK = SUBS * SPAN
COLS = GROUP * SPAN
WIDTH = GROUP * HEAD
QSPANS = 2 * SHARE
TURN = 10
SCALE = HEAD ** (-0.5)
LOG2E = math.log2(math.e)
SCALE2 = SCALE * LOG2E
NEG = -1e30
F32 = jnp.float32
BF16 = jnp.bfloat16


def dot(left, right, left_dim, right_dim):
    return lax.dot_general(
        left, right, (((left_dim,), (right_dim,)), ((), ())), preferred_element_type=F32
    )


def rows_at(index, size):
    return pl.ds(pl.multiple_of(index * size, size), size)


def span_rows(slot, value):
    return rows_at(slot // 2 * 4 + slot % 2 + 2 * value, SPAN)


def load_all(sources, buffers, sems):
    copies = [
        pltpu.make_async_copy(source, buffer, sems.at[n])
        for n, (source, buffer) in enumerate(zip(sources, buffers))
    ]
    for copy in copies:
        copy.start()
    return copies


def head_cols(head, first=0):
    return slice(first + head * HEAD, first + (head + 1) * HEAD)


def span_slice(half):
    return slice(half * SPAN, (half + 1) * SPAN)


def part_slice(index, size):
    return slice(index * size, (index + 1) * size)


def tile_kernel(k_ref, v_ref, out_ref):
    tokens = k_ref.shape[0]
    for member in range(out_ref.shape[0] // (2 * tokens)):
        out_ref[part_slice(2 * member, tokens), :] = k_ref[...]
        out_ref[part_slice(2 * member + 1, tokens), :] = v_ref[...]


def pack_kernel(g_ref, o_ref, out_ref):
    out_ref[:, :WIDTH] = g_ref[...]
    lane = lax.broadcasted_iota(jnp.int32, (g_ref.shape[0], HEAD), 1)
    extra = jnp.zeros((g_ref.shape[0], HEAD), F32)
    for head in range(GROUP):
        cols = head_cols(head)
        products = g_ref[:, cols].astype(F32) * o_ref[:, cols].astype(F32)
        rest = jnp.sum(products, axis=1, keepdims=True)
        for term in range(3):
            part = rest.astype(BF16).astype(F32)
            extra = jnp.where(lane == term * GROUP + head, part, extra)
            rest = rest - part
    out_ref[:, WIDTH:] = extra.astype(BF16)


def mask_pattern():
    row = lax.broadcasted_iota(jnp.int32, (SPAN, COLS), 0)
    col = lax.broadcasted_iota(jnp.int32, (SPAN, COLS), 1)
    return row - col % SPAN


def step_of(meta, spans, step):
    at = 2 * spans + 3 * step
    return meta[at], meta[at + 1], meta[at + 2]


def stats_kernel(
    spans, steps, meta, kv_ref, q0, q1, q2, q3, before, out_ref, kin, qin, ks, qs, ms, ls, sems
):
    copies = load_all((kv_ref, q0, q1, q2, q3), (kin, *[qin.at[n] for n in range(SHARE)]), sems)
    copies[0].wait()

    def copy_span(n, carry):
        ks[rows_at(n, SPAN), :] = kin[span_rows(meta[n], 0), :]
        return carry

    lax.fori_loop(0, spans, copy_span, 0, unroll=8)
    for copy in copies[1:]:
        copy.wait()
    for i in range(QSPANS):
        for h in range(GROUP):
            qs[part_slice(i * GROUP + h, SPAN), :] = qin[i // 2, span_slice(i % 2), head_cols(h)]
    ms[...] = jnp.full_like(ms, NEG)
    ls[...] = jnp.zeros_like(ls)
    pattern = mask_pattern()

    def turn(index, carry):
        todo = [step_of(meta, spans, index * TURN + u) for u in range(TURN)]
        scores = [
            dot(ks[rows_at(block, BLOCK), :], qs[rows_at(q_at, COLS), :], 1, 1)
            for q_at, block, _ in todo
        ]
        tops, totals = [], []
        for (_, block, query_pos), score in zip(todo, scores):
            parts = []
            for sub in range(SUBS):
                gap = (query_pos - meta[spans + block * SUBS + sub]) * SPAN
                part = jnp.where(pattern <= gap, score[part_slice(sub, SPAN)] * SCALE2, NEG)
                parts.append(part.reshape(SPAN // 8, 8, COLS))
            top = functools.reduce(jnp.maximum, [jnp.max(part, axis=0) for part in parts])
            tops.append(top)
            totals.append(sum(jnp.sum(jnp.exp2(part - top[None]), axis=0) for part in parts))
        for (q_at, _, _), top, total in zip(todo, tops, totals):
            rows = rows_at(q_at, 8)
            old = ms[rows, :]
            new = jnp.maximum(old, top)
            ls[rows, :] = ls[rows, :] * jnp.exp2(old - new) + total * jnp.exp2(top - new)
            ms[rows, :] = new
        return carry

    lax.fori_loop(0, steps // TURN, turn, 0)
    for i in range(QSPANS):
        run_max, run_sum = ms[part_slice(i, 8), :], ls[part_slice(i, 8), :]
        old_max, old_sum = before[i : i + 1, :], before[QSPANS + i : QSPANS + i + 1, :]
        top = jnp.maximum(jnp.max(run_max, axis=0, keepdims=True), old_max)
        total = jnp.sum(run_sum * jnp.exp2(run_max - top), axis=0, keepdims=True)
        out_ref[i : i + 1, :] = top
        out_ref[QSPANS + i : QSPANS + i + 1, :] = total + old_sum * jnp.exp2(old_max - top)


def grads_kernel(spans, steps, last, *refs):
    meta, kv_ref, *queries = refs[: 2 + SHARE]
    grads, stats, refs = refs[6:10], refs[10:14], refs[14:]
    if last:
        dq_before, dkv_ref, *dq_refs = refs[: 2 + SHARE]
        kvin, qin, gin, dkv, own, others, ks, vs, kt, dka, dva, qs, gs, lt, dqa, sems = refs[6:]
    else:
        dkv_ref, dq_ref, kvin, qin, gin, dkv, ks, vs, kt, dka, dva, qs, gs, lt, dqa, sems = refs
    copies = load_all(
        (kv_ref, *queries, *grads),
        (kvin, *[qin.at[n] for n in range(SHARE)], *[gin.at[n] for n in range(SHARE)]),
        sems,
    )
    if last:
        copies.append(pltpu.make_async_copy(dq_before, dqa, sems.at[2 * SHARE + 1]))
        copies[-1].start()
    else:
        dqa[...] = jnp.zeros_like(dqa)
    dka[...] = jnp.zeros_like(dka)
    dva[...] = jnp.zeros_like(dva)
    vs[:, HEAD:] = jnp.full((spans * SPAN, HEAD), -1.0, BF16)
    copies[0].wait()

    def copy_span(n, carry):
        rows = rows_at(n, SPAN)
        ks[rows, :] = kvin[span_rows(meta[n], 0), :]
        vs[rows, :HEAD] = kvin[span_rows(meta[n], 1), :]
        return carry

    lax.fori_loop(0, spans, copy_span, 0, unroll=8)
    for block in range(spans // SUBS):
        kt[part_slice(block, HEAD), :] = ks[part_slice(block, BLOCK), :].astype(F32).T.astype(BF16)
    pattern = mask_pattern()
    lane = lax.broadcasted_iota(jnp.int32, (SPAN, HEAD), 1)
    for copy in copies[1:]:
        copy.wait()
    for i in range(QSPANS):
        slot, half = i // 2, i % 2
        tokens = span_slice(half)
        extra = gin[slot, tokens, WIDTH:].astype(F32)
        for h in range(GROUP):
            rows = part_slice(i * GROUP + h, SPAN)
            qs[rows, :] = qin[slot, tokens, head_cols(h)]
            gs[rows, :HEAD] = gin[slot, tokens, head_cols(h)]
            ours = jnp.logical_and(lane % GROUP == h, lane < 3 * GROUP)
            gs[rows, HEAD:] = jnp.where(ours, extra, 0.0).astype(BF16)
        tops, sums = [], []
        for shift in range(SHARE):
            row = ((slot - shift) % SHARE) * 2 + half
            tops.append(stats[shift][row : row + 1, :])
            sums.append(stats[shift][QSPANS + row : QSPANS + row + 1, :])
        top = functools.reduce(jnp.maximum, tops)
        total = sum(s * jnp.exp2(t - top) for s, t in zip(sums, tops))
        lt[part_slice(i, 8), :] = jnp.broadcast_to(top + jnp.log(total) * LOG2E, (8, COLS))

    def turn(index, carry):
        todo = [step_of(meta, spans, index * TURN + u) for u in range(TURN)]
        key_rows = [rows_at(block, BLOCK) for _, block, _ in todo]
        query_rows = [rows_at(q_at, COLS) for q_at, _, _ in todo]
        scores, grad_probs = [], []
        for kr, qr in zip(key_rows, query_rows):
            scores.append(dot(ks[kr, :], qs[qr, :], 1, 1))
            grad_probs.append(dot(vs[kr, :], gs[qr, :], 1, 1))
        probs, grad_scores = [], []
        for u, (q_at, block, query_pos) in enumerate(todo):
            log_total = lt[rows_at(q_at, 8), :][None]
            low, low_grad = [], []
            for sub in range(SUBS):
                gap = (query_pos - meta[spans + block * SUBS + sub]) * SPAN
                rows = part_slice(sub, SPAN)
                part = scores[u][rows].reshape(SPAN // 8, 8, COLS) * SCALE2 - log_total
                part = jnp.where(pattern <= gap, jnp.exp2(part.reshape(SPAN, COLS)), 0.0)
                low.append(part.astype(BF16))
                low_grad.append((part * grad_probs[u][rows]).astype(BF16))
            probs.append(jnp.concatenate(low, axis=0))
            grad_scores.append(jnp.concatenate(low_grad, axis=0))
        to_value, to_key, to_query = [], [], []
        for u, (_, block, _) in enumerate(todo):
            to_value.append(dot(probs[u], gs[query_rows[u], :HEAD], 1, 0))
            to_key.append(dot(grad_scores[u], qs[query_rows[u], :], 1, 0))
            to_query.append(dot(kt[rows_at(block, HEAD), :], grad_scores[u], 1, 0))
        for u, (q_at, _, _) in enumerate(todo):
            dva[key_rows[u], :] += to_value[u]
            dka[key_rows[u], :] += to_key[u]
            dqa[rows_at(q_at, HEAD), :] += to_query[u]
        return carry

    lax.fori_loop(0, steps // TURN, turn, 0)
    copies = []
    if last:
        for slot in reversed(range(SHARE)):
            out = own if slot == 0 else others.at[slot - 1]
            for half in range(2):
                full = dqa[part_slice(2 * slot + half, HEAD), :].T * SCALE
                for h in range(GROUP):
                    out[span_slice(half), head_cols(h)] = full[part_slice(h, SPAN)].astype(out.dtype)
            copies.append(pltpu.make_async_copy(out, dq_refs[slot], sems.at[slot]))
            copies[-1].start()
    else:
        copies.append(pltpu.make_async_copy(dqa, dq_ref, sems.at[0]))
        copies[-1].start()

    def place_span(n, carry):
        rows = rows_at(n, SPAN)
        dkv[span_rows(meta[n], 0), :] = (dka[rows, :] * SCALE).astype(dkv.dtype)
        dkv[span_rows(meta[n], 1), :] = dva[rows, :].astype(dkv.dtype)
        return carry

    lax.fori_loop(0, spans, place_span, 0, unroll=8)
    copies.append(pltpu.make_async_copy(dkv, dkv_ref, sems.at[SHARE]))
    copies[-1].start()
    for copy in copies:
        copy.wait()


def query_part_kernel(peers, d0, d1, d2, d3, w_ref, out_ref):
    query = d0[...]
    for part in (d1, d2, d3):
        query = query + part[...].astype(F32)
    query = query.astype(BF16)
    feats = out_ref.shape[2]
    for s in range(out_ref.shape[0]):
        out_ref[s, :, :] = dot(query, w_ref[rows_at(peers[s], feats), :], 1, 1)


def project_kernel(peers, dkv_ref, part_ref, wk_ref, wv_ref, o0, o1, o2, o3):
    tokens, feats = o0.shape
    sums = jnp.zeros((2 * tokens, HEAD), F32)
    for member in range(dkv_ref.shape[0] // (2 * tokens)):
        sums = sums + dkv_ref[part_slice(member, 2 * tokens), :].astype(F32)
    sums = sums.astype(BF16)
    for s, out in enumerate((o0, o1, o2, o3)):
        rows = rows_at(peers[s], feats)
        total = part_ref[s, :, :] + dot(sums[:tokens], wk_ref[rows, :], 1, 1)
        total = total + dot(sums[tokens:], wv_ref[rows, :], 1, 1)
        out[...] = total.astype(out.dtype)


VMEM = pl.BlockSpec(memory_space=pltpu.VMEM)
SMEM = pl.BlockSpec(memory_space=pltpu.SMEM)
HBM = pl.BlockSpec(memory_space=pltpu.HBM)
LARGE = pltpu.CompilerParams(vmem_limit_bytes=60 * 1024 * 1024)
SMALL = pltpu.CompilerParams(vmem_limit_bytes=16 * 1024 * 1024)


def shape(dims, dtype):
    return jax.ShapeDtypeStruct(dims, dtype)


def step_tables(span_pos, side, member, share, members, steps):
    spans = 2 * members
    cut = span_pos.reshape(SIDES, members, SHARE, 2)
    key_pos = lax.dynamic_slice_in_dim(cut, share, 1, axis=2).reshape(SIDES, spans)
    key_pos = jnp.where(side == 0, key_pos, key_pos[::-1])
    ids = jnp.arange(spans, dtype=jnp.int32)
    rank = jnp.sum((key_pos[:, None, :] < key_pos[:, :, None]).astype(jnp.int32), axis=2)
    placed = rank[:, None, :] == ids[None, :, None]
    order = jnp.sum(jnp.where(placed, ids[None, None, :], 0), axis=2)
    sorted_pos = jnp.sum(jnp.where(placed, key_pos[:, None, :], 0), axis=2)
    slots = jnp.arange(SHARE, dtype=jnp.int32)
    source = ((side * members + member) * SHARE + (share + SHARE - slots) % SHARE) * 2
    places = jnp.arange(span_pos.shape[0], dtype=jnp.int32)
    query_pos = [
        jnp.sum(jnp.where(places[None, :] == source[:, None] + h, span_pos[None, :], 0), axis=1)
        for h in range(2)
    ]
    blocks = [
        (jnp.sum((key_pos[:, None, :] <= qp[None, :, None]).astype(jnp.int32), axis=2) + SUBS - 1)
        // SUBS
        for qp in query_pos
    ]
    first, other = blocks[0][:, :, None], blocks[1][:, :, None]
    at = jnp.arange(steps // SHARE, dtype=jnp.int32)[None, None, :]
    second = at >= first
    block = jnp.where(second, at - first, at)
    used = jnp.logical_or(jnp.logical_not(second), block < other)
    q_at = jnp.where(second, 1, 0) + 2 * slots[None, :, None]
    pos = jnp.where(second, query_pos[1][None, :, None], query_pos[0][None, :, None])
    table = jnp.stack([q_at, jnp.where(used, block, 0), jnp.where(used, pos, -1)], axis=3)
    return jnp.concatenate([order, sorted_pos, table.reshape(SIDES, -1)], axis=1)


def local(q, k, v, o, g, w_query, key_weight, value_weight, span_pos):
    tokens = q.shape[0]
    cycle = lax.axis_size("ctx")
    tp_size = lax.axis_size("tp")
    members = cycle // SHARE // SIDES
    spans = 2 * members
    half_rows = 2 * spans * SPAN
    steps = SHARE * ((spans + 1 + 2 * (SUBS - 1)) // SUBS)
    index = lax.axis_index("ctx")
    share, member, side = index % SHARE, index // SHARE % members, index // (SHARE * members)

    def device(side_at, member_at, share_at):
        return (side_at % SIDES * members + member_at) * SHARE + share_at % SHARE

    places = [(a, b, c) for a in range(SIDES) for b in range(members) for c in range(SHARE)]
    key_groups = [
        [device(a, b, c) for b in range(members)] for a in range(SIDES) for c in range(SHARE)
    ]

    def exchanged(array):
        return lax.all_to_all(array, "ctx", 0, 0, tiled=True, axis_index_groups=key_groups)

    def shifted(array, by):
        return lax.ppermute(array, "ctx", [(device(a, b, c), device(a, b, c + by)) for a, b, c in places])

    def crossed(array):
        return lax.ppermute(array, "ctx", [(device(a, b, c), device(a + 1, b, c)) for a, b, c in places])

    copies = pl.pallas_call(
        tile_kernel,
        out_shape=shape((half_rows, HEAD), BF16),
        in_specs=[VMEM] * 2,
        out_specs=VMEM,
        name="tile",
    )(k, v)
    kv_own = exchanged(copies)
    queries = [q] + [shifted(q, s) for s in range(1, SHARE)]
    packed = pl.pallas_call(
        pack_kernel,
        out_shape=shape((tokens, WIDTH + HEAD), BF16),
        in_specs=[VMEM] * 2,
        out_specs=VMEM,
        name="pack",
    )(g, o)
    packs = [packed] + [shifted(packed, s) for s in range(1, SHARE)]
    meta = step_tables(span_pos, side, member, share, members, steps)
    meta_own, meta_other = meta[0], meta[1]
    kv_other = crossed(kv_own)

    def stats_of(table, kv, before):
        return pl.pallas_call(
            functools.partial(stats_kernel, spans, steps),
            out_shape=shape((2 * QSPANS, COLS), F32),
            in_specs=[SMEM] + [HBM] * 5 + [VMEM],
            out_specs=VMEM,
            scratch_shapes=[
                pltpu.VMEM((half_rows, HEAD), BF16),
                pltpu.VMEM((SHARE, tokens, WIDTH), BF16),
                pltpu.VMEM((spans * SPAN, HEAD), BF16),
                pltpu.VMEM((QSPANS * COLS, HEAD), BF16),
                pltpu.VMEM((QSPANS * 8, COLS), F32),
                pltpu.VMEM((QSPANS * 8, COLS), F32),
                pltpu.SemaphoreType.DMA((5,)),
            ],
            compiler_params=LARGE,
            cost_estimate=pl.CostEstimate(
                flops=1 << 30, bytes_accessed=1 << 22, transcendentals=1 << 22
            ),
            name="stats",
        )(table, kv, *queries, before)

    empty = jnp.concatenate(
        [jnp.full((QSPANS, COLS), NEG, F32), jnp.zeros((QSPANS, COLS), F32)], axis=0
    )
    stats = stats_of(meta_other, kv_other, stats_of(meta_own, kv_own, empty))
    all_stats = [stats] + [shifted(stats, s) for s in range(1, SHARE)]

    def grads_of(table, kv, last, extra_in, outs, extra_scratch):
        return pl.pallas_call(
            functools.partial(grads_kernel, spans, steps, last),
            out_shape=outs,
            in_specs=[SMEM] + [HBM] * 9 + [VMEM] * 4 + [HBM] * len(extra_in),
            out_specs=[HBM] * len(outs),
            scratch_shapes=[
                pltpu.VMEM((half_rows, HEAD), BF16),
                pltpu.VMEM((SHARE, tokens, WIDTH), BF16),
                pltpu.VMEM((SHARE, tokens, WIDTH + HEAD), BF16),
                pltpu.VMEM((half_rows, HEAD), outs[0].dtype),
                *extra_scratch,
                pltpu.VMEM((spans * SPAN, HEAD), BF16),
                pltpu.VMEM((spans * SPAN, 2 * HEAD), BF16),
                pltpu.VMEM((spans // SUBS * HEAD, BLOCK), BF16),
                pltpu.VMEM((spans * SPAN, HEAD), F32),
                pltpu.VMEM((spans * SPAN, HEAD), F32),
                pltpu.VMEM((QSPANS * COLS, HEAD), BF16),
                pltpu.VMEM((QSPANS * COLS, 2 * HEAD), BF16),
                pltpu.VMEM((QSPANS * 8, COLS), F32),
                pltpu.VMEM((QSPANS * HEAD, COLS), F32),
                pltpu.SemaphoreType.DMA((2 * SHARE + 2,)),
            ],
            compiler_params=LARGE,
            cost_estimate=pl.CostEstimate(
                flops=1 << 31, bytes_accessed=1 << 23, transcendentals=1 << 22
            ),
            name="grads",
        )(table, kv, *queries, *packs, *all_stats, *extra_in)

    dkv_other, dq_before = grads_of(
        meta_other,
        kv_other,
        False,
        [],
        [shape((half_rows, HEAD), BF16), shape((QSPANS * HEAD, COLS), F32)],
        [],
    )
    dkv_crossed = crossed(dkv_other)
    dkv_own, *dqs = grads_of(
        meta_own,
        kv_own,
        True,
        [dq_before],
        [shape((half_rows, HEAD), F32), shape((tokens, WIDTH), F32)]
        + [shape((tokens, WIDTH), BF16)] * (SHARE - 1),
        [pltpu.VMEM((tokens, WIDTH), F32), pltpu.VMEM((SHARE - 1, tokens, WIDTH), BF16)],
    )
    dkv_parts = exchanged((dkv_own + dkv_crossed.astype(F32)).astype(BF16))
    dq_parts = [shifted(dqs[s], -s) for s in range(1, SHARE)]
    peers = (lax.axis_index("tp") + jnp.arange(tp_size, dtype=jnp.int32)) % tp_size
    feats = w_query.shape[0] // tp_size
    query_part = pl.pallas_call(
        query_part_kernel,
        out_shape=shape((tp_size, tokens, feats), F32),
        in_specs=[SMEM] + [VMEM] * 5,
        out_specs=VMEM,
        compiler_params=SMALL,
        name="query_part",
    )(peers, dqs[0], *dq_parts, w_query)
    own, *pieces = pl.pallas_call(
        project_kernel,
        out_shape=[shape((tokens, feats), F32)] + [shape((tokens, feats), BF16)] * (tp_size - 1),
        in_specs=[SMEM] + [VMEM] * 4,
        out_specs=[VMEM] * tp_size,
        compiler_params=SMALL,
        name="project",
    )(peers, dkv_parts, query_part, key_weight, value_weight)
    for s in range(1, tp_size):
        pairs = [(d, (d + s) % tp_size) for d in range(tp_size)]
        own = own + lax.ppermute(pieces[s - 1], "tp", pairs).astype(F32)
    return own.astype(BF16)


def solution(mesh):
    row, col = P("ctx", "tp"), P(None, "tp")
    in_specs = (row, row, row, row, row, col, col, col, P())
    return jax.shard_map(local, mesh=mesh, in_specs=in_specs, out_specs=row, check_vma=False)
```

time: 133 us -> 114 us (0.86)
  waiting for transfers between devices: 46.1 us -> 31 us
  matrix products: 3.42 us -> 0 us
  Pallas kernels: 32.4 us -> 30.4 us
    all_to_all x2, waiting for transfers between devices: 29.4 us -> 14.7 us  [exchanged(): lax.all_to_all(array, 'ctx', 0, 0, tiled=True, axis_index_groups=key_groups)]
    ppermute x12 -> x17, starting transfers between devices: 20.1 us -> 26.7 us  [the longest x12 12.7 us: shifted(): lax.ppermute(array, 'ctx', [(device(a, b, c), device(a, b, c + by)) for a...]
    all_to_all x2, starting transfers between devices: 17.7 us -> 12.3 us  [exchanged(): lax.all_to_all(array, 'ctx', 0, 0, tiled=True, axis_index_groups=key_groups)]
    dot_general x3 -> x0, matrix products: 3.42 us -> none  [dot(): lax.dot_general(left, right, (((left_dim,), (right_dim,)), ((), ())), pre...]
    pallas_call x3 -> x8, Pallas kernels: 32.4 us -> 30.4 us  [the longest x2 15.1 us: grads_of(): pl.pallas_call(functools.partial(grads_kernel, spans, steps, last), out_s...]
    unnamed x30 -> x46, local copies, waits for them, and re-layouts: 5.56 us -> 7.52 us
    convert_element_type x1 -> x2, other arithmetic: 1.67 us -> 3.03 us  [the longest x1 2.3 us: local(): dkv_parts = exchanged((dkv_own + dkv_crossed.astype(F32)).astype(BF16))]
    broadcast_in_dim x3 -> x0, local copies, waits for them, and re-layouts: 1.35 us -> none  [the longest x1 1.17 us: local(): jnp.broadcast_to(own_kv[None], (members,) + own_kv.shape).reshape(-1, HEAD)]
  transfers between devices with their start and end apart: 14 -> 19, of which waited for: 7 -> 12; matrix products, arithmetic and copies ran while one was open for 3% -> 2% of each run, Pallas kernels for 1% -> 19%
where the time goes in v2:
time: 114 us; the launch traced here: 113 us
  starting transfers between devices  39.1 us (34%)
  waiting for transfers between devices  31 us (27%)
  Pallas kernels  30.4 us (27%)
  local copies, waits for them, and re-layouts  8.66 us (8%)
  other arithmetic  3.99 us (4%)
    pallas_call x2, Pallas kernels, grads_of(): pl.pallas_call(functools.partial(grads_kernel, spans, steps, last), out_s...  15.1 us
    all_to_all x2, waiting for transfers between devices, exchanged(): lax.all_to_all(array, 'ctx', 0, 0, tiled=True, axis_index_groups=key_groups)  14.7 us
    ppermute x12, starting transfers between devices, shifted(): lax.ppermute(array, 'ctx', [(device(a, b, c), device(a, b, c + by)) for a...  12.7 us
    all_to_all x2, starting transfers between devices, exchanged(): lax.all_to_all(array, 'ctx', 0, 0, tiled=True, axis_index_groups=key_groups)  12.3 us
    pallas_call x2, Pallas kernels, stats_of(): pl.pallas_call(functools.partial(stats_kernel, spans, steps), out_shape=s...  9.02 us
    ppermute x3, starting transfers between devices, local(): own = own + lax.ppermute(pieces[s - 1], 'tp', pairs).astype(F32)  8.27 us
    ppermute x12, waiting for transfers between devices, shifted(): lax.ppermute(array, 'ctx', [(device(a, b, c), device(a, b, c + by)) for a...  7.87 us
    unnamed x46, local copies, waits for them, and re-layouts  7.52 us
  transfers between devices with their start and end apart: 19, of which 12 were waited for; matrix products, arithmetic and copies ran while one was open for 2% of the time, Pallas kernels for 19%

profile of v2, /device:TPU:1, one launch (start us, length us, event | category | flops | bytes accessed | tf_op | source)
XLA Modules:
  0.0 113.4 jit_solution(8714718908478001565)
XLA Ops:
  0.0 3.3 %collective-permute-start.2 = (bf16[128,512]{1,0:T(8,128)(2,1)}, bf16[128,512]{1,0:T(8,128)(2,1)S(1)}, u32[]{:S(2)}, u32[]{:S(2)}) collective-permute-start(bf16[128,512]{1,0:T(8,128)(2,1)} %refs_2_.3), channel_id=1, source_target_pairs={{0,12},{4,0},{8,4},{12,8},{16,28},{20,16},{24,20},{28,24},{32,44},... | collective-permute-start | bytes 393224 | tf_op jit(solution)/shard_map/ppermute | solution.py:358
  4.4 1.8 %pack.1.refs_6_ = bf16[128,640]{1,0:T(8,128)(2,1)} custom-call(bf16[128,512]{1,0:T(8,128)(2,1)} %g_ref.1, bf16[128,512]{1,0:T(8,128)(2,1)} %o_ref.1), custom_call_target="tpu_custom_call" | custom-call | tf_op jit(solution)/shard_map/pack/pallas_call | solution.py:372
  6.2 2.1 %collective-permute-start.5 = (bf16[128,640]{1,0:T(8,128)(2,1)}, bf16[128,640]{1,0:T(8,128)(2,1)S(1)}, u32[]{:S(2)}, u32[]{:S(2)}) collective-permute-start(bf16[128,640]{1,0:T(8,128)(2,1)} %pack.1.refs_6_), channel_id=1, source_target_pairs={{0,12},{4,0},{8,4},{12,8},{16,28},{20,16},{24,20},{28,24},{32,44},... | collective-permute-start | bytes 491528 | tf_op jit(solution)/shard_map/ppermute | solution.py:358
  8.3 1.7 %tile.1 = bf16[2048,128]{1,0:T(8,128)(2,1)} custom-call(bf16[128,128]{1,0:T(8,128)(2,1)} %k_ref.1, bf16[128,128]{1,0:T(8,128)(2,1)} %v_ref.1), custom_call_target="tpu_custom_call" | custom-call | tf_op jit(solution)/shard_map/tile/pallas_call | solution.py:363
  10.0 8.2 %all-to-all-start = ((bf16[8,256,128]{2,1,0:T(8,128)(2,1)}), bf16[8,256,128]{2,1,0:T(8,128)(2,1)S(1)}, u32[]{:S(2)}, u32[]{:S(2)}) async-start(bf16[8,256,128]{2,1,0:T(8,128)(2,1)} %bitcast.8), calls=%async_computation | async-start | bytes 1048576 | tf_op jit(solution)/shard_map/all_to_all | solution.py:355
  19.5 14.4 %all-to-all-done = bf16[8,256,128]{2,1,0:T(8,128)(2,1)S(1)} async-done(((bf16[8,256,128]{2,1,0:T(8,128)(2,1)}), bf16[8,256,128]{2,1,0:T(8,128)(2,1)S(1)}, u32[]{:S(2)}, u32[]{:S(2)}) %all-to-all-start) | async-done | bytes 524320 | tf_op jit(solution)/shard_map/all_to_all | solution.py:355
  33.8 2.9 %collective-permute-start.6 = (bf16[2048,128]{1,0:T(8,128)(2,1)S(1)}, bf16[2048,128]{1,0:T(8,128)(2,1)S(1)}, u32[]{:S(2)}, u32[]{:S(2)}) collective-permute-start(bf16[2048,128]{1,0:T(8,128)(2,1)S(1)} %bitcast.9), channel_id=1, source_target_pairs={{0,128},{4,132},{8,136},{12,140},{16,144},{20,148},{24,152},{28,15... | collective-permute-start | bytes 1572872 | tf_op jit(solution)/shard_map/ppermute | solution.py:361
  37.6 1.2 %collective-permute-start.4 = (bf16[128,640]{1,0:T(8,128)(2,1)}, bf16[128,640]{1,0:T(8,128)(2,1)S(1)}, u32[]{:S(2)}, u32[]{:S(2)}) collective-permute-start(bf16[128,640]{1,0:T(8,128)(2,1)} %pack.1.refs_6_), channel_id=1, source_target_pairs={{0,8},{4,12},{8,0},{12,4},{16,24},{20,28},{24,16},{28,20},{32,40},... | collective-permute-start | bytes 491528 | tf_op jit(solution)/shard_map/ppermute | solution.py:358
  39.5 4.5 %stats.2.before = f32[16,256]{1,0:T(8,128)} custom-call(s32[92]{0:T(128)} %get-tuple-element.38.meta.refs_0_, bf16[2048,128]{1,0:T(8,128)(2,1)} %bitcast.10, bf16[128,512]{1,0:T(8,128)(2,1)} %refs_2_.3, bf16[128,512]{1,0:T(8,128)(2,1)} %copy-done.16, bf16[128,512]{1,0:T(8,128)(2,1)} %copy-done.15, bf16[128,512]{1,0:T(8,128)(2,1)} %copy-done.14, ...), custom_call_target="tpu_custom_call" | custom-call | flops 1073741824 | bytes 4194304 | tf_op jit(solution)/shard_map/stats/pallas_call | solution.py:385
  44.1 1.9 %collective-permute-done.6.kv_ref.refs_1_ = bf16[2048,128]{1,0:T(8,128)(2,1)S(1)} collective-permute-done((bf16[2048,128]{1,0:T(8,128)(2,1)S(1)}, bf16[2048,128]{1,0:T(8,128)(2,1)S(1)}, u32[]{:S(2)}, u32[]{:S(2)}) %collective-permute-start.6) | collective-permute-done | bytes 524320 | tf_op jit(solution)/shard_map/ppermute | solution.py:361
  46.0 0.8 copy-done.10
  46.8 4.5 %stats.3.refs_10_ = f32[16,256]{1,0:T(8,128)} custom-call(s32[92]{0:T(128)} %get-tuple-element.37.meta.refs_0_, bf16[2048,128]{1,0:T(8,128)(2,1)} %copy-done.10, bf16[128,512]{1,0:T(8,128)(2,1)} %refs_2_.3, bf16[128,512]{1,0:T(8,128)(2,1)} %copy-done.16, bf16[128,512]{1,0:T(8,128)(2,1)} %copy-done.15, bf16[128,512]{1,0:T(8,128)(2,1)} %copy-done.14, ...), custom_call_target="tpu_custom_call" | custom-call | flops 1073741824 | bytes 4194304 | tf_op jit(solution)/shard_map/stats/pallas_call | solution.py:385
  51.3 0.8 collective-permute-start.9
  54.2 2.2 %collective-permute-done.8.refs_12_ = f32[16,256]{1,0:T(8,128)S(1)} collective-permute-done((f32[16,256]{1,0:T(8,128)}, f32[16,256]{1,0:T(8,128)S(1)}, u32[]{:S(2)}, u32[]{:S(2)}) %collective-permute-start.8) | collective-permute-done | bytes 16416 | tf_op jit(solution)/shard_map/ppermute | solution.py:358
  57.6 7.2 %grads.2 = (bf16[2048,128]{1,0:T(8,128)(2,1)}, f32[1024,256]{1,0:T(8,128)}) custom-call(s32[92]{0:T(128)} %get-tuple-element.37.meta.refs_0_, bf16[2048,128]{1,0:T(8,128)(2,1)} %copy-done.10, bf16[128,512]{1,0:T(8,128)(2,1)} %refs_2_.3, bf16[128,512]{1,0:T(8,128)(2,1)} %copy-done.16, bf16[128,512]{1,0:T(8,128)(2,1)} %copy-done.15, ...), custom_call_target="tpu_custom_call" | custom-call | flops 2147483648 | bytes 8388608 | tf_op jit(solution)/shard_map/grads/pallas_call | solution.py:413
  64.8 2.9 %collective-permute-start.10 = (bf16[2048,128]{1,0:T(8,128)(2,1)}, bf16[2048,128]{1,0:T(8,128)(2,1)S(1)}, u32[]{:S(2)}, u32[]{:S(2)}) collective-permute-start(bf16[2048,128]{1,0:T(8,128)(2,1)} %get-tuple-element.18), channel_id=1, source_target_pairs={{0,128},{4,132},{8,136},{12,140},{16,144},{20,148},{24,152},{28,15... | collective-permute-start | bytes 1572872 | tf_op jit(solution)/shard_map/ppermute | solution.py:361
  67.7 7.9 %grads.3 = (f32[2048,128]{1,0:T(8,128)}, f32[128,512]{1,0:T(8,128)}, bf16[128,512]{1,0:T(8,128)(2,1)}, bf16[128,512]{1,0:T(8,128)(2,1)}, bf16[128,512]{1,0:T(8,128)(2,1)}) custom-call(s32[92]{0:T(128)} %get-tuple-element.38.meta.refs_0_, bf16[2048,128]{1,0:T(8,128)(2,1)} %bitcast.11, bf16[128,512]{1,0:T(8,128)(2,1)} %refs_2_.3, bf16[128,512]{1,0:T(8,128)(2,1)} %copy-done.16, ...), custom_call_target="tpu_custom_call" | custom-call | flops 2147483648 | bytes 8388608 | tf_op jit(solution)/shard_map/grads/pallas_call | solution.py:413
  75.7 2.3 %add_convert_fusion = bf16[2048,128]{1,0:T(8,128)(2,1)} fusion(f32[2048,128]{1,0:T(8,128)} %get-tuple-element.17, bf16[2048,128]{1,0:T(8,128)(2,1)S(1)} %collective-permute-done.10), kind=kLoop, calls=%fused_computation | loop fusion | flops 786432 | bytes 2097152 | tf_op jit(solution)/shard_map/convert_element_type | solution.py:460
  78.0 4.1 %all-to-all-start.1 = ((bf16[8,256,128]{2,1,0:T(8,128)(2,1)}), bf16[8,256,128]{2,1,0:T(8,128)(2,1)}, u32[]{:S(2)}, u32[]{:S(2)}) async-start(bf16[8,256,128]{2,1,0:T(8,128)(2,1)} %bitcast.4), calls=%async_computation.1 | async-start | bytes 1048576 | tf_op jit(solution)/shard_map/all_to_all | solution.py:355
  82.1 1.3 %collective-permute-start.11 = (bf16[128,512]{1,0:T(8,128)(2,1)S(1)}, bf16[128,512]{1,0:T(8,128)(2,1)S(1)}, u32[]{:S(2)}, u32[]{:S(2)}) collective-permute-start(bf16[128,512]{1,0:T(8,128)(2,1)S(1)} %copy-done.19), channel_id=1, source_target_pairs={{0,12},{4,0},{8,4},{12,8},{16,28},{20,16},{24,20},{28,24},{32,44},... | collective-permute-start | bytes 393224 | tf_op jit(solution)/shard_map/ppermute | solution.py:358
  83.4 1.5 %collective-permute-start.12 = (bf16[128,512]{1,0:T(8,128)(2,1)S(1)}, bf16[128,512]{1,0:T(8,128)(2,1)S(1)}, u32[]{:S(2)}, u32[]{:S(2)}) collective-permute-start(bf16[128,512]{1,0:T(8,128)(2,1)S(1)} %copy-done.18), channel_id=1, source_target_pairs={{0,8},{4,12},{8,0},{12,4},{16,24},{20,28},{24,16},{28,20},{32,40},... | collective-permute-start | bytes 393224 | tf_op jit(solution)/shard_map/ppermute | solution.py:358
  84.9 1.1 collective-permute-done.11.d1
  86.0 2.8 %collective-permute-done.12.d2 = bf16[128,512]{1,0:T(8,128)(2,1)S(1)} collective-permute-done((bf16[128,512]{1,0:T(8,128)(2,1)S(1)}, bf16[128,512]{1,0:T(8,128)(2,1)S(1)}, u32[]{:S(2)}, u32[]{:S(2)}) %collective-permute-start.12) | collective-permute-done | bytes 131104 | tf_op jit(solution)/shard_map/ppermute | solution.py:358
  90.8 0.9 copy-done.5
  91.7 0.9 copy-done.7
  92.6 1.3 %query_part.1.part_ref = f32[4,128,512]{2,1,0:T(8,128)S(1)} custom-call(s32[4]{0:T(128)S(1)} %and_select_fusion.3.peers, f32[128,512]{1,0:T(8,128)S(1)} %copy-done.3, bf16[128,512]{1,0:T(8,128)(2,1)S(1)} %collective-permute-done.11.d1, bf16[128,512]{1,0:T(8,128)(2,1)S(1)} %copy-done.5, bf16[128,512]{1,0:T(8,128)(2,1)S(1)} %copy-done.7, ...), custom_call_target="tpu_custom_call" | custom-call | tf_op jit(solution)/shard_map/query_part/pallas_call | solution.py:464
  94.4 1.0 copy-done.1
  95.4 1.0 copy-done.2
  96.4 1.5 %project.1 = (f32[128,512]{1,0:T(8,128)S(1)}, bf16[128,512]{1,0:T(8,128)(2,1)S(1)}, bf16[128,512]{1,0:T(8,128)(2,1)S(1)}, bf16[128,512]{1,0:T(8,128)(2,1)S(1)}) custom-call(s32[4]{0:T(128)S(1)} %and_select_fusion.3.peers, bf16[2048,128]{1,0:T(8,128)(2,1)} %bitcast.5.dkv_ref, f32[4,128,512]{2,1,0:T(8,128)S(1)} %query_part.1.part_ref, ...), custom_call_target="tpu_custom_call" | custom-call | tf_op jit(solution)/shard_map/project/pallas_call | solution.py:472
  97.9 7.8 %collective-permute-start.14 = (bf16[128,512]{1,0:T(8,128)(2,1)S(1)}, bf16[128,512]{1,0:T(8,128)(2,1)S(1)}, u32[]{:S(2)}, u32[]{:S(2)}) collective-permute-start(bf16[128,512]{1,0:T(8,128)(2,1)S(1)} %get-tuple-element.24), channel_id=1, source_target_pairs={{0,1},{1,2},{2,3},{3,0},{4,5},{5,6},{6,7},{7,4},{8,9},{9,10},{10,1... | collective-permute-start | bytes 393224 | tf_op jit(solution)/shard_map/ppermute | solution.py:482
  106.2 2.2 %collective-permute-done.14 = bf16[128,512]{1,0:T(8,128)(2,1)S(1)} collective-permute-done((bf16[128,512]{1,0:T(8,128)(2,1)S(1)}, bf16[128,512]{1,0:T(8,128)(2,1)S(1)}, u32[]{:S(2)}, u32[]{:S(2)}) %collective-permute-start.14) | collective-permute-done | bytes 131104 | tf_op jit(solution)/shard_map/ppermute | solution.py:482
  108.4 3.6 %collective-permute-done.15 = bf16[128,512]{1,0:T(8,128)(2,1)S(1)} collective-permute-done((bf16[128,512]{1,0:T(8,128)(2,1)S(1)}, bf16[128,512]{1,0:T(8,128)(2,1)S(1)}, u32[]{:S(2)}, u32[]{:S(2)}) %collective-permute-start.15) | collective-permute-done | bytes 131104 | tf_op jit(solution)/shard_map/ppermute | solution.py:482
  (81 shorter events, 11.5 us)
Async XLA Ops:
  0.0 18.2 %copy-start.9 = (s32[128]{0:T(128)S(1)}, s32[128]{0:T(128)}, u32[]{:S(2)}) copy-start(s32[128]{0:T(128)} %param.17) | copy-start | bytes 1540
  0.0 37.6 %collective-permute-start.2 = (bf16[128,512]{1,0:T(8,128)(2,1)}, bf16[128,512]{1,0:T(8,128)(2,1)S(1)}, u32[]{:S(2)}, u32[]{:S(2)}) collective-permute-start(bf16[128,512]{1,0:T(8,128)(2,1)} %refs_2_.3), channel_id=1, source_target_pairs={{0,12},{4,0},{8,4},{12,8},{16,28},{20,16},{24,20},{28,24},{32,44},... | collective-permute-start | bytes 393224 | tf_op jit(solution)/shard_map/ppermute | solution.py:358
  3.3 35.5 %collective-permute-start.1 = (bf16[128,512]{1,0:T(8,128)(2,1)}, bf16[128,512]{1,0:T(8,128)(2,1)S(1)}, u32[]{:S(2)}, u32[]{:S(2)}) collective-permute-start(bf16[128,512]{1,0:T(8,128)(2,1)} %refs_2_.3), channel_id=1, source_target_pairs={{0,8},{4,12},{8,0},{12,4},{16,24},{20,28},{24,16},{28,20},{32,40},... | collective-permute-start | bytes 393224 | tf_op jit(solution)/shard_map/ppermute | solution.py:358
  3.8 35.0 %collective-permute-start = (bf16[128,512]{1,0:T(8,128)(2,1)}, bf16[128,512]{1,0:T(8,128)(2,1)S(1)}, u32[]{:S(2)}, u32[]{:S(2)}) collective-permute-start(bf16[128,512]{1,0:T(8,128)(2,1)} %refs_2_.3), channel_id=1, source_target_pairs={{0,4},{4,8},{8,12},{12,0},{16,20},{20,24},{24,28},{28,16},{32,36},... | collective-permute-start | bytes 393224 | tf_op jit(solution)/shard_map/ppermute | solution.py:358
  6.2 46.6 %collective-permute-start.5 = (bf16[128,640]{1,0:T(8,128)(2,1)}, bf16[128,640]{1,0:T(8,128)(2,1)S(1)}, u32[]{:S(2)}, u32[]{:S(2)}) collective-permute-start(bf16[128,640]{1,0:T(8,128)(2,1)} %pack.1.refs_6_), channel_id=1, source_target_pairs={{0,12},{4,0},{8,4},{12,8},{16,28},{20,16},{24,20},{28,24},{32,44},... | collective-permute-start | bytes 491528 | tf_op jit(solution)/shard_map/ppermute | solution.py:358
  10.0 23.9 %all-to-all-start = ((bf16[8,256,128]{2,1,0:T(8,128)(2,1)}), bf16[8,256,128]{2,1,0:T(8,128)(2,1)S(1)}, u32[]{:S(2)}, u32[]{:S(2)}) async-start(bf16[8,256,128]{2,1,0:T(8,128)(2,1)} %bitcast.8), calls=%async_computation | async-start | bytes 1048576 | tf_op jit(solution)/shard_map/all_to_all | solution.py:355
  33.8 5.0 %copy-start.8 = (bf16[8,256,128]{2,1,0:T(8,128)(2,1)}, bf16[8,256,128]{2,1,0:T(8,128)(2,1)S(1)}, u32[]{:S(2)}) copy-start(bf16[8,256,128]{2,1,0:T(8,128)(2,1)S(1)} %all-to-all-done) | copy-start | bytes 1572868
  33.8 12.2 %collective-permute-start.6 = (bf16[2048,128]{1,0:T(8,128)(2,1)S(1)}, bf16[2048,128]{1,0:T(8,128)(2,1)S(1)}, u32[]{:S(2)}, u32[]{:S(2)}) collective-permute-start(bf16[2048,128]{1,0:T(8,128)(2,1)S(1)} %bitcast.9), channel_id=1, source_target_pairs={{0,128},{4,132},{8,136},{12,140},{16,144},{20,148},{24,152},{28,15... | collective-permute-start | bytes 1572872 | tf_op jit(solution)/shard_map/ppermute | solution.py:361
  37.6 1.3 %copy-start.14 = (bf16[128,512]{1,0:T(8,128)(2,1)}, bf16[128,512]{1,0:T(8,128)(2,1)S(1)}, u32[]{:S(2)}) copy-start(bf16[128,512]{1,0:T(8,128)(2,1)S(1)} %collective-permute-done.2.q3.refs_5_) | copy-start | bytes 393220
  37.6 15.9 %collective-permute-start.4 = (bf16[128,640]{1,0:T(8,128)(2,1)}, bf16[128,640]{1,0:T(8,128)(2,1)S(1)}, u32[]{:S(2)}, u32[]{:S(2)}) collective-permute-start(bf16[128,640]{1,0:T(8,128)(2,1)} %pack.1.refs_6_), channel_id=1, source_target_pairs={{0,8},{4,12},{8,0},{12,4},{16,24},{20,28},{24,16},{28,20},{32,40},... | collective-permute-start | bytes 491528 | tf_op jit(solution)/shard_map/ppermute | solution.py:358
  38.8 14.7 %collective-permute-start.3 = (bf16[128,640]{1,0:T(8,128)(2,1)}, bf16[128,640]{1,0:T(8,128)(2,1)S(1)}, u32[]{:S(2)}, u32[]{:S(2)}) collective-permute-start(bf16[128,640]{1,0:T(8,128)(2,1)} %pack.1.refs_6_), channel_id=1, source_target_pairs={{0,4},{4,8},{8,12},{12,0},{16,20},{20,24},{24,28},{28,16},{32,36},... | collective-permute-start | bytes 491528 | tf_op jit(solution)/shard_map/ppermute | solution.py:358
  51.3 2.9 %collective-permute-start.9 = (f32[16,256]{1,0:T(8,128)}, f32[16,256]{1,0:T(8,128)S(1)}, u32[]{:S(2)}, u32[]{:S(2)}) collective-permute-start(f32[16,256]{1,0:T(8,128)} %stats.3.refs_10_), channel_id=1, source_target_pairs={{0,12},{4,0},{8,4},{12,8},{16,28},{20,16},{24,20},{28,24},{32,44},... | collective-permute-start | bytes 49160 | tf_op jit(solution)/shard_map/ppermute | solution.py:358
  52.1 4.3 %collective-permute-start.8 = (f32[16,256]{1,0:T(8,128)}, f32[16,256]{1,0:T(8,128)S(1)}, u32[]{:S(2)}, u32[]{:S(2)}) collective-permute-start(f32[16,256]{1,0:T(8,128)} %stats.3.refs_10_), channel_id=1, source_target_pairs={{0,8},{4,12},{8,0},{12,4},{16,24},{20,28},{24,16},{28,20},{32,40},... | collective-permute-start | bytes 49160 | tf_op jit(solution)/shard_map/ppermute | solution.py:358
  52.8 4.0 %copy-start.11 = (bf16[128,640]{1,0:T(8,128)(2,1)}, bf16[128,640]{1,0:T(8,128)(2,1)S(1)}, u32[]{:S(2)}) copy-start(bf16[128,640]{1,0:T(8,128)(2,1)S(1)} %collective-permute-done.5.refs_9_) | copy-start | bytes 491524
  52.8 4.0 %collective-permute-start.7 = (f32[16,256]{1,0:T(8,128)}, f32[16,256]{1,0:T(8,128)S(1)}, u32[]{:S(2)}, u32[]{:S(2)}) collective-permute-start(f32[16,256]{1,0:T(8,128)} %stats.3.refs_10_), channel_id=1, source_target_pairs={{0,4},{4,8},{8,12},{12,0},{16,20},{20,24},{24,28},{28,16},{32,36},... | collective-permute-start | bytes 49160 | tf_op jit(solution)/shard_map/ppermute | solution.py:358
  53.5 3.3 %copy-start.12 = (bf16[128,640]{1,0:T(8,128)(2,1)}, bf16[128,640]{1,0:T(8,128)(2,1)S(1)}, u32[]{:S(2)}) copy-start(bf16[128,640]{1,0:T(8,128)(2,1)S(1)} %collective-permute-done.4.refs_8_) | copy-start | bytes 491524
  53.5 3.3 %copy-start.13 = (bf16[128,640]{1,0:T(8,128)(2,1)}, bf16[128,640]{1,0:T(8,128)(2,1)S(1)}, u32[]{:S(2)}) copy-start(bf16[128,640]{1,0:T(8,128)(2,1)S(1)} %collective-permute-done.3.refs_7_) | copy-start | bytes 491524
  54.2 2.6 %copy-start.20 = (f32[16,256]{1,0:T(8,128)}, f32[16,256]{1,0:T(8,128)S(1)}, u32[]{:S(2)}) copy-start(f32[16,256]{1,0:T(8,128)S(1)} %collective-permute-done.9.refs_13_) | copy-start | bytes 49156
  64.8 10.9 %collective-permute-start.10 = (bf16[2048,128]{1,0:T(8,128)(2,1)}, bf16[2048,128]{1,0:T(8,128)(2,1)S(1)}, u32[]{:S(2)}, u32[]{:S(2)}) collective-permute-start(bf16[2048,128]{1,0:T(8,128)(2,1)} %get-tuple-element.18), channel_id=1, source_target_pairs={{0,128},{4,132},{8,136},{12,140},{16,144},{20,148},{24,152},{28,15... | collective-permute-start | bytes 1572872 | tf_op jit(solution)/shard_map/ppermute | solution.py:361
  75.6 6.5 %copy-start.19 = (bf16[128,512]{1,0:T(8,128)(2,1)S(1)}, bf16[128,512]{1,0:T(8,128)(2,1)}, u32[]{:S(2)}) copy-start(bf16[128,512]{1,0:T(8,128)(2,1)} %get-tuple-element.20) | copy-start | bytes 393220
  75.6 7.8 %copy-start.18 = (bf16[128,512]{1,0:T(8,128)(2,1)S(1)}, bf16[128,512]{1,0:T(8,128)(2,1)}, u32[]{:S(2)}) copy-start(bf16[128,512]{1,0:T(8,128)(2,1)} %get-tuple-element.21) | copy-start | bytes 393220
  75.6 9.3 %copy-start.17 = (bf16[128,512]{1,0:T(8,128)(2,1)S(1)}, bf16[128,512]{1,0:T(8,128)(2,1)}, u32[]{:S(2)}) copy-start(bf16[128,512]{1,0:T(8,128)(2,1)} %get-tuple-element.22) | copy-start | bytes 393220
  75.6 15.2 %copy-start = (bf16[2048,512]{1,0:T(8,128)(2,1)S(1)}, bf16[2048,512]{1,0:T(8,128)(2,1)}, u32[]{:S(2)}) copy-start(bf16[2048,512]{1,0:T(8,128)(2,1)} %w_ref.1) | copy-start | bytes 6291460
  75.6 15.2 %copy-start.3 = (f32[128,512]{1,0:T(8,128)S(1)}, f32[128,512]{1,0:T(8,128)}, u32[]{:S(2)}) copy-start(f32[128,512]{1,0:T(8,128)} %get-tuple-element.19.d0) | copy-start | bytes 786436
  78.0 16.4 %all-to-all-start.1 = ((bf16[8,256,128]{2,1,0:T(8,128)(2,1)}), bf16[8,256,128]{2,1,0:T(8,128)(2,1)}, u32[]{:S(2)}, u32[]{:S(2)}) async-start(bf16[8,256,128]{2,1,0:T(8,128)(2,1)} %bitcast.4), calls=%async_computation.1 | async-start | bytes 1048576 | tf_op jit(solution)/shard_map/all_to_all | solution.py:355
  82.1 3.9 %collective-permute-start.11 = (bf16[128,512]{1,0:T(8,128)(2,1)S(1)}, bf16[128,512]{1,0:T(8,128)(2,1)S(1)}, u32[]{:S(2)}, u32[]{:S(2)}) collective-permute-start(bf16[128,512]{1,0:T(8,128)(2,1)S(1)} %copy-done.19), channel_id=1, source_target_pairs={{0,12},{4,0},{8,4},{12,8},{16,28},{20,16},{24,20},{28,24},{32,44},... | collective-permute-start | bytes 393224 | tf_op jit(solution)/shard_map/ppermute | solution.py:358
  83.4 5.3 %collective-permute-start.12 = (bf16[128,512]{1,0:T(8,128)(2,1)S(1)}, bf16[128,512]{1,0:T(8,128)(2,1)S(1)}, u32[]{:S(2)}, u32[]{:S(2)}) collective-permute-start(bf16[128,512]{1,0:T(8,128)(2,1)S(1)} %copy-done.18), channel_id=1, source_target_pairs={{0,8},{4,12},{8,0},{12,4},{16,24},{20,28},{24,16},{28,20},{32,40},... | collective-permute-start | bytes 393224 | tf_op jit(solution)/shard_map/ppermute | solution.py:358
  84.9 5.3 %collective-permute-start.13 = (bf16[128,512]{1,0:T(8,128)(2,1)S(1)}, bf16[128,512]{1,0:T(8,128)(2,1)S(1)}, u32[]{:S(2)}, u32[]{:S(2)}) collective-permute-start(bf16[128,512]{1,0:T(8,128)(2,1)S(1)} %copy-done.17), channel_id=1, source_target_pairs={{0,4},{4,8},{8,12},{12,0},{16,20},{20,24},{24,28},{28,16},{32,36},... | collective-permute-start | bytes 393224 | tf_op jit(solution)/shard_map/ppermute | solution.py:358
  94.3 1.0 copy-start.1
  97.9 10.5 %collective-permute-start.14 = (bf16[128,512]{1,0:T(8,128)(2,1)S(1)}, bf16[128,512]{1,0:T(8,128)(2,1)S(1)}, u32[]{:S(2)}, u32[]{:S(2)}) collective-permute-start(bf16[128,512]{1,0:T(8,128)(2,1)S(1)} %get-tuple-element.24), channel_id=1, source_target_pairs={{0,1},{1,2},{2,3},{3,0},{4,5},{5,6},{6,7},{7,4},{8,9},{9,10},{10,1... | collective-permute-start | bytes 393224 | tf_op jit(solution)/shard_map/ppermute | solution.py:482
  105.7 6.3 %collective-permute-start.15 = (bf16[128,512]{1,0:T(8,128)(2,1)S(1)}, bf16[128,512]{1,0:T(8,128)(2,1)S(1)}, u32[]{:S(2)}, u32[]{:S(2)}) collective-permute-start(bf16[128,512]{1,0:T(8,128)(2,1)S(1)} %get-tuple-element.25), channel_id=1, source_target_pairs={{0,2},{1,3},{2,0},{3,1},{4,6},{5,7},{6,4},{7,5},{8,10},{9,11},{10,... | collective-permute-start | bytes 393224 | tf_op jit(solution)/shard_map/ppermute | solution.py:482
  106.1 6.6 %collective-permute-start.16 = (bf16[128,512]{1,0:T(8,128)(2,1)S(1)}, bf16[128,512]{1,0:T(8,128)(2,1)S(1)}, u32[]{:S(2)}, u32[]{:S(2)}) collective-permute-start(bf16[128,512]{1,0:T(8,128)(2,1)S(1)} %get-tuple-element.26), channel_id=1, source_target_pairs={{0,3},{1,0},{2,1},{3,2},{4,7},{5,4},{6,5},{7,6},{8,11},{9,8},{10,9... | collective-permute-start | bytes 393224 | tf_op jit(solution)/shard_map/ppermute | solution.py:482
  (10 other events, 7.5 us)

commit v3 on v2

v3 whole, which is shorter than its diff:
```python
import functools
import math

import jax
import jax.numpy as jnp
from jax import lax
from jax.experimental import pallas as pl
from jax.experimental.pallas import tpu as pltpu
from jax.sharding import PartitionSpec as P

HEAD = 128
SPAN = 64
GROUP = 4
SHARE = 4
SIDES = 2
SUBS = 4
BLOCK = SUBS * SPAN
COLS = GROUP * SPAN
WIDTH = GROUP * HEAD
QSPANS = 2 * SHARE
STATS = 3 * QSPANS
SCALE = HEAD ** (-0.5)
LOG2E = math.log2(math.e)
SCALE2 = SCALE * LOG2E
NEG = -1e30
F32 = jnp.float32
BF16 = jnp.bfloat16


def dot(left, right, left_dim, right_dim):
    return lax.dot_general(
        left, right, (((left_dim,), (right_dim,)), ((), ())), preferred_element_type=F32
    )


def rows_at(index, size):
    return pl.ds(pl.multiple_of(index * size, size), size)


def span_rows(slot, value):
    return rows_at(slot // 2 * 4 + slot % 2 + 2 * value, SPAN)


def load_all(sources, buffers, sems):
    copies = [
        pltpu.make_async_copy(source, buffer, sems.at[n])
        for n, (source, buffer) in enumerate(zip(sources, buffers))
    ]
    for copy in copies:
        copy.start()
    return copies


def head_cols(head, first=0):
    return slice(first + head * HEAD, first + (head + 1) * HEAD)


def span_slice(half):
    return slice(half * SPAN, (half + 1) * SPAN)


def part_slice(index, size):
    return slice(index * size, (index + 1) * size)


def tile_kernel(k_ref, v_ref, out_ref):
    tokens = k_ref.shape[0]
    for member in range(out_ref.shape[0] // (2 * tokens)):
        out_ref[part_slice(2 * member, tokens), :] = k_ref[...]
        out_ref[part_slice(2 * member + 1, tokens), :] = v_ref[...]


def pack_kernel(q_ref, g_ref, o_ref, out_ref, start_ref):
    start_ref[:QSPANS, :] = jnp.full((QSPANS, COLS), NEG, F32)
    start_ref[QSPANS:, :] = jnp.zeros((STATS - QSPANS, COLS), F32)
    ones = jnp.ones((8, HEAD), BF16)
    for half in range(2):
        products = []
        for h in range(GROUP):
            rows, tokens = part_slice(half * GROUP + h, SPAN), span_slice(half)
            grad = g_ref[tokens, head_cols(h)]
            out_ref[rows, :HEAD] = q_ref[tokens, head_cols(h)]
            out_ref[rows, HEAD:] = grad
            products.append(grad.astype(F32) * o_ref[tokens, head_cols(h)].astype(F32))
        rest = jnp.concatenate(products, axis=0)
        delta = jnp.zeros((8, COLS), F32)
        for _ in range(3):
            part = rest.astype(BF16)
            delta = delta + dot(ones, part, 1, 1)
            rest = rest - part.astype(F32)
        start_ref[2 * QSPANS + half : 2 * QSPANS + half + 1, :] = delta[:1]


def mask_pattern():
    row = lax.broadcasted_iota(jnp.int32, (SPAN, COLS), 0)
    col = lax.broadcasted_iota(jnp.int32, (SPAN, COLS), 1)
    return row - col % SPAN


def slot_steps(meta, spans, steps, slot):
    count = steps // SHARE
    starts = [2 * spans + 3 * (slot * count + n) for n in range(count)]
    return [(meta[at], meta[at + 1], meta[at + 2]) for at in starts]


def slot_rows(ref, slot):
    return ref.at[part_slice(slot, 2 * COLS)]


def stats_kernel(spans, steps, meta, k_ref, b0, b1, b2, b3, before, out_ref, kin, ks, qs, ms, ls, sems):
    copies = load_all(
        (k_ref, *[b.at[:, :HEAD] for b in (b0, b1, b2, b3)]),
        (kin, *[slot_rows(qs, n) for n in range(SHARE)]),
        sems,
    )
    copies[0].wait()

    def copy_span(n, carry):
        ks[rows_at(n, SPAN), :] = kin[rows_at(meta[n], SPAN), :]
        return carry

    lax.fori_loop(0, spans, copy_span, 0, unroll=8)
    ms[...] = jnp.full_like(ms, NEG)
    ls[...] = jnp.zeros_like(ls)
    pattern = mask_pattern()
    for slot in range(SHARE):
        copies[1 + slot].wait()
        todo = slot_steps(meta, spans, steps, slot)
        scores = [
            dot(ks[rows_at(block, BLOCK), :], qs[rows_at(q_at, COLS), :], 1, 1)
            for q_at, block, _ in todo
        ]
        tops, totals = [], []
        for (_, block, query_pos), score in zip(todo, scores):
            parts = []
            for sub in range(SUBS):
                gap = (query_pos - meta[spans + block * SUBS + sub]) * SPAN
                part = jnp.where(pattern <= gap, score[part_slice(sub, SPAN)] * SCALE2, NEG)
                parts.append(part.reshape(SPAN // 8, 8, COLS))
            top = functools.reduce(jnp.maximum, [jnp.max(part, axis=0) for part in parts])
            tops.append(top)
            totals.append(sum(jnp.sum(jnp.exp2(part - top[None]), axis=0) for part in parts))
        for (q_at, _, _), top, total in zip(todo, tops, totals):
            rows = rows_at(q_at, 8)
            old = ms[rows, :]
            new = jnp.maximum(old, top)
            ls[rows, :] = ls[rows, :] * jnp.exp2(old - new) + total * jnp.exp2(top - new)
            ms[rows, :] = new
    out_ref[2 * QSPANS :, :] = before[2 * QSPANS :, :]
    for i in range(QSPANS):
        run_max, run_sum = ms[part_slice(i, 8), :], ls[part_slice(i, 8), :]
        old_max, old_sum = before[i : i + 1, :], before[QSPANS + i : QSPANS + i + 1, :]
        top = jnp.maximum(jnp.max(run_max, axis=0, keepdims=True), old_max)
        total = jnp.sum(run_sum * jnp.exp2(run_max - top), axis=0, keepdims=True)
        out_ref[i : i + 1, :] = top
        out_ref[QSPANS + i : QSPANS + i + 1, :] = total + old_sum * jnp.exp2(old_max - top)


def grads_kernel(spans, steps, last, *refs):
    meta, k_ref, v_ref = refs[:3]
    blocks, stats, refs = refs[3:7], refs[7:11], refs[11:]
    if last:
        dq_before, dkv_ref, *dq_refs = refs[: 2 + SHARE]
        kin, vin, dkv, own, others, ks, vs, kt, dka, dva, qs, gs, lt, dl, dqa, sems = refs[6:]
    else:
        dkv_ref, dq_ref, kin, vin, dkv, ks, vs, kt, dka, dva, qs, gs, lt, dl, dqa, sems = refs
    copies = load_all(
        (k_ref, v_ref, *[b.at[:, :HEAD] for b in blocks], *[b.at[:, HEAD:] for b in blocks]),
        (
            kin,
            vin,
            *[slot_rows(qs, n) for n in range(SHARE)],
            *[slot_rows(gs, n) for n in range(SHARE)],
        ),
        sems,
    )
    if last:
        before = [dq_before.at[part_slice(n, 2 * HEAD)] for n in range(SHARE)]
        targets = [dqa.at[part_slice(n, 2 * HEAD)] for n in range(SHARE)]
        copies += load_all(before, targets, sems.at[2 * SHARE + 2 :])
    else:
        dqa[...] = jnp.zeros_like(dqa)
    dka[...] = jnp.zeros_like(dka)
    dva[...] = jnp.zeros_like(dva)
    copies[0].wait()
    copies[1].wait()

    def copy_span(n, carry):
        rows = rows_at(n, SPAN)
        ks[rows, :] = kin[rows_at(meta[n], SPAN), :]
        vs[rows, :] = vin[rows_at(meta[n], SPAN), :]
        return carry

    lax.fori_loop(0, spans, copy_span, 0, unroll=8)
    for block in range(spans // SUBS):
        kt[part_slice(block, HEAD), :] = ks[part_slice(block, BLOCK), :].astype(F32).T.astype(BF16)
    pattern = mask_pattern()
    for i in range(QSPANS):
        slot, half = i // 2, i % 2
        delta = stats[slot][2 * QSPANS + half : 2 * QSPANS + half + 1, :]
        dl[part_slice(i, 8), :] = jnp.broadcast_to(delta, (8, COLS))
        tops, sums = [], []
        for shift in range(SHARE):
            row = ((slot - shift) % SHARE) * 2 + half
            tops.append(stats[shift][row : row + 1, :])
            sums.append(stats[shift][QSPANS + row : QSPANS + row + 1, :])
        top = functools.reduce(jnp.maximum, tops)
        total = sum(s * jnp.exp2(t - top) for s, t in zip(sums, tops))
        lt[part_slice(i, 8), :] = jnp.broadcast_to(top + jnp.log(total) * LOG2E, (8, COLS))
    stores = []
    for slot in range(SHARE):
        for copy in copies[2 + slot :: SHARE]:
            copy.wait()
        todo = slot_steps(meta, spans, steps, slot)
        key_rows = [rows_at(block, BLOCK) for _, block, _ in todo]
        query_rows = [rows_at(q_at, COLS) for q_at, _, _ in todo]
        scores, grad_probs = [], []
        for kr, qr in zip(key_rows, query_rows):
            scores.append(dot(ks[kr, :], qs[qr, :], 1, 1))
            grad_probs.append(dot(vs[kr, :], gs[qr, :], 1, 1))
        probs, grad_scores = [], []
        for u, (q_at, block, query_pos) in enumerate(todo):
            log_total, delta = lt[rows_at(q_at, 8), :][None], dl[rows_at(q_at, 8), :][None]
            low, low_grad = [], []
            for sub in range(SUBS):
                gap = (query_pos - meta[spans + block * SUBS + sub]) * SPAN
                rows = part_slice(sub, SPAN)
                part = scores[u][rows].reshape(SPAN // 8, 8, COLS) * SCALE2 - log_total
                part = jnp.where(pattern <= gap, jnp.exp2(part.reshape(SPAN, COLS)), 0.0)
                low.append(part.astype(BF16))
                change = grad_probs[u][rows].reshape(SPAN // 8, 8, COLS) - delta
                low_grad.append((part * change.reshape(SPAN, COLS)).astype(BF16))
            probs.append(jnp.concatenate(low, axis=0))
            grad_scores.append(jnp.concatenate(low_grad, axis=0))
        to_value, to_key, to_query = [], [], []
        for u, (_, block, _) in enumerate(todo):
            to_value.append(dot(probs[u], gs[query_rows[u], :], 1, 0))
            to_key.append(dot(grad_scores[u], qs[query_rows[u], :], 1, 0))
            to_query.append(dot(kt[rows_at(block, HEAD), :], grad_scores[u], 1, 0))
        for u, (q_at, _, _) in enumerate(todo):
            dva[key_rows[u], :] += to_value[u]
            dka[key_rows[u], :] += to_key[u]
            dqa[rows_at(q_at, HEAD), :] += to_query[u]
        store_sem = sems.at[3 * SHARE + 2 + slot]
        if last:
            out = own if slot == 0 else others.at[slot - 1]
            for half in range(2):
                full = dqa[part_slice(2 * slot + half, HEAD), :].T * SCALE
                for h in range(GROUP):
                    out[span_slice(half), head_cols(h)] = full[part_slice(h, SPAN)].astype(out.dtype)
            stores.append(pltpu.make_async_copy(out, dq_refs[slot], store_sem))
        else:
            rows = part_slice(slot, 2 * HEAD)
            stores.append(pltpu.make_async_copy(dqa.at[rows], dq_ref.at[rows], store_sem))
        stores[-1].start()

    def place_span(n, carry):
        rows = rows_at(n, SPAN)
        dkv[span_rows(meta[n], 0), :] = (dka[rows, :] * SCALE).astype(dkv.dtype)
        dkv[span_rows(meta[n], 1), :] = dva[rows, :].astype(dkv.dtype)
        return carry

    lax.fori_loop(0, spans, place_span, 0, unroll=8)
    stores.append(pltpu.make_async_copy(dkv, dkv_ref, sems.at[4 * SHARE + 2]))
    stores[-1].start()
    for store in stores:
        store.wait()


def project_kernel(
    peers, d0, d1, d2, d3, dkv_ref, wk_ref, wv_ref, wq_ref, o0, o1, o2, o3,
    own, others, dkv, wk, wv, sems,
):
    tokens, feats = o0.shape
    copies = load_all(
        (d0, d1, d2, d3, dkv_ref, wk_ref, wv_ref),
        (own, *[others.at[n] for n in range(SHARE - 1)], dkv, wk, wv),
        sems,
    )
    for copy in copies[:SHARE]:
        copy.wait()
    query = own[...]
    for n in range(SHARE - 1):
        query = query + others[n].astype(F32)
    query = query.astype(BF16)
    rows = [rows_at(peers[s], feats) for s in range(SHARE)]
    totals = [dot(query, wq_ref[at, :], 1, 1) for at in rows]
    copies[SHARE].wait()
    sums = jnp.zeros((2 * tokens, HEAD), F32)
    for member in range(dkv.shape[0] // (2 * tokens)):
        sums = sums + dkv[part_slice(member, 2 * tokens), :].astype(F32)
    sums = sums.astype(BF16)
    for copy in copies[SHARE + 1 :]:
        copy.wait()
    for at, total, out in zip(rows, totals, (o0, o1, o2, o3)):
        total = total + dot(sums[:tokens], wk[at, :], 1, 1)
        total = total + dot(sums[tokens:], wv[at, :], 1, 1)
        out[...] = total.astype(out.dtype)


VMEM = pl.BlockSpec(memory_space=pltpu.VMEM)
SMEM = pl.BlockSpec(memory_space=pltpu.SMEM)
HBM = pl.BlockSpec(memory_space=pltpu.HBM)
LARGE = pltpu.CompilerParams(vmem_limit_bytes=60 * 1024 * 1024)
SMALL = pltpu.CompilerParams(vmem_limit_bytes=16 * 1024 * 1024)


def shape(dims, dtype):
    return jax.ShapeDtypeStruct(dims, dtype)


def step_tables(span_pos, side, member, share, members, steps):
    spans = 2 * members
    cut = span_pos.reshape(SIDES, members, SHARE, 2)
    key_pos = lax.dynamic_slice_in_dim(cut, share, 1, axis=2).reshape(SIDES, spans)
    key_pos = jnp.where(side == 0, key_pos, key_pos[::-1])
    ids = jnp.arange(spans, dtype=jnp.int32)
    rank = jnp.sum((key_pos[:, None, :] < key_pos[:, :, None]).astype(jnp.int32), axis=2)
    placed = rank[:, None, :] == ids[None, :, None]
    order = jnp.sum(jnp.where(placed, ids[None, None, :], 0), axis=2)
    sorted_pos = jnp.sum(jnp.where(placed, key_pos[:, None, :], 0), axis=2)
    slots = jnp.arange(SHARE, dtype=jnp.int32)
    source = ((side * members + member) * SHARE + (share + SHARE - slots) % SHARE) * 2
    places = jnp.arange(span_pos.shape[0], dtype=jnp.int32)
    query_pos = [
        jnp.sum(jnp.where(places[None, :] == source[:, None] + h, span_pos[None, :], 0), axis=1)
        for h in range(2)
    ]
    blocks = [
        (jnp.sum((key_pos[:, None, :] <= qp[None, :, None]).astype(jnp.int32), axis=2) + SUBS - 1)
        // SUBS
        for qp in query_pos
    ]
    first, other = blocks[0][:, :, None], blocks[1][:, :, None]
    at = jnp.arange(steps // SHARE, dtype=jnp.int32)[None, None, :]
    second = at >= first
    block = jnp.where(second, at - first, at)
    used = jnp.logical_or(jnp.logical_not(second), block < other)
    q_at = jnp.where(second, 1, 0) + 2 * slots[None, :, None]
    pos = jnp.where(second, query_pos[1][None, :, None], query_pos[0][None, :, None])
    table = jnp.stack([q_at, jnp.where(used, block, 0), jnp.where(used, pos, -1)], axis=3)
    return jnp.concatenate([order, sorted_pos, table.reshape(SIDES, -1)], axis=1)


def local(q, k, v, o, g, w_query, key_weight, value_weight, span_pos):
    tokens = q.shape[0]
    cycle = lax.axis_size("ctx")
    tp_size = lax.axis_size("tp")
    members = cycle // SHARE // SIDES
    spans = 2 * members
    half_rows = 2 * spans * SPAN
    steps = SHARE * ((spans + 1 + 2 * (SUBS - 1)) // SUBS)
    index = lax.axis_index("ctx")
    share, member, side = index % SHARE, index // SHARE % members, index // (SHARE * members)

    def device(side_at, member_at, share_at):
        return (side_at % SIDES * members + member_at) * SHARE + share_at % SHARE

    places = [(a, b, c) for a in range(SIDES) for b in range(members) for c in range(SHARE)]
    key_groups = [
        [device(a, b, c) for b in range(members)] for a in range(SIDES) for c in range(SHARE)
    ]

    def exchanged(array):
        return lax.all_to_all(array, "ctx", 0, 0, tiled=True, axis_index_groups=key_groups)

    def shifted(array, by):
        return lax.ppermute(array, "ctx", [(device(a, b, c), device(a, b, c + by)) for a, b, c in places])

    def crossed(array):
        return lax.ppermute(array, "ctx", [(device(a, b, c), device(a + 1, b, c)) for a, b, c in places])

    copies = pl.pallas_call(
        tile_kernel,
        out_shape=shape((half_rows, HEAD), BF16),
        in_specs=[VMEM] * 2,
        out_specs=VMEM,
        name="tile",
    )(k, v)
    q, copies = lax.optimization_barrier((q, copies))
    block, start = pl.pallas_call(
        pack_kernel,
        out_shape=[shape((2 * COLS, 2 * HEAD), BF16), shape((STATS, COLS), F32)],
        in_specs=[VMEM] * 3,
        out_specs=[VMEM] * 2,
        cost_estimate=pl.CostEstimate(flops=1 << 35, bytes_accessed=1 << 20, transcendentals=0),
        name="pack",
    )(q, g, o)
    kv_own = exchanged(copies)
    blocks = [block] + [shifted(block, s) for s in range(1, SHARE)]
    meta = step_tables(span_pos, side, member, share, members, steps)
    meta_own, meta_other = meta[0], meta[1]
    sides = kv_own.reshape(members, 2, tokens, HEAD)
    k_own, v_own = [sides[:, n].reshape(spans * SPAN, HEAD) for n in range(2)]
    k_other = crossed(k_own)

    def stats_of(table, keys, before):
        return pl.pallas_call(
            functools.partial(stats_kernel, spans, steps),
            out_shape=shape((STATS, COLS), F32),
            in_specs=[SMEM] + [HBM] * 5 + [VMEM],
            out_specs=VMEM,
            scratch_shapes=[
                pltpu.VMEM((spans * SPAN, HEAD), BF16),
                pltpu.VMEM((spans * SPAN, HEAD), BF16),
                pltpu.VMEM((QSPANS * COLS, HEAD), BF16),
                pltpu.VMEM((QSPANS * 8, COLS), F32),
                pltpu.VMEM((QSPANS * 8, COLS), F32),
                pltpu.SemaphoreType.DMA((5,)),
            ],
            compiler_params=LARGE,
            cost_estimate=pl.CostEstimate(
                flops=1 << 30, bytes_accessed=1 << 22, transcendentals=1 << 22
            ),
            name="stats",
        )(table, keys, *blocks, before)

    stats_own, v_late = lax.optimization_barrier((stats_of(meta_own, k_own, start), v_own))
    v_other = crossed(v_late)
    stats = stats_of(meta_other, k_other, stats_own)
    all_stats = [stats] + [shifted(stats, s) for s in range(1, SHARE)]

    def grads_of(table, keys, values, last, extra_in, outs, extra_scratch):
        return pl.pallas_call(
            functools.partial(grads_kernel, spans, steps, last),
            out_shape=outs,
            in_specs=[SMEM] + [HBM] * 6 + [VMEM] * 4 + [HBM] * len(extra_in),
            out_specs=[HBM] * len(outs),
            scratch_shapes=[
                pltpu.VMEM((spans * SPAN, HEAD), BF16),
                pltpu.VMEM((spans * SPAN, HEAD), BF16),
                pltpu.VMEM((half_rows, HEAD), outs[0].dtype),
                *extra_scratch,
                pltpu.VMEM((spans * SPAN, HEAD), BF16),
                pltpu.VMEM((spans * SPAN, HEAD), BF16),
                pltpu.VMEM((spans // SUBS * HEAD, BLOCK), BF16),
                pltpu.VMEM((spans * SPAN, HEAD), F32),
                pltpu.VMEM((spans * SPAN, HEAD), F32),
                pltpu.VMEM((QSPANS * COLS, HEAD), BF16),
                pltpu.VMEM((QSPANS * COLS, HEAD), BF16),
                pltpu.VMEM((QSPANS * 8, COLS), F32),
                pltpu.VMEM((QSPANS * 8, COLS), F32),
                pltpu.VMEM((QSPANS * HEAD, COLS), F32),
                pltpu.SemaphoreType.DMA((4 * SHARE + 3,)),
            ],
            compiler_params=LARGE,
            cost_estimate=pl.CostEstimate(
                flops=1 << 31, bytes_accessed=1 << 23, transcendentals=1 << 22
            ),
            name="grads",
        )(table, keys, values, *blocks, *all_stats, *extra_in)

    dkv_other, dq_before = grads_of(
        meta_other,
        k_other,
        v_other,
        False,
        [],
        [shape((half_rows, HEAD), BF16), shape((QSPANS * HEAD, COLS), F32)],
        [],
    )
    dkv_crossed = crossed(dkv_other)
    dkv_own, *dqs = grads_of(
        meta_own,
        k_own,
        v_own,
        True,
        [dq_before],
        [shape((half_rows, HEAD), BF16), shape((tokens, WIDTH), F32)]
        + [shape((tokens, WIDTH), BF16)] * (SHARE - 1),
        [pltpu.VMEM((tokens, WIDTH), F32), pltpu.VMEM((SHARE - 1, tokens, WIDTH), BF16)],
    )
    dkv_parts = exchanged((dkv_own.astype(F32) + dkv_crossed.astype(F32)).astype(BF16))
    dq_parts = [shifted(dqs[s], -s) for s in range(1, SHARE)]
    peers = (lax.axis_index("tp") + jnp.arange(tp_size, dtype=jnp.int32)) % tp_size
    feats = w_query.shape[0] // tp_size
    own, *pieces = pl.pallas_call(
        project_kernel,
        out_shape=[shape((tokens, feats), F32)] + [shape((tokens, feats), BF16)] * (tp_size - 1),
        in_specs=[SMEM] + [HBM] * 7 + [VMEM],
        out_specs=[VMEM] * tp_size,
        scratch_shapes=[
            pltpu.VMEM((tokens, WIDTH), F32),
            pltpu.VMEM((SHARE - 1, tokens, WIDTH), BF16),
            pltpu.VMEM((half_rows, HEAD), BF16),
            pltpu.VMEM(key_weight.shape, BF16),
            pltpu.VMEM(value_weight.shape, BF16),
            pltpu.SemaphoreType.DMA((7,)),
        ],
        compiler_params=SMALL,
        name="project",
    )(peers, dqs[0], *dq_parts, dkv_parts, key_weight, value_weight, w_query)
    for s in range(1, tp_size):
        pairs = [(d, (d + s) % tp_size) for d in range(tp_size)]
        own = own + lax.ppermute(pieces[s - 1], "tp", pairs).astype(F32)
    return own.astype(BF16)


def solution(mesh):
    row, col = P("ctx", "tp"), P(None, "tp")
    in_specs = (row, row, row, row, row, col, col, col, P())
    return jax.shard_map(local, mesh=mesh, in_specs=in_specs, out_specs=row, check_vma=False)
```

time: 114 us -> 111 us (0.974)
  waiting for transfers between devices: 31 us -> 35.2 us
  starting transfers between devices: 39.1 us -> 35.4 us
  local copies, waits for them, and re-layouts: 8.66 us -> 5.31 us
    all_to_all x2, waiting for transfers between devices: 14.7 us -> 18.9 us  [exchanged(): lax.all_to_all(array, 'ctx', 0, 0, tiled=True, axis_index_groups=key_groups)]
    unnamed x46 -> x30, local copies, waits for them, and re-layouts: 7.52 us -> 4.17 us
    ppermute x12 -> x9, starting transfers between devices: 12.7 us -> 9.64 us  [shifted(): lax.ppermute(array, 'ctx', [(device(a, b, c), device(a, b, c + by)) for a...]
    ppermute x12 -> x9, waiting for transfers between devices: 7.87 us -> 9.85 us  [shifted(): lax.ppermute(array, 'ctx', [(device(a, b, c), device(a, b, c + by)) for a...]
    ppermute x2 -> x3, waiting for transfers between devices: 1.94 us -> 0.01 us  [crossed(): lax.ppermute(array, 'ctx', [(device(a, b, c), device(a + 1, b, c)) for a,...]
    pallas_call x2 -> x1, Pallas kernels: 3.14 us -> 1.91 us  [local(): pl.pallas_call(pack_kernel, out_shape=[shape((2 * COLS, 2 * HEAD), BF16),...]
    pallas_call x1, Pallas kernels: 1.5 us -> 2.65 us  [local(): pl.pallas_call(project_kernel, out_shape=[shape((tokens, feats), F32)] +...]
    ppermute x2 -> x3, starting transfers between devices: 5.78 us -> 6.15 us  [crossed(): lax.ppermute(array, 'ctx', [(device(a, b, c), device(a + 1, b, c)) for a,...]
  transfers between devices with their start and end apart: 19 -> 17, of which waited for: 12 -> 10; matrix products, arithmetic and copies ran while one was open for 2% -> 2% of each run, Pallas kernels for 19% -> 15%
where the time goes in v3:
time: 111 us; the launch traced here: 110 us
  starting transfers between devices  35.4 us (32%)
  waiting for transfers between devices  35.2 us (32%)
  Pallas kernels  30.3 us (27%)
  local copies, waits for them, and re-layouts  5.31 us (5%)
  other arithmetic  3.83 us (3%)
    all_to_all x2, waiting for transfers between devices, exchanged(): lax.all_to_all(array, 'ctx', 0, 0, tiled=True, axis_index_groups=key_groups)  18.9 us
    pallas_call x2, Pallas kernels, grads_of(): pl.pallas_call(functools.partial(grads_kernel, spans, steps, last), out_s...  15 us
    all_to_all x2, starting transfers between devices, exchanged(): lax.all_to_all(array, 'ctx', 0, 0, tiled=True, axis_index_groups=key_groups)  11.7 us
    ppermute x9, waiting for transfers between devices, shifted(): lax.ppermute(array, 'ctx', [(device(a, b, c), device(a, b, c + by)) for a...  9.85 us
    ppermute x9, starting transfers between devices, shifted(): lax.ppermute(array, 'ctx', [(device(a, b, c), device(a, b, c + by)) for a...  9.64 us
    pallas_call x2, Pallas kernels, stats_of(): pl.pallas_call(functools.partial(stats_kernel, spans, steps), out_shape=s...  9.09 us
    ppermute x3, starting transfers between devices, local(): own = own + lax.ppermute(pieces[s - 1], 'tp', pairs).astype(F32)  7.95 us
    ppermute x3, waiting for transfers between devices, local(): own = own + lax.ppermute(pieces[s - 1], 'tp', pairs).astype(F32)  6.46 us
  transfers between devices with their start and end apart: 17, of which 10 were waited for; matrix products, arithmetic and copies ran while one was open for 2% of the time, Pallas kernels for 15%

profile of v3, /device:TPU:1, one launch (start us, length us, event | category | flops | bytes accessed | tf_op | source)
XLA Modules:
  0.0 110.3 jit_solution(4686211235488048215)
XLA Ops:
  0.0 1.6 %tile.1 = bf16[2048,128]{1,0:T(8,128)(2,1)} custom-call(bf16[128,128]{1,0:T(8,128)(2,1)} %k_ref.1, bf16[128,128]{1,0:T(8,128)(2,1)} %v_ref.1), custom_call_target="tpu_custom_call" | custom-call | tf_op jit(solution)/shard_map/tile/pallas_call | solution.py:373
  1.7 1.9 %pack.1 = (bf16[512,256]{1,0:T(8,128)(2,1)}, f32[24,256]{1,0:T(8,128)}) custom-call(bf16[128,512]{1,0:T(8,128)(2,1)} %q_ref, bf16[128,512]{1,0:T(8,128)(2,1)} %g_ref.1, bf16[128,512]{1,0:T(8,128)(2,1)} %o_ref.1), custom_call_target="tpu_custom_call" | custom-call | flops 34359738368 | bytes 1048576 | tf_op jit(solution)/shard_map/pack/pallas_call | solution.py:381
  3.6 3.3 %collective-permute-start.2 = (bf16[512,256]{1,0:T(8,128)(2,1)}, bf16[512,256]{1,0:T(8,128)(2,1)S(1)}, u32[]{:S(2)}, u32[]{:S(2)}) collective-permute-start(bf16[512,256]{1,0:T(8,128)(2,1)} %get-tuple-element.24.b0.refs_3_), channel_id=1, source_target_pairs={{0,12},{4,0},{8,4},{12,8},{16,28},{20,16},{24,20},{28,24},{32,44},... | collective-permute-start | bytes 786440 | tf_op jit(solution)/shard_map/ppermute | solution.py:368
  8.0 8.2 %all-to-all-start = ((bf16[8,256,128]{2,1,0:T(8,128)(2,1)}), bf16[8,256,128]{2,1,0:T(8,128)(2,1)S(1)}, u32[]{:S(2)}, u32[]{:S(2)}) async-start(bf16[8,256,128]{2,1,0:T(8,128)(2,1)} %bitcast.1), calls=%async_computation | async-start | bytes 1048576 | tf_op jit(solution)/shard_map/all_to_all | solution.py:365
  17.7 14.4 %all-to-all-done = bf16[8,256,128]{2,1,0:T(8,128)(2,1)S(1)} async-done(((bf16[8,256,128]{2,1,0:T(8,128)(2,1)}), bf16[8,256,128]{2,1,0:T(8,128)(2,1)S(1)}, u32[]{:S(2)}, u32[]{:S(2)}) %all-to-all-start) | async-done | bytes 524320 | tf_op jit(solution)/shard_map/all_to_all | solution.py:365
  32.2 3.0 %collective-permute-start.3 = (bf16[1024,128]{1,0:T(8,128)(2,1)S(1)}, bf16[1024,128]{1,0:T(8,128)(2,1)S(1)}, u32[]{:S(2)}, u32[]{:S(2)}) collective-permute-start(bf16[1024,128]{1,0:T(8,128)(2,1)S(1)} %bitcast.15), channel_id=1, source_target_pairs={{0,128},{4,132},{8,136},{12,140},{16,144},{20,148},{24,152},{28,15... | collective-permute-start | bytes 786440 | tf_op jit(solution)/shard_map/ppermute | solution.py:371
  35.8 0.7 copy-done.7
  36.6 4.5 %stats.2.before = f32[24,256]{1,0:T(8,128)} custom-call(s32[92]{0:T(128)} %get-tuple-element.52.meta.refs_0_, bf16[1024,128]{1,0:T(8,128)(2,1)} %bitcast.16, bf16[512,256]{1,0:T(8,128)(2,1)} %get-tuple-element.24.b0.refs_3_, bf16[512,256]{1,0:T(8,128)(2,1)} %copy-done.9, bf16[512,256]{1,0:T(8,128)(2,1)} %copy-done.8, bf16[512,256]{1,0:T(8,128)(2,1)} %copy-done.7, ...), custom_call_target="tpu_custom_call" | custom-call | flops 1073741824 | bytes 4194304 | tf_op jit(solution)/shard_map/stats/pallas_call | solution.py:398
  41.4 0.7 copy-done.10
  42.1 4.5 %stats.3.refs_7_ = f32[24,256]{1,0:T(8,128)} custom-call(s32[92]{0:T(128)} %get-tuple-element.51.meta.refs_0_, bf16[1024,128]{1,0:T(8,128)(2,1)} %copy-done.10, bf16[512,256]{1,0:T(8,128)(2,1)} %get-tuple-element.24.b0.refs_3_, bf16[512,256]{1,0:T(8,128)(2,1)} %copy-done.9, bf16[512,256]{1,0:T(8,128)(2,1)} %copy-done.8, bf16[512,256]{1,0:T(8,128)(2,1)} %copy-done.7, ...), custom_call_target="tpu_custom_call" | custom-call | flops 1073741824 | bytes 4194304 | tf_op jit(solution)/shard_map/stats/pallas_call | solution.py:398
  46.7 2.1 %collective-permute-start.6 = (f32[24,256]{1,0:T(8,128)}, f32[24,256]{1,0:T(8,128)S(1)}, u32[]{:S(2)}, u32[]{:S(2)}) collective-permute-start(f32[24,256]{1,0:T(8,128)} %stats.3.refs_7_), channel_id=1, source_target_pairs={{0,12},{4,0},{8,4},{12,8},{16,28},{20,16},{24,20},{28,24},{32,44},... | collective-permute-start | bytes 73736 | tf_op jit(solution)/shard_map/ppermute | solution.py:368
  48.8 1.2 %collective-permute-start.5 = (f32[24,256]{1,0:T(8,128)}, f32[24,256]{1,0:T(8,128)S(1)}, u32[]{:S(2)}, u32[]{:S(2)}) collective-permute-start(f32[24,256]{1,0:T(8,128)} %stats.3.refs_7_), channel_id=1, source_target_pairs={{0,8},{4,12},{8,0},{12,4},{16,24},{20,28},{24,16},{28,20},{32,40},... | collective-permute-start | bytes 73736 | tf_op jit(solution)/shard_map/ppermute | solution.py:368
  50.1 3.1 %collective-permute-done.5.refs_9_ = f32[24,256]{1,0:T(8,128)S(1)} collective-permute-done((f32[24,256]{1,0:T(8,128)}, f32[24,256]{1,0:T(8,128)S(1)}, u32[]{:S(2)}, u32[]{:S(2)}) %collective-permute-start.5) | collective-permute-done | bytes 24608 | tf_op jit(solution)/shard_map/ppermute | solution.py:368
  53.2 0.9 collective-permute-done.4.refs_8_
  54.8 7.1 %grads.2 = (bf16[2048,128]{1,0:T(8,128)(2,1)}, f32[1024,256]{1,0:T(8,128)}) custom-call(s32[92]{0:T(128)} %get-tuple-element.51.meta.refs_0_, bf16[1024,128]{1,0:T(8,128)(2,1)} %copy-done.10, bf16[1024,128]{1,0:T(8,128)(2,1)} %copy-done.11, bf16[512,256]{1,0:T(8,128)(2,1)} %get-tuple-element.24.b0.refs_3_, bf16[512,256]{1,0:T(8,128)(2,1)} %copy-done.9, ...), custom_call_target="tpu_custom_call" | custom-call | flops 2147483648 | bytes 8388608 | tf_op jit(solution)/shard_map/grads/pallas_call | solution.py:424
  61.9 2.9 %collective-permute-start.11 = (bf16[2048,128]{1,0:T(8,128)(2,1)}, bf16[2048,128]{1,0:T(8,128)(2,1)S(1)}, u32[]{:S(2)}, u32[]{:S(2)}) collective-permute-start(bf16[2048,128]{1,0:T(8,128)(2,1)} %get-tuple-element.34), channel_id=1, source_target_pairs={{0,128},{4,132},{8,136},{12,140},{16,144},{20,148},{24,152},{28,15... | collective-permute-start | bytes 1572872 | tf_op jit(solution)/shard_map/ppermute | solution.py:371
  64.8 7.9 %grads.3 = (bf16[2048,128]{1,0:T(8,128)(2,1)}, f32[128,512]{1,0:T(8,128)}, bf16[128,512]{1,0:T(8,128)(2,1)}, bf16[128,512]{1,0:T(8,128)(2,1)}, bf16[128,512]{1,0:T(8,128)(2,1)}) custom-call(s32[92]{0:T(128)} %get-tuple-element.52.meta.refs_0_, bf16[1024,128]{1,0:T(8,128)(2,1)} %bitcast.17, bf16[1024,128]{1,0:T(8,128)(2,1)} %bitcast.14, ...), custom_call_target="tpu_custom_call" | custom-call | flops 2147483648 | bytes 8388608 | tf_op jit(solution)/shard_map/grads/pallas_call | solution.py:424
  72.8 2.1 %add_convert_fusion = bf16[2048,128]{1,0:T(8,128)(2,1)} fusion(bf16[2048,128]{1,0:T(8,128)(2,1)S(1)} %collective-permute-done.11, bf16[2048,128]{1,0:T(8,128)(2,1)} %get-tuple-element.33), kind=kLoop, calls=%fused_computation | loop fusion | flops 1048576 | bytes 1572864 | tf_op jit(solution)/shard_map/convert_element_type | solution.py:473
  74.9 3.5 %all-to-all-start.1 = ((bf16[8,256,128]{2,1,0:T(8,128)(2,1)}), bf16[8,256,128]{2,1,0:T(8,128)(2,1)S(1)}, u32[]{:S(2)}, u32[]{:S(2)}) async-start(bf16[8,256,128]{2,1,0:T(8,128)(2,1)} %bitcast.11), calls=%async_computation.1 | async-start | bytes 1048576 | tf_op jit(solution)/shard_map/all_to_all | solution.py:365
  78.4 0.7 collective-permute-start.8
  79.1 1.0 collective-permute-start.9
  80.2 2.3 %collective-permute-done.8.d1 = bf16[128,512]{1,0:T(8,128)(2,1)S(1)} collective-permute-done((bf16[128,512]{1,0:T(8,128)(2,1)}, bf16[128,512]{1,0:T(8,128)(2,1)S(1)}, u32[]{:S(2)}, u32[]{:S(2)}) %collective-permute-start.8) | collective-permute-done | bytes 131104 | tf_op jit(solution)/shard_map/ppermute | solution.py:368
  82.5 2.2 %collective-permute-done.9.d2 = bf16[128,512]{1,0:T(8,128)(2,1)S(1)} collective-permute-done((bf16[128,512]{1,0:T(8,128)(2,1)}, bf16[128,512]{1,0:T(8,128)(2,1)S(1)}, u32[]{:S(2)}, u32[]{:S(2)}) %collective-permute-start.9) | collective-permute-done | bytes 131104 | tf_op jit(solution)/shard_map/ppermute | solution.py:368
  84.7 1.3 %collective-permute-done.10.d3 = bf16[128,512]{1,0:T(8,128)(2,1)S(1)} collective-permute-done((bf16[128,512]{1,0:T(8,128)(2,1)}, bf16[128,512]{1,0:T(8,128)(2,1)S(1)}, u32[]{:S(2)}, u32[]{:S(2)}) %collective-permute-start.10) | collective-permute-done | bytes 131104 | tf_op jit(solution)/shard_map/ppermute | solution.py:368
  86.0 4.5 %all-to-all-done.1 = bf16[8,256,128]{2,1,0:T(8,128)(2,1)S(1)} async-done(((bf16[8,256,128]{2,1,0:T(8,128)(2,1)}), bf16[8,256,128]{2,1,0:T(8,128)(2,1)S(1)}, u32[]{:S(2)}, u32[]{:S(2)}) %all-to-all-start.1) | async-done | bytes 524320 | tf_op jit(solution)/shard_map/all_to_all | solution.py:365
  90.5 1.0 copy-done.2
  91.5 0.9 copy-done.3
  92.5 2.6 %project.1 = (f32[128,512]{1,0:T(8,128)S(1)}, bf16[128,512]{1,0:T(8,128)(2,1)S(1)}, bf16[128,512]{1,0:T(8,128)(2,1)S(1)}, bf16[128,512]{1,0:T(8,128)(2,1)S(1)}) custom-call(s32[4]{0:T(128)S(1)} %and_select_fusion.3.peers, f32[128,512]{1,0:T(8,128)S(1)} %copy-done.3, bf16[128,512]{1,0:T(8,128)(2,1)S(1)} %collective-permute-done.8.d1, ...), custom_call_target="tpu_custom_call" | custom-call | tf_op jit(solution)/shard_map/project/pallas_call | solution.py:477
  95.1 7.5 %collective-permute-start.12 = (bf16[128,512]{1,0:T(8,128)(2,1)S(1)}, bf16[128,512]{1,0:T(8,128)(2,1)S(1)}, u32[]{:S(2)}, u32[]{:S(2)}) collective-permute-start(bf16[128,512]{1,0:T(8,128)(2,1)S(1)} %get-tuple-element.36), channel_id=1, source_target_pairs={{0,1},{1,2},{2,3},{3,0},{4,5},{5,6},{6,7},{7,4},{8,9},{9,10},{10,1... | collective-permute-start | bytes 393224 | tf_op jit(solution)/shard_map/ppermute | solution.py:495
  103.1 2.2 %collective-permute-done.12 = bf16[128,512]{1,0:T(8,128)(2,1)S(1)} collective-permute-done((bf16[128,512]{1,0:T(8,128)(2,1)S(1)}, bf16[128,512]{1,0:T(8,128)(2,1)S(1)}, u32[]{:S(2)}, u32[]{:S(2)}) %collective-permute-start.12) | collective-permute-done | bytes 131104 | tf_op jit(solution)/shard_map/ppermute | solution.py:495
  105.3 3.6 %collective-permute-done.13 = bf16[128,512]{1,0:T(8,128)(2,1)S(1)} collective-permute-done((bf16[128,512]{1,0:T(8,128)(2,1)S(1)}, bf16[128,512]{1,0:T(8,128)(2,1)S(1)}, u32[]{:S(2)}, u32[]{:S(2)}) %collective-permute-start.13) | collective-permute-done | bytes 131104 | tf_op jit(solution)/shard_map/ppermute | solution.py:495
  109.5 0.7 add_convert_fusion.1
  (61 shorter events, 5.6 us)
Async XLA Ops:
  1.7 14.6 %copy-start.6 = (s32[128]{0:T(128)S(1)}, s32[128]{0:T(128)}, u32[]{:S(2)}) copy-start(s32[128]{0:T(128)} %param.17) | copy-start | bytes 1540
  3.6 32.2 %collective-permute-start.2 = (bf16[512,256]{1,0:T(8,128)(2,1)}, bf16[512,256]{1,0:T(8,128)(2,1)S(1)}, u32[]{:S(2)}, u32[]{:S(2)}) collective-permute-start(bf16[512,256]{1,0:T(8,128)(2,1)} %get-tuple-element.24.b0.refs_3_), channel_id=1, source_target_pairs={{0,12},{4,0},{8,4},{12,8},{16,28},{20,16},{24,20},{28,24},{32,44},... | collective-permute-start | bytes 786440 | tf_op jit(solution)/shard_map/ppermute | solution.py:368
  6.9 28.9 %collective-permute-start.1 = (bf16[512,256]{1,0:T(8,128)(2,1)}, bf16[512,256]{1,0:T(8,128)(2,1)S(1)}, u32[]{:S(2)}, u32[]{:S(2)}) collective-permute-start(bf16[512,256]{1,0:T(8,128)(2,1)} %get-tuple-element.24.b0.refs_3_), channel_id=1, source_target_pairs={{0,8},{4,12},{8,0},{12,4},{16,24},{20,28},{24,16},{28,20},{32,40},... | collective-permute-start | bytes 786440 | tf_op jit(solution)/shard_map/ppermute | solution.py:368
  7.4 28.4 %collective-permute-start = (bf16[512,256]{1,0:T(8,128)(2,1)}, bf16[512,256]{1,0:T(8,128)(2,1)S(1)}, u32[]{:S(2)}, u32[]{:S(2)}) collective-permute-start(bf16[512,256]{1,0:T(8,128)(2,1)} %get-tuple-element.24.b0.refs_3_), channel_id=1, source_target_pairs={{0,4},{4,8},{8,12},{12,0},{16,20},{20,24},{24,28},{28,16},{32,36},... | collective-permute-start | bytes 786440 | tf_op jit(solution)/shard_map/ppermute | solution.py:368
  8.0 24.1 %all-to-all-start = ((bf16[8,256,128]{2,1,0:T(8,128)(2,1)}), bf16[8,256,128]{2,1,0:T(8,128)(2,1)S(1)}, u32[]{:S(2)}, u32[]{:S(2)}) async-start(bf16[8,256,128]{2,1,0:T(8,128)(2,1)} %bitcast.1), calls=%async_computation | async-start | bytes 1048576 | tf_op jit(solution)/shard_map/all_to_all | solution.py:365
  32.2 3.6 %copy-start.5 = (bf16[8,1,128,128]{3,2,1,0:T(8,128)(2,1)}, bf16[8,1,128,128]{3,2,1,0:T(8,128)(2,1)S(1)}, u32[]{:S(2)}) copy-start(bf16[8,1,128,128]{3,2,1,0:T(8,128)(2,1)S(1)} %get-tuple-element.48) | copy-start | bytes 786436
  32.2 9.0 %copy-start.4 = (bf16[8,1,128,128]{3,2,1,0:T(8,128)(2,1)}, bf16[8,1,128,128]{3,2,1,0:T(8,128)(2,1)S(1)}, u32[]{:S(2)}) copy-start(bf16[8,1,128,128]{3,2,1,0:T(8,128)(2,1)S(1)} %get-tuple-element.47) | copy-start | bytes 786436
  32.2 9.2 %collective-permute-start.3 = (bf16[1024,128]{1,0:T(8,128)(2,1)S(1)}, bf16[1024,128]{1,0:T(8,128)(2,1)S(1)}, u32[]{:S(2)}, u32[]{:S(2)}) collective-permute-start(bf16[1024,128]{1,0:T(8,128)(2,1)S(1)} %bitcast.15), channel_id=1, source_target_pairs={{0,128},{4,132},{8,136},{12,140},{16,144},{20,148},{24,152},{28,15... | collective-permute-start | bytes 786440 | tf_op jit(solution)/shard_map/ppermute | solution.py:371
  35.8 0.7 copy-start.7
  35.8 0.8 copy-start.8
  35.8 0.8 copy-start.9
  41.2 8.9 %collective-permute-start.7 = (bf16[1024,128]{1,0:T(8,128)(2,1)S(1)}, bf16[1024,128]{1,0:T(8,128)(2,1)S(1)}, u32[]{:S(2)}, u32[]{:S(2)}) collective-permute-start(bf16[1024,128]{1,0:T(8,128)(2,1)S(1)} %bitcast.13), channel_id=1, source_target_pairs={{0,128},{4,132},{8,136},{12,140},{16,144},{20,148},{24,152},{28,15... | collective-permute-start | bytes 786440 | tf_op jit(solution)/shard_map/ppermute | solution.py:371
  41.4 0.7 copy-start.10
  46.7 3.4 %collective-permute-start.6 = (f32[24,256]{1,0:T(8,128)}, f32[24,256]{1,0:T(8,128)S(1)}, u32[]{:S(2)}, u32[]{:S(2)}) collective-permute-start(f32[24,256]{1,0:T(8,128)} %stats.3.refs_7_), channel_id=1, source_target_pairs={{0,12},{4,0},{8,4},{12,8},{16,28},{20,16},{24,20},{28,24},{32,44},... | collective-permute-start | bytes 73736 | tf_op jit(solution)/shard_map/ppermute | solution.py:368
  48.8 4.4 %collective-permute-start.5 = (f32[24,256]{1,0:T(8,128)}, f32[24,256]{1,0:T(8,128)S(1)}, u32[]{:S(2)}, u32[]{:S(2)}) collective-permute-start(f32[24,256]{1,0:T(8,128)} %stats.3.refs_7_), channel_id=1, source_target_pairs={{0,8},{4,12},{8,0},{12,4},{16,24},{20,28},{24,16},{28,20},{32,40},... | collective-permute-start | bytes 73736 | tf_op jit(solution)/shard_map/ppermute | solution.py:368
  50.1 4.1 %collective-permute-start.4 = (f32[24,256]{1,0:T(8,128)}, f32[24,256]{1,0:T(8,128)S(1)}, u32[]{:S(2)}, u32[]{:S(2)}) collective-permute-start(f32[24,256]{1,0:T(8,128)} %stats.3.refs_7_), channel_id=1, source_target_pairs={{0,4},{4,8},{8,12},{12,0},{16,20},{20,24},{24,28},{28,16},{32,36},... | collective-permute-start | bytes 73736 | tf_op jit(solution)/shard_map/ppermute | solution.py:368
  50.1 4.1 %copy-start.11 = (bf16[1024,128]{1,0:T(8,128)(2,1)}, bf16[1024,128]{1,0:T(8,128)(2,1)S(1)}, u32[]{:S(2)}) copy-start(bf16[1024,128]{1,0:T(8,128)(2,1)S(1)} %collective-permute-done.7.refs_2_) | copy-start | bytes 786436
  50.1 4.1 %copy-start.12 = (f32[24,256]{1,0:T(8,128)}, f32[24,256]{1,0:T(8,128)S(1)}, u32[]{:S(2)}) copy-start(f32[24,256]{1,0:T(8,128)S(1)} %collective-permute-done.6.refs_10_) | copy-start | bytes 73732
  53.2 0.9 copy-start.13
  54.2 0.6 copy-start.14
  61.9 10.8 %collective-permute-start.11 = (bf16[2048,128]{1,0:T(8,128)(2,1)}, bf16[2048,128]{1,0:T(8,128)(2,1)S(1)}, u32[]{:S(2)}, u32[]{:S(2)}) collective-permute-start(bf16[2048,128]{1,0:T(8,128)(2,1)} %get-tuple-element.34), channel_id=1, source_target_pairs={{0,128},{4,132},{8,136},{12,140},{16,144},{20,148},{24,152},{28,15... | collective-permute-start | bytes 1572872 | tf_op jit(solution)/shard_map/ppermute | solution.py:371
  72.7 17.8 %copy-start = (bf16[2048,512]{1,0:T(8,128)(2,1)S(1)}, bf16[2048,512]{1,0:T(8,128)(2,1)}, u32[]{:S(2)}) copy-start(bf16[2048,512]{1,0:T(8,128)(2,1)} %wq_ref.1) | copy-start | bytes 6291460
  72.7 17.7 %copy-start.1 = (bf16[2048,128]{1,0:T(8,128)(2,1)S(1)}, bf16[2048,128]{1,0:T(8,128)(2,1)}, u32[]{:S(2)}) copy-start(bf16[2048,128]{1,0:T(8,128)(2,1)} %wk_ref.1) | copy-start | bytes 1572868
  74.9 15.6 %all-to-all-start.1 = ((bf16[8,256,128]{2,1,0:T(8,128)(2,1)}), bf16[8,256,128]{2,1,0:T(8,128)(2,1)S(1)}, u32[]{:S(2)}, u32[]{:S(2)}) async-start(bf16[8,256,128]{2,1,0:T(8,128)(2,1)} %bitcast.11), calls=%async_computation.1 | async-start | bytes 1048576 | tf_op jit(solution)/shard_map/all_to_all | solution.py:365
  78.4 4.1 %collective-permute-start.8 = (bf16[128,512]{1,0:T(8,128)(2,1)}, bf16[128,512]{1,0:T(8,128)(2,1)S(1)}, u32[]{:S(2)}, u32[]{:S(2)}) collective-permute-start(bf16[128,512]{1,0:T(8,128)(2,1)} %get-tuple-element.30), channel_id=1, source_target_pairs={{0,12},{4,0},{8,4},{12,8},{16,28},{20,16},{24,20},{28,24},{32,44},... | collective-permute-start | bytes 393224 | tf_op jit(solution)/shard_map/ppermute | solution.py:368
  79.1 5.6 %collective-permute-start.9 = (bf16[128,512]{1,0:T(8,128)(2,1)}, bf16[128,512]{1,0:T(8,128)(2,1)S(1)}, u32[]{:S(2)}, u32[]{:S(2)}) collective-permute-start(bf16[128,512]{1,0:T(8,128)(2,1)} %get-tuple-element.31), channel_id=1, source_target_pairs={{0,8},{4,12},{8,0},{12,4},{16,24},{20,28},{24,16},{28,20},{32,40},... | collective-permute-start | bytes 393224 | tf_op jit(solution)/shard_map/ppermute | solution.py:368
  80.1 6.0 %collective-permute-start.10 = (bf16[128,512]{1,0:T(8,128)(2,1)}, bf16[128,512]{1,0:T(8,128)(2,1)S(1)}, u32[]{:S(2)}, u32[]{:S(2)}) collective-permute-start(bf16[128,512]{1,0:T(8,128)(2,1)} %get-tuple-element.32), channel_id=1, source_target_pairs={{0,4},{4,8},{8,12},{12,0},{16,20},{20,24},{24,28},{28,16},{32,36},... | collective-permute-start | bytes 393224 | tf_op jit(solution)/shard_map/ppermute | solution.py:368
  90.5 1.0 copy-start.2
  91.5 0.9 copy-start.3
  95.1 10.1 %collective-permute-start.12 = (bf16[128,512]{1,0:T(8,128)(2,1)S(1)}, bf16[128,512]{1,0:T(8,128)(2,1)S(1)}, u32[]{:S(2)}, u32[]{:S(2)}) collective-permute-start(bf16[128,512]{1,0:T(8,128)(2,1)S(1)} %get-tuple-element.36), channel_id=1, source_target_pairs={{0,1},{1,2},{2,3},{3,0},{4,5},{5,6},{6,7},{7,4},{8,9},{9,10},{10,1... | collective-permute-start | bytes 393224 | tf_op jit(solution)/shard_map/ppermute | solution.py:495
  102.6 6.3 %collective-permute-start.13 = (bf16[128,512]{1,0:T(8,128)(2,1)S(1)}, bf16[128,512]{1,0:T(8,128)(2,1)S(1)}, u32[]{:S(2)}, u32[]{:S(2)}) collective-permute-start(bf16[128,512]{1,0:T(8,128)(2,1)S(1)} %get-tuple-element.37), channel_id=1, source_target_pairs={{0,2},{1,3},{2,0},{3,1},{4,6},{5,7},{6,4},{7,5},{8,10},{9,11},{10,... | collective-permute-start | bytes 393224 | tf_op jit(solution)/shard_map/ppermute | solution.py:495
  103.0 6.6 %collective-permute-start.14 = (bf16[128,512]{1,0:T(8,128)(2,1)S(1)}, bf16[128,512]{1,0:T(8,128)(2,1)S(1)}, u32[]{:S(2)}, u32[]{:S(2)}) collective-permute-start(bf16[128,512]{1,0:T(8,128)(2,1)S(1)} %get-tuple-element.38), channel_id=1, source_target_pairs={{0,3},{1,0},{2,1},{3,2},{4,7},{5,4},{6,5},{7,6},{8,11},{9,8},{10,9... | collective-permute-start | bytes 393224 | tf_op jit(solution)/shard_map/ppermute | solution.py:495

commit v4 on v3

--- a/solution.py
+++ b/solution.py
@@ -63,14 +63,11 @@
     return slice(index * size, (index + 1) * size)
 
 
-def tile_kernel(k_ref, v_ref, out_ref):
+def pack_kernel(k_ref, v_ref, q_ref, g_ref, o_ref, copies_ref, out_ref, start_ref):
     tokens = k_ref.shape[0]
-    for member in range(out_ref.shape[0] // (2 * tokens)):
-        out_ref[part_slice(2 * member, tokens), :] = k_ref[...]
-        out_ref[part_slice(2 * member + 1, tokens), :] = v_ref[...]
-
-
-def pack_kernel(q_ref, g_ref, o_ref, out_ref, start_ref):
+    for member in range(copies_ref.shape[0] // (2 * tokens)):
+        copies_ref[part_slice(2 * member, tokens), :] = k_ref[...]
+        copies_ref[part_slice(2 * member + 1, tokens), :] = v_ref[...]
     start_ref[:QSPANS, :] = jnp.full((QSPANS, COLS), NEG, F32)
     start_ref[QSPANS:, :] = jnp.zeros((STATS - QSPANS, COLS), F32)
     ones = jnp.ones((8, HEAD), BF16)
@@ -256,8 +253,9 @@
 
     def place_span(n, carry):
         rows = rows_at(n, SPAN)
-        dkv[span_rows(meta[n], 0), :] = (dka[rows, :] * SCALE).astype(dkv.dtype)
-        dkv[span_rows(meta[n], 1), :] = dva[rows, :].astype(dkv.dtype)
+        dest = spans - 2 - meta[n] + 2 * (meta[n] % 2)
+        dkv[span_rows(dest, 0), :] = (dka[rows, :] * SCALE).astype(dkv.dtype)
+        dkv[span_rows(dest, 1), :] = dva[rows, :].astype(dkv.dtype)
         return carry
 
     lax.fori_loop(0, spans, place_span, 0, unroll=8)
@@ -361,8 +359,8 @@
         [device(a, b, c) for b in range(members)] for a in range(SIDES) for c in range(SHARE)
     ]
 
-    def exchanged(array):
-        return lax.all_to_all(array, "ctx", 0, 0, tiled=True, axis_index_groups=key_groups)
+    def exchanged(array, groups):
+        return lax.all_to_all(array, "ctx", 0, 0, tiled=True, axis_index_groups=groups)
 
     def shifted(array, by):
         return lax.ppermute(array, "ctx", [(device(a, b, c), device(a, b, c + by)) for a, b, c in places])
@@ -370,23 +368,18 @@
     def crossed(array):
         return lax.ppermute(array, "ctx", [(device(a, b, c), device(a + 1, b, c)) for a, b, c in places])
 
-    copies = pl.pallas_call(
-        tile_kernel,
-        out_shape=shape((half_rows, HEAD), BF16),
-        in_specs=[VMEM] * 2,
-        out_specs=VMEM,
-        name="tile",
-    )(k, v)
-    q, copies = lax.optimization_barrier((q, copies))
-    block, start = pl.pallas_call(
+    copies, block, start = pl.pallas_call(
         pack_kernel,
-        out_shape=[shape((2 * COLS, 2 * HEAD), BF16), shape((STATS, COLS), F32)],
-        in_specs=[VMEM] * 3,
-        out_specs=[VMEM] * 2,
-        cost_estimate=pl.CostEstimate(flops=1 << 35, bytes_accessed=1 << 20, transcendentals=0),
+        out_shape=[
+            shape((half_rows, HEAD), BF16),
+            shape((2 * COLS, 2 * HEAD), BF16),
+            shape((STATS, COLS), F32),
+        ],
+        in_specs=[VMEM] * 5,
+        out_specs=[VMEM] * 3,
         name="pack",
-    )(q, g, o)
-    kv_own = exchanged(copies)
+    )(k, v, q, g, o)
+    kv_own = exchanged(copies, key_groups)
     blocks = [block] + [shifted(block, s) for s in range(1, SHARE)]
     meta = step_tables(span_pos, side, member, share, members, steps)
     meta_own, meta_other = meta[0], meta[1]
@@ -470,7 +463,8 @@
         + [shape((tokens, WIDTH), BF16)] * (SHARE - 1),
         [pltpu.VMEM((tokens, WIDTH), F32), pltpu.VMEM((SHARE - 1, tokens, WIDTH), BF16)],
     )
-    dkv_parts = exchanged((dkv_own.astype(F32) + dkv_crossed.astype(F32)).astype(BF16))
+    turned_groups = [group[::-1] for group in key_groups]
+    dkv_parts = exchanged((dkv_own.astype(F32) + dkv_crossed.astype(F32)).astype(BF16), turned_groups)
     dq_parts = [shifted(dqs[s], -s) for s in range(1, SHARE)]
     peers = (lax.axis_index("tp") + jnp.arange(tp_size, dtype=jnp.int32)) % tp_size
     feats = w_query.shape[0] // tp_size

time: 111 us -> 107 us (0.964)
  waiting for transfers between devices: 35.2 us -> 29.7 us
  starting transfers between devices: 35.4 us -> 37.4 us
  Pallas kernels: 30.3 us -> 28.8 us
    all_to_all x2, waiting for transfers between devices: 18.9 us -> 13.1 us  [exchanged(): lax.all_to_all(array, 'ctx', 0, 0, tiled=True, axis_index_groups=groups)]
    ppermute x3, starting transfers between devices: 7.95 us -> 9.59 us  [local(): own = own + lax.ppermute(pieces[s - 1], 'tp', pairs).astype(F32)]
    pallas_call x2 -> x1, Pallas kernels: 3.56 us -> 2.1 us  [local(): pl.pallas_call(pack_kernel, out_shape=[shape((half_rows, HEAD), BF16), sh...]
    unnamed x30 -> x28, local copies, waits for them, and re-layouts: 4.17 us -> 4.12 us
  transfers between devices with their start and end apart: 17 -> 17, of which waited for: 10 -> 9; matrix products, arithmetic and copies ran while one was open for 2% -> 3% of each run, Pallas kernels for 15% -> 16%
where the time goes in v4:
time: 107 us
  starting transfers between devices  37.4 us (35%)
  waiting for transfers between devices  29.7 us (28%)
  Pallas kernels  28.8 us (27%)
  local copies, waits for them, and re-layouts  5.94 us (6%)
  other arithmetic  4.48 us (4%)
    pallas_call x2, Pallas kernels, grads_of(): pl.pallas_call(functools.partial(grads_kernel, spans, steps, last), out_s...  14.9 us
    all_to_all x2, waiting for transfers between devices, exchanged(): lax.all_to_all(array, 'ctx', 0, 0, tiled=True, axis_index_groups=groups)  13.1 us
    all_to_all x2, starting transfers between devices, exchanged(): lax.all_to_all(array, 'ctx', 0, 0, tiled=True, axis_index_groups=groups)  12.1 us
    ppermute x9, waiting for transfers between devices, shifted(): lax.ppermute(array, 'ctx', [(device(a, b, c), device(a, b, c + by)) for a...  10.1 us
    ppermute x3, starting transfers between devices, local(): own = own + lax.ppermute(pieces[s - 1], 'tp', pairs).astype(F32)  9.59 us
    ppermute x9, starting transfers between devices, shifted(): lax.ppermute(array, 'ctx', [(device(a, b, c), device(a, b, c + by)) for a...  9.57 us
    pallas_call x2, Pallas kernels, stats_of(): pl.pallas_call(functools.partial(stats_kernel, spans, steps), out_shape=s...  9.09 us
    ppermute x3, waiting for transfers between devices, local(): own = own + lax.ppermute(pieces[s - 1], 'tp', pairs).astype(F32)  6.56 us
  transfers between devices with their start and end apart: 17, of which 9 were waited for; matrix products, arithmetic and copies ran while one was open for 3% of the time, Pallas kernels for 16%

profile of v4, /device:TPU:1, one launch (start us, length us, event | category | flops | bytes accessed | tf_op | source)
XLA Modules:
  0.0 106.6 jit_solution(17434182750560352298)
XLA Ops:
  0.0 2.1 %pack.1 = (bf16[2048,128]{1,0:T(8,128)(2,1)}, bf16[512,256]{1,0:T(8,128)(2,1)}, f32[24,256]{1,0:T(8,128)}) custom-call(bf16[128,128]{1,0:T(8,128)(2,1)} %k_ref.1, bf16[128,128]{1,0:T(8,128)(2,1)} %v_ref.1, bf16[128,512]{1,0:T(8,128)(2,1)} %q_ref.1, bf16[128,512]{1,0:T(8,128)(2,1)} %g_ref.1, bf16[128,512]{1,0:T(8,128)(2,1)} %o_ref.1), custom_call_target="tpu_custom_call" | custom-call | tf_op jit(solution)/shard_map/pack/pallas_call | solution.py:371
  2.1 3.3 %collective-permute-start.2 = (bf16[512,256]{1,0:T(8,128)(2,1)}, bf16[512,256]{1,0:T(8,128)(2,1)S(1)}, u32[]{:S(2)}, u32[]{:S(2)}) collective-permute-start(bf16[512,256]{1,0:T(8,128)(2,1)} %get-tuple-element.22.b0.refs_3_), channel_id=1, source_target_pairs={{0,12},{4,0},{8,4},{12,8},{16,28},{20,16},{24,20},{28,24},{32,44},... | collective-permute-start | bytes 786440 | tf_op jit(solution)/shard_map/ppermute | solution.py:366
  6.5 8.2 %all-to-all-start = ((bf16[8,256,128]{2,1,0:T(8,128)(2,1)}), bf16[8,256,128]{2,1,0:T(8,128)(2,1)S(1)}, u32[]{:S(2)}, u32[]{:S(2)}) async-start(bf16[8,256,128]{2,1,0:T(8,128)(2,1)} %bitcast.13), calls=%async_computation | async-start | bytes 1048576 | tf_op jit(solution)/shard_map/all_to_all | solution.py:363
  14.7 0.8 reshape.127
  15.7 0.9 select_reduce_fusion.2
  17.6 13.1 %all-to-all-done = bf16[8,256,128]{2,1,0:T(8,128)(2,1)S(1)} async-done(((bf16[8,256,128]{2,1,0:T(8,128)(2,1)}), bf16[8,256,128]{2,1,0:T(8,128)(2,1)S(1)}, u32[]{:S(2)}, u32[]{:S(2)}) %all-to-all-start) | async-done | bytes 524320 | tf_op jit(solution)/shard_map/all_to_all | solution.py:363
  30.7 3.0 %collective-permute-start.3 = (bf16[1024,128]{1,0:T(8,128)(2,1)S(1)}, bf16[1024,128]{1,0:T(8,128)(2,1)S(1)}, u32[]{:S(2)}, u32[]{:S(2)}) collective-permute-start(bf16[1024,128]{1,0:T(8,128)(2,1)S(1)} %bitcast.16), channel_id=1, source_target_pairs={{0,128},{4,132},{8,136},{12,140},{16,144},{20,148},{24,152},{28,15... | collective-permute-start | bytes 786440 | tf_op jit(solution)/shard_map/ppermute | solution.py:369
  34.4 0.6 copy-done.6
  35.2 4.5 %stats.2.before = f32[24,256]{1,0:T(8,128)} custom-call(s32[92]{0:T(128)} %get-tuple-element.50.meta.refs_0_, bf16[1024,128]{1,0:T(8,128)(2,1)} %bitcast.17, bf16[512,256]{1,0:T(8,128)(2,1)} %get-tuple-element.22.b0.refs_3_, bf16[512,256]{1,0:T(8,128)(2,1)} %copy-done.8, bf16[512,256]{1,0:T(8,128)(2,1)} %copy-done.7, bf16[512,256]{1,0:T(8,128)(2,1)} %copy-done.6, ...), custom_call_target="tpu_custom_call" | custom-call | flops 1073741824 | bytes 4194304 | tf_op jit(solution)/shard_map/stats/pallas_call | solution.py:391
  39.9 0.7 copy-done.9
  40.6 4.6 %stats.3.refs_7_ = f32[24,256]{1,0:T(8,128)} custom-call(s32[92]{0:T(128)} %get-tuple-element.49.meta.refs_0_, bf16[1024,128]{1,0:T(8,128)(2,1)} %copy-done.9, bf16[512,256]{1,0:T(8,128)(2,1)} %get-tuple-element.22.b0.refs_3_, bf16[512,256]{1,0:T(8,128)(2,1)} %copy-done.8, bf16[512,256]{1,0:T(8,128)(2,1)} %copy-done.7, bf16[512,256]{1,0:T(8,128)(2,1)} %copy-done.6, ...), custom_call_target="tpu_custom_call" | custom-call | flops 1073741824 | bytes 4194304 | tf_op jit(solution)/shard_map/stats/pallas_call | solution.py:391
  45.2 2.1 %collective-permute-start.6 = (f32[24,256]{1,0:T(8,128)}, f32[24,256]{1,0:T(8,128)S(1)}, u32[]{:S(2)}, u32[]{:S(2)}) collective-permute-start(f32[24,256]{1,0:T(8,128)} %stats.3.refs_7_), channel_id=1, source_target_pairs={{0,12},{4,0},{8,4},{12,8},{16,28},{20,16},{24,20},{28,24},{32,44},... | collective-permute-start | bytes 73736 | tf_op jit(solution)/shard_map/ppermute | solution.py:366
  47.3 1.2 %collective-permute-start.5 = (f32[24,256]{1,0:T(8,128)}, f32[24,256]{1,0:T(8,128)S(1)}, u32[]{:S(2)}, u32[]{:S(2)}) collective-permute-start(f32[24,256]{1,0:T(8,128)} %stats.3.refs_7_), channel_id=1, source_target_pairs={{0,8},{4,12},{8,0},{12,4},{16,24},{20,28},{24,16},{28,20},{32,40},... | collective-permute-start | bytes 73736 | tf_op jit(solution)/shard_map/ppermute | solution.py:366
  48.6 3.1 %collective-permute-done.5.refs_9_ = f32[24,256]{1,0:T(8,128)S(1)} collective-permute-done((f32[24,256]{1,0:T(8,128)}, f32[24,256]{1,0:T(8,128)S(1)}, u32[]{:S(2)}, u32[]{:S(2)}) %collective-permute-start.5) | collective-permute-done | bytes 24608 | tf_op jit(solution)/shard_map/ppermute | solution.py:366
  51.7 0.9 collective-permute-done.4.refs_8_
  53.3 7.1 %grads.2 = (bf16[2048,128]{1,0:T(8,128)(2,1)}, f32[1024,256]{1,0:T(8,128)}) custom-call(s32[92]{0:T(128)} %get-tuple-element.49.meta.refs_0_, bf16[1024,128]{1,0:T(8,128)(2,1)} %copy-done.9, bf16[1024,128]{1,0:T(8,128)(2,1)} %copy-done.10, bf16[512,256]{1,0:T(8,128)(2,1)} %get-tuple-element.22.b0.refs_3_, bf16[512,256]{1,0:T(8,128)(2,1)} %copy-done.8, ...), custom_call_target="tpu_custom_call" | custom-call | flops 2147483648 | bytes 8388608 | tf_op jit(solution)/shard_map/grads/pallas_call | solution.py:417
  60.3 3.0 %collective-permute-start.11 = (bf16[2048,128]{1,0:T(8,128)(2,1)}, bf16[2048,128]{1,0:T(8,128)(2,1)S(1)}, u32[]{:S(2)}, u32[]{:S(2)}) collective-permute-start(bf16[2048,128]{1,0:T(8,128)(2,1)} %get-tuple-element.32), channel_id=1, source_target_pairs={{0,128},{4,132},{8,136},{12,140},{16,144},{20,148},{24,152},{28,15... | collective-permute-start | bytes 1572872 | tf_op jit(solution)/shard_map/ppermute | solution.py:369
  63.3 7.8 %grads.3 = (bf16[2048,128]{1,0:T(8,128)(2,1)}, f32[128,512]{1,0:T(8,128)}, bf16[128,512]{1,0:T(8,128)(2,1)}, bf16[128,512]{1,0:T(8,128)(2,1)}, bf16[128,512]{1,0:T(8,128)(2,1)}) custom-call(s32[92]{0:T(128)} %get-tuple-element.50.meta.refs_0_, bf16[1024,128]{1,0:T(8,128)(2,1)} %bitcast.18, bf16[1024,128]{1,0:T(8,128)(2,1)} %bitcast.15, ...), custom_call_target="tpu_custom_call" | custom-call | flops 2147483648 | bytes 8388608 | tf_op jit(solution)/shard_map/grads/pallas_call | solution.py:417
  71.2 2.1 %add_convert_fusion = bf16[2048,128]{1,0:T(8,128)(2,1)} fusion(bf16[2048,128]{1,0:T(8,128)(2,1)S(1)} %collective-permute-done.11, bf16[2048,128]{1,0:T(8,128)(2,1)} %get-tuple-element.31), kind=kLoop, calls=%fused_computation | loop fusion | flops 1048576 | bytes 1572864 | tf_op jit(solution)/shard_map/convert_element_type | solution.py:467
  73.3 4.0 %all-to-all-start.1 = ((bf16[8,256,128]{2,1,0:T(8,128)(2,1)}), bf16[8,256,128]{2,1,0:T(8,128)(2,1)S(1)}, u32[]{:S(2)}, u32[]{:S(2)}) async-start(bf16[8,256,128]{2,1,0:T(8,128)(2,1)} %bitcast.11), calls=%async_computation.1 | async-start | bytes 1048576 | tf_op jit(solution)/shard_map/all_to_all | solution.py:363
  77.8 1.1 %collective-permute-start.9 = (bf16[128,512]{1,0:T(8,128)(2,1)}, bf16[128,512]{1,0:T(8,128)(2,1)S(1)}, u32[]{:S(2)}, u32[]{:S(2)}) collective-permute-start(bf16[128,512]{1,0:T(8,128)(2,1)} %get-tuple-element.29), channel_id=1, source_target_pairs={{0,8},{4,12},{8,0},{12,4},{16,24},{20,28},{24,16},{28,20},{32,40},... | collective-permute-start | bytes 393224 | tf_op jit(solution)/shard_map/ppermute | solution.py:366
  79.0 2.3 %collective-permute-done.8.d1 = bf16[128,512]{1,0:T(8,128)(2,1)S(1)} collective-permute-done((bf16[128,512]{1,0:T(8,128)(2,1)}, bf16[128,512]{1,0:T(8,128)(2,1)S(1)}, u32[]{:S(2)}, u32[]{:S(2)}) %collective-permute-start.8) | collective-permute-done | bytes 131104 | tf_op jit(solution)/shard_map/ppermute | solution.py:366
  81.3 2.1 %collective-permute-done.9.d2 = bf16[128,512]{1,0:T(8,128)(2,1)S(1)} collective-permute-done((bf16[128,512]{1,0:T(8,128)(2,1)}, bf16[128,512]{1,0:T(8,128)(2,1)S(1)}, u32[]{:S(2)}, u32[]{:S(2)}) %collective-permute-start.9) | collective-permute-done | bytes 131104 | tf_op jit(solution)/shard_map/ppermute | solution.py:366
  83.4 1.6 %collective-permute-done.10.d3 = bf16[128,512]{1,0:T(8,128)(2,1)S(1)} collective-permute-done((bf16[128,512]{1,0:T(8,128)(2,1)}, bf16[128,512]{1,0:T(8,128)(2,1)S(1)}, u32[]{:S(2)}, u32[]{:S(2)}) %collective-permute-start.10) | collective-permute-done | bytes 131104 | tf_op jit(solution)/shard_map/ppermute | solution.py:366
  85.0 1.0 copy-done.2
  86.1 0.9 copy-done.3
  87.0 2.7 %project.1 = (f32[128,512]{1,0:T(8,128)S(1)}, bf16[128,512]{1,0:T(8,128)(2,1)S(1)}, bf16[128,512]{1,0:T(8,128)(2,1)S(1)}, bf16[128,512]{1,0:T(8,128)(2,1)S(1)}) custom-call(s32[4]{0:T(128)S(1)} %and_select_fusion.3.peers, f32[128,512]{1,0:T(8,128)S(1)} %copy-done.3, bf16[128,512]{1,0:T(8,128)(2,1)S(1)} %collective-permute-done.8.d1, ...), custom_call_target="tpu_custom_call" | custom-call | tf_op jit(solution)/shard_map/project/pallas_call | solution.py:471
  89.7 9.1 %collective-permute-start.12 = (bf16[128,512]{1,0:T(8,128)(2,1)S(1)}, bf16[128,512]{1,0:T(8,128)(2,1)S(1)}, u32[]{:S(2)}, u32[]{:S(2)}) collective-permute-start(bf16[128,512]{1,0:T(8,128)(2,1)S(1)} %get-tuple-element.34), channel_id=1, source_target_pairs={{0,1},{1,2},{2,3},{3,0},{4,5},{5,6},{6,7},{7,4},{8,9},{9,10},{10,1... | collective-permute-start | bytes 393224 | tf_op jit(solution)/shard_map/ppermute | solution.py:489
  99.3 2.2 %collective-permute-done.12 = bf16[128,512]{1,0:T(8,128)(2,1)S(1)} collective-permute-done((bf16[128,512]{1,0:T(8,128)(2,1)S(1)}, bf16[128,512]{1,0:T(8,128)(2,1)S(1)}, u32[]{:S(2)}, u32[]{:S(2)}) %collective-permute-start.12) | collective-permute-done | bytes 131104 | tf_op jit(solution)/shard_map/ppermute | solution.py:489
  101.4 3.8 %collective-permute-done.13 = bf16[128,512]{1,0:T(8,128)(2,1)S(1)} collective-permute-done((bf16[128,512]{1,0:T(8,128)(2,1)S(1)}, bf16[128,512]{1,0:T(8,128)(2,1)S(1)}, u32[]{:S(2)}, u32[]{:S(2)}) %collective-permute-start.13) | collective-permute-done | bytes 131104 | tf_op jit(solution)/shard_map/ppermute | solution.py:489
  105.2 0.6 collective-permute-done.14
  105.8 0.7 add_convert_fusion.1
  (58 shorter events, 5.1 us)
Async XLA Ops:
  2.1 32.2 %collective-permute-start.2 = (bf16[512,256]{1,0:T(8,128)(2,1)}, bf16[512,256]{1,0:T(8,128)(2,1)S(1)}, u32[]{:S(2)}, u32[]{:S(2)}) collective-permute-start(bf16[512,256]{1,0:T(8,128)(2,1)} %get-tuple-element.22.b0.refs_3_), channel_id=1, source_target_pairs={{0,12},{4,0},{8,4},{12,8},{16,28},{20,16},{24,20},{28,24},{32,44},... | collective-permute-start | bytes 786440 | tf_op jit(solution)/shard_map/ppermute | solution.py:366
  5.4 28.9 %collective-permute-start.1 = (bf16[512,256]{1,0:T(8,128)(2,1)}, bf16[512,256]{1,0:T(8,128)(2,1)S(1)}, u32[]{:S(2)}, u32[]{:S(2)}) collective-permute-start(bf16[512,256]{1,0:T(8,128)(2,1)} %get-tuple-element.22.b0.refs_3_), channel_id=1, source_target_pairs={{0,8},{4,12},{8,0},{12,4},{16,24},{20,28},{24,16},{28,20},{32,40},... | collective-permute-start | bytes 786440 | tf_op jit(solution)/shard_map/ppermute | solution.py:366
  5.9 28.4 %collective-permute-start = (bf16[512,256]{1,0:T(8,128)(2,1)}, bf16[512,256]{1,0:T(8,128)(2,1)S(1)}, u32[]{:S(2)}, u32[]{:S(2)}) collective-permute-start(bf16[512,256]{1,0:T(8,128)(2,1)} %get-tuple-element.22.b0.refs_3_), channel_id=1, source_target_pairs={{0,4},{4,8},{8,12},{12,0},{16,20},{20,24},{24,28},{28,16},{32,36},... | collective-permute-start | bytes 786440 | tf_op jit(solution)/shard_map/ppermute | solution.py:366
  6.5 24.1 %all-to-all-start = ((bf16[8,256,128]{2,1,0:T(8,128)(2,1)}), bf16[8,256,128]{2,1,0:T(8,128)(2,1)S(1)}, u32[]{:S(2)}, u32[]{:S(2)}) async-start(bf16[8,256,128]{2,1,0:T(8,128)(2,1)} %bitcast.13), calls=%async_computation | async-start | bytes 1048576 | tf_op jit(solution)/shard_map/all_to_all | solution.py:363
  30.7 3.7 %copy-start.5 = (bf16[8,1,128,128]{3,2,1,0:T(8,128)(2,1)}, bf16[8,1,128,128]{3,2,1,0:T(8,128)(2,1)S(1)}, u32[]{:S(2)}) copy-start(bf16[8,1,128,128]{3,2,1,0:T(8,128)(2,1)S(1)} %get-tuple-element.46) | copy-start | bytes 786436
  30.7 9.0 %copy-start.4 = (bf16[8,1,128,128]{3,2,1,0:T(8,128)(2,1)}, bf16[8,1,128,128]{3,2,1,0:T(8,128)(2,1)S(1)}, u32[]{:S(2)}) copy-start(bf16[8,1,128,128]{3,2,1,0:T(8,128)(2,1)S(1)} %get-tuple-element.45) | copy-start | bytes 786436
  30.7 9.2 %collective-permute-start.3 = (bf16[1024,128]{1,0:T(8,128)(2,1)S(1)}, bf16[1024,128]{1,0:T(8,128)(2,1)S(1)}, u32[]{:S(2)}, u32[]{:S(2)}) collective-permute-start(bf16[1024,128]{1,0:T(8,128)(2,1)S(1)} %bitcast.16), channel_id=1, source_target_pairs={{0,128},{4,132},{8,136},{12,140},{16,144},{20,148},{24,152},{28,15... | collective-permute-start | bytes 786440 | tf_op jit(solution)/shard_map/ppermute | solution.py:369
  34.3 0.7 copy-start.6
  34.3 0.8 copy-start.7
  34.4 0.8 copy-start.8
  39.8 8.8 %collective-permute-start.7 = (bf16[1024,128]{1,0:T(8,128)(2,1)S(1)}, bf16[1024,128]{1,0:T(8,128)(2,1)S(1)}, u32[]{:S(2)}, u32[]{:S(2)}) collective-permute-start(bf16[1024,128]{1,0:T(8,128)(2,1)S(1)} %bitcast.14), channel_id=1, source_target_pairs={{0,128},{4,132},{8,136},{12,140},{16,144},{20,148},{24,152},{28,15... | collective-permute-start | bytes 786440 | tf_op jit(solution)/shard_map/ppermute | solution.py:369
  39.9 0.7 copy-start.9
  45.2 3.4 %collective-permute-start.6 = (f32[24,256]{1,0:T(8,128)}, f32[24,256]{1,0:T(8,128)S(1)}, u32[]{:S(2)}, u32[]{:S(2)}) collective-permute-start(f32[24,256]{1,0:T(8,128)} %stats.3.refs_7_), channel_id=1, source_target_pairs={{0,12},{4,0},{8,4},{12,8},{16,28},{20,16},{24,20},{28,24},{32,44},... | collective-permute-start | bytes 73736 | tf_op jit(solution)/shard_map/ppermute | solution.py:366
  47.3 4.4 %collective-permute-start.5 = (f32[24,256]{1,0:T(8,128)}, f32[24,256]{1,0:T(8,128)S(1)}, u32[]{:S(2)}, u32[]{:S(2)}) collective-permute-start(f32[24,256]{1,0:T(8,128)} %stats.3.refs_7_), channel_id=1, source_target_pairs={{0,8},{4,12},{8,0},{12,4},{16,24},{20,28},{24,16},{28,20},{32,40},... | collective-permute-start | bytes 73736 | tf_op jit(solution)/shard_map/ppermute | solution.py:366
  48.6 4.1 %collective-permute-start.4 = (f32[24,256]{1,0:T(8,128)}, f32[24,256]{1,0:T(8,128)S(1)}, u32[]{:S(2)}, u32[]{:S(2)}) collective-permute-start(f32[24,256]{1,0:T(8,128)} %stats.3.refs_7_), channel_id=1, source_target_pairs={{0,4},{4,8},{8,12},{12,0},{16,20},{20,24},{24,28},{28,16},{32,36},... | collective-permute-start | bytes 73736 | tf_op jit(solution)/shard_map/ppermute | solution.py:366
  48.6 4.1 %copy-start.10 = (bf16[1024,128]{1,0:T(8,128)(2,1)}, bf16[1024,128]{1,0:T(8,128)(2,1)S(1)}, u32[]{:S(2)}) copy-start(bf16[1024,128]{1,0:T(8,128)(2,1)S(1)} %collective-permute-done.7.refs_2_) | copy-start | bytes 786436
  48.6 4.1 %copy-start.11 = (f32[24,256]{1,0:T(8,128)}, f32[24,256]{1,0:T(8,128)S(1)}, u32[]{:S(2)}) copy-start(f32[24,256]{1,0:T(8,128)S(1)} %collective-permute-done.6.refs_10_) | copy-start | bytes 73732
  51.7 1.0 copy-start.12
  52.7 0.6 copy-start.13
  60.3 10.8 %collective-permute-start.11 = (bf16[2048,128]{1,0:T(8,128)(2,1)}, bf16[2048,128]{1,0:T(8,128)(2,1)S(1)}, u32[]{:S(2)}, u32[]{:S(2)}) collective-permute-start(bf16[2048,128]{1,0:T(8,128)(2,1)} %get-tuple-element.32), channel_id=1, source_target_pairs={{0,128},{4,132},{8,136},{12,140},{16,144},{20,148},{24,152},{28,15... | collective-permute-start | bytes 1572872 | tf_op jit(solution)/shard_map/ppermute | solution.py:369
  71.2 13.9 %copy-start = (bf16[2048,512]{1,0:T(8,128)(2,1)S(1)}, bf16[2048,512]{1,0:T(8,128)(2,1)}, u32[]{:S(2)}) copy-start(bf16[2048,512]{1,0:T(8,128)(2,1)} %wq_ref.1) | copy-start | bytes 6291460
  71.2 13.9 %copy-start.1 = (bf16[2048,128]{1,0:T(8,128)(2,1)S(1)}, bf16[2048,128]{1,0:T(8,128)(2,1)}, u32[]{:S(2)}) copy-start(bf16[2048,128]{1,0:T(8,128)(2,1)} %wk_ref.1) | copy-start | bytes 1572868
  73.3 11.7 %all-to-all-start.1 = ((bf16[8,256,128]{2,1,0:T(8,128)(2,1)}), bf16[8,256,128]{2,1,0:T(8,128)(2,1)S(1)}, u32[]{:S(2)}, u32[]{:S(2)}) async-start(bf16[8,256,128]{2,1,0:T(8,128)(2,1)} %bitcast.11), calls=%async_computation.1 | async-start | bytes 1048576 | tf_op jit(solution)/shard_map/all_to_all | solution.py:363
  77.3 4.0 %collective-permute-start.8 = (bf16[128,512]{1,0:T(8,128)(2,1)}, bf16[128,512]{1,0:T(8,128)(2,1)S(1)}, u32[]{:S(2)}, u32[]{:S(2)}) collective-permute-start(bf16[128,512]{1,0:T(8,128)(2,1)} %get-tuple-element.28), channel_id=1, source_target_pairs={{0,12},{4,0},{8,4},{12,8},{16,28},{20,16},{24,20},{28,24},{32,44},... | collective-permute-start | bytes 393224 | tf_op jit(solution)/shard_map/ppermute | solution.py:366
  77.8 5.6 %collective-permute-start.9 = (bf16[128,512]{1,0:T(8,128)(2,1)}, bf16[128,512]{1,0:T(8,128)(2,1)S(1)}, u32[]{:S(2)}, u32[]{:S(2)}) collective-permute-start(bf16[128,512]{1,0:T(8,128)(2,1)} %get-tuple-element.29), channel_id=1, source_target_pairs={{0,8},{4,12},{8,0},{12,4},{16,24},{20,28},{24,16},{28,20},{32,40},... | collective-permute-start | bytes 393224 | tf_op jit(solution)/shard_map/ppermute | solution.py:366
  78.9 6.1 %collective-permute-start.10 = (bf16[128,512]{1,0:T(8,128)(2,1)}, bf16[128,512]{1,0:T(8,128)(2,1)S(1)}, u32[]{:S(2)}, u32[]{:S(2)}) collective-permute-start(bf16[128,512]{1,0:T(8,128)(2,1)} %get-tuple-element.30), channel_id=1, source_target_pairs={{0,4},{4,8},{8,12},{12,0},{16,20},{20,24},{24,28},{28,16},{32,36},... | collective-permute-start | bytes 393224 | tf_op jit(solution)/shard_map/ppermute | solution.py:366
  85.0 1.0 copy-start.2
  86.1 0.9 copy-start.3
  89.7 11.8 %collective-permute-start.12 = (bf16[128,512]{1,0:T(8,128)(2,1)S(1)}, bf16[128,512]{1,0:T(8,128)(2,1)S(1)}, u32[]{:S(2)}, u32[]{:S(2)}) collective-permute-start(bf16[128,512]{1,0:T(8,128)(2,1)S(1)} %get-tuple-element.34), channel_id=1, source_target_pairs={{0,1},{1,2},{2,3},{3,0},{4,5},{5,6},{6,7},{7,4},{8,9},{9,10},{10,1... | collective-permute-start | bytes 393224 | tf_op jit(solution)/shard_map/ppermute | solution.py:489
  98.8 6.4 %collective-permute-start.13 = (bf16[128,512]{1,0:T(8,128)(2,1)S(1)}, bf16[128,512]{1,0:T(8,128)(2,1)S(1)}, u32[]{:S(2)}, u32[]{:S(2)}) collective-permute-start(bf16[128,512]{1,0:T(8,128)(2,1)S(1)} %get-tuple-element.35), channel_id=1, source_target_pairs={{0,2},{1,3},{2,0},{3,1},{4,6},{5,7},{6,4},{7,5},{8,10},{9,11},{10,... | collective-permute-start | bytes 393224 | tf_op jit(solution)/shard_map/ppermute | solution.py:489
  99.3 6.6 %collective-permute-start.14 = (bf16[128,512]{1,0:T(8,128)(2,1)S(1)}, bf16[128,512]{1,0:T(8,128)(2,1)S(1)}, u32[]{:S(2)}, u32[]{:S(2)}) collective-permute-start(bf16[128,512]{1,0:T(8,128)(2,1)S(1)} %get-tuple-element.36), channel_id=1, source_target_pairs={{0,3},{1,0},{2,1},{3,2},{4,7},{5,4},{6,5},{7,6},{8,11},{9,8},{10,9... | collective-permute-start | bytes 393224 | tf_op jit(solution)/shard_map/ppermute | solution.py:489

commit v5 on v4

--- a/solution.py
+++ b/solution.py
@@ -104,12 +104,20 @@
     return ref.at[part_slice(slot, 2 * COLS)]
 
 
-def stats_kernel(spans, steps, meta, k_ref, b0, b1, b2, b3, before, out_ref, kin, ks, qs, ms, ls, sems):
+def stats_kernel(spans, steps, meta, k_ref, b0, b1, b2, b3, before, *refs):
+    moves = []
+    if len(refs) == 11:
+        weights, out_ref, joined, held = refs[:2], refs[2], refs[3], refs[4]
+        halves = [held.at[part_slice(n, joined.shape[0] // 2)] for n in range(2)]
+        kin, ks, qs, ms, ls, sems = refs[5:]
+    else:
+        weights, halves, out_ref, (kin, ks, qs, ms, ls, sems) = [], [], refs[0], refs[1:]
     copies = load_all(
         (k_ref, *[b.at[:, :HEAD] for b in (b0, b1, b2, b3)]),
         (kin, *[slot_rows(qs, n) for n in range(SHARE)]),
         sems,
     )
+    fetched = load_all(weights, halves, sems.at[SHARE + 1 :])
     copies[0].wait()
 
     def copy_span(n, carry):
@@ -121,6 +129,11 @@
     ls[...] = jnp.zeros_like(ls)
     pattern = mask_pattern()
     for slot in range(SHARE):
+        if slot == 1 and fetched:
+            for copy in fetched:
+                copy.wait()
+            moves.append(pltpu.make_async_copy(held, joined, sems.at[SHARE + 3]))
+            moves[0].start()
         copies[1 + slot].wait()
         todo = slot_steps(meta, spans, steps, slot)
         scores = [
@@ -151,6 +164,8 @@
         total = jnp.sum(run_sum * jnp.exp2(run_max - top), axis=0, keepdims=True)
         out_ref[i : i + 1, :] = top
         out_ref[QSPANS + i : QSPANS + i + 1, :] = total + old_sum * jnp.exp2(old_max - top)
+    for move in moves:
+        move.wait()
 
 
 def grads_kernel(spans, steps, last, *refs):
@@ -266,13 +281,13 @@
 
 
 def project_kernel(
-    peers, d0, d1, d2, d3, dkv_ref, wk_ref, wv_ref, wq_ref, o0, o1, o2, o3,
-    own, others, dkv, wk, wv, sems,
+    peers, d0, d1, d2, d3, dkv_ref, narrow_ref, wq_ref, o0, o1, o2, o3,
+    own, others, dkv, narrow, sems,
 ):
     tokens, feats = o0.shape
     copies = load_all(
-        (d0, d1, d2, d3, dkv_ref, wk_ref, wv_ref),
-        (own, *[others.at[n] for n in range(SHARE - 1)], dkv, wk, wv),
+        (d0, d1, d2, d3, dkv_ref, narrow_ref),
+        (own, *[others.at[n] for n in range(SHARE - 1)], dkv, narrow),
         sems,
     )
     for copy in copies[:SHARE]:
@@ -290,9 +305,10 @@
     sums = sums.astype(BF16)
     for copy in copies[SHARE + 1 :]:
         copy.wait()
-    for at, total, out in zip(rows, totals, (o0, o1, o2, o3)):
-        total = total + dot(sums[:tokens], wk[at, :], 1, 1)
-        total = total + dot(sums[tokens:], wv[at, :], 1, 1)
+    lower = [rows_at(peers[s] + SHARE, feats) for s in range(SHARE)]
+    for at, low, total, out in zip(rows, lower, totals, (o0, o1, o2, o3)):
+        total = total + dot(sums[:tokens], narrow[at, :], 1, 1)
+        total = total + dot(sums[tokens:], narrow[low, :], 1, 1)
         out[...] = total.astype(out.dtype)
 
 
@@ -387,30 +403,33 @@
     k_own, v_own = [sides[:, n].reshape(spans * SPAN, HEAD) for n in range(2)]
     k_other = crossed(k_own)
 
-    def stats_of(table, keys, before):
+    def stats_of(table, keys, before, weights):
         return pl.pallas_call(
             functools.partial(stats_kernel, spans, steps),
-            out_shape=shape((STATS, COLS), F32),
-            in_specs=[SMEM] + [HBM] * 5 + [VMEM],
-            out_specs=VMEM,
+            out_shape=[shape((STATS, COLS), F32)]
+            + [shape((2 * w.shape[0], HEAD), BF16) for w in weights[:1]],
+            in_specs=[SMEM] + [HBM] * 5 + [VMEM] + [HBM] * len(weights),
+            out_specs=[VMEM] + [HBM] * len(weights[:1]),
             scratch_shapes=[
+                *[pltpu.VMEM((2 * w.shape[0], HEAD), BF16) for w in weights[:1]],
                 pltpu.VMEM((spans * SPAN, HEAD), BF16),
                 pltpu.VMEM((spans * SPAN, HEAD), BF16),
                 pltpu.VMEM((QSPANS * COLS, HEAD), BF16),
                 pltpu.VMEM((QSPANS * 8, COLS), F32),
                 pltpu.VMEM((QSPANS * 8, COLS), F32),
-                pltpu.SemaphoreType.DMA((5,)),
+                pltpu.SemaphoreType.DMA((8,)),
             ],
             compiler_params=LARGE,
             cost_estimate=pl.CostEstimate(
                 flops=1 << 30, bytes_accessed=1 << 22, transcendentals=1 << 22
             ),
             name="stats",
-        )(table, keys, *blocks, before)
-
-    stats_own, v_late = lax.optimization_barrier((stats_of(meta_own, k_own, start), v_own))
+        )(table, keys, *blocks, before, *weights)
+
+    stats_own, narrow = stats_of(meta_own, k_own, start, [key_weight, value_weight])
+    stats_own, v_late = lax.optimization_barrier((stats_own, v_own))
     v_other = crossed(v_late)
-    stats = stats_of(meta_other, k_other, stats_own)
+    (stats,) = stats_of(meta_other, k_other, stats_own, [])
     all_stats = [stats] + [shifted(stats, s) for s in range(1, SHARE)]
 
     def grads_of(table, keys, values, last, extra_in, outs, extra_scratch):
@@ -471,19 +490,18 @@
     own, *pieces = pl.pallas_call(
         project_kernel,
         out_shape=[shape((tokens, feats), F32)] + [shape((tokens, feats), BF16)] * (tp_size - 1),
-        in_specs=[SMEM] + [HBM] * 7 + [VMEM],
+        in_specs=[SMEM] + [HBM] * 6 + [VMEM],
         out_specs=[VMEM] * tp_size,
         scratch_shapes=[
             pltpu.VMEM((tokens, WIDTH), F32),
             pltpu.VMEM((SHARE - 1, tokens, WIDTH), BF16),
             pltpu.VMEM((half_rows, HEAD), BF16),
-            pltpu.VMEM(key_weight.shape, BF16),
-            pltpu.VMEM(value_weight.shape, BF16),
-            pltpu.SemaphoreType.DMA((7,)),
+            pltpu.VMEM(narrow.shape, BF16),
+            pltpu.SemaphoreType.DMA((6,)),
         ],
         compiler_params=SMALL,
         name="project",
-    )(peers, dqs[0], *dq_parts, dkv_parts, key_weight, value_weight, w_query)
+    )(peers, dqs[0], *dq_parts, dkv_parts, narrow, w_query)
     for s in range(1, tp_size):
         pairs = [(d, (d + s) % tp_size) for d in range(tp_size)]
         own = own + lax.ppermute(pieces[s - 1], "tp", pairs).astype(F32)

time: 107 us -> 107 us (level)
    unnamed x28 -> x30, local copies, waits for them, and re-layouts: 4.12 us -> 3.42 us
where the time goes in v5:
time: 107 us; the launch traced here: 106 us
  starting transfers between devices  37.6 us (35%)
  waiting for transfers between devices  29.6 us (28%)
  Pallas kernels  28.7 us (27%)
  local copies, waits for them, and re-layouts  5.23 us (5%)
  other arithmetic  4.47 us (4%)
    pallas_call x2, Pallas kernels, grads_of(): pl.pallas_call(functools.partial(grads_kernel, spans, steps, last), out_s...  14.9 us
    all_to_all x2, waiting for transfers between devices, exchanged(): lax.all_to_all(array, 'ctx', 0, 0, tiled=True, axis_index_groups=groups)  13.1 us
    all_to_all x2, starting transfers between devices, exchanged(): lax.all_to_all(array, 'ctx', 0, 0, tiled=True, axis_index_groups=groups)  12.1 us
    ppermute x9, waiting for transfers between devices, shifted(): lax.ppermute(array, 'ctx', [(device(a, b, c), device(a, b, c + by)) for a...  9.96 us
    ppermute x3, starting transfers between devices, local(): own = own + lax.ppermute(pieces[s - 1], 'tp', pairs).astype(F32)  9.7 us
    ppermute x9, starting transfers between devices, shifted(): lax.ppermute(array, 'ctx', [(device(a, b, c), device(a, b, c + by)) for a...  9.6 us
    pallas_call x2, Pallas kernels, stats_of(): pl.pallas_call(functools.partial(stats_kernel, spans, steps), out_shape=[...  9.15 us
    ppermute x3, waiting for transfers between devices, local(): own = own + lax.ppermute(pieces[s - 1], 'tp', pairs).astype(F32)  6.52 us
  transfers between devices with their start and end apart: 17, of which 9 were waited for; matrix products, arithmetic and copies ran while one was open for 3% of the time, Pallas kernels for 16%

profile of v5, /device:TPU:1, one launch (start us, length us, event | category | flops | bytes accessed | tf_op | source)
XLA Modules:
  0.0 105.9 jit_solution(7808912506513444550)
XLA Ops:
  0.0 2.1 %pack.1 = (bf16[2048,128]{1,0:T(8,128)(2,1)}, bf16[512,256]{1,0:T(8,128)(2,1)}, f32[24,256]{1,0:T(8,128)}) custom-call(bf16[128,128]{1,0:T(8,128)(2,1)} %k_ref.1, bf16[128,128]{1,0:T(8,128)(2,1)} %v_ref.1, bf16[128,512]{1,0:T(8,128)(2,1)} %q_ref.1, bf16[128,512]{1,0:T(8,128)(2,1)} %g_ref.1, bf16[128,512]{1,0:T(8,128)(2,1)} %o_ref.1), custom_call_target="tpu_custom_call" | custom-call | tf_op jit(solution)/shard_map/pack/pallas_call | solution.py:387
  2.1 3.3 %collective-permute-start.2 = (bf16[512,256]{1,0:T(8,128)(2,1)}, bf16[512,256]{1,0:T(8,128)(2,1)S(1)}, u32[]{:S(2)}, u32[]{:S(2)}) collective-permute-start(bf16[512,256]{1,0:T(8,128)(2,1)} %get-tuple-element.24.b0.refs_3_), channel_id=1, source_target_pairs={{0,12},{4,0},{8,4},{12,8},{16,28},{20,16},{24,20},{28,24},{32,44},... | collective-permute-start | bytes 786440 | tf_op jit(solution)/shard_map/ppermute | solution.py:382
  6.5 8.2 %all-to-all-start = ((bf16[8,256,128]{2,1,0:T(8,128)(2,1)}), bf16[8,256,128]{2,1,0:T(8,128)(2,1)S(1)}, u32[]{:S(2)}, u32[]{:S(2)}) async-start(bf16[8,256,128]{2,1,0:T(8,128)(2,1)} %bitcast.12), calls=%async_computation | async-start | bytes 1048576 | tf_op jit(solution)/shard_map/all_to_all | solution.py:379
  14.7 0.8 reshape.127
  15.7 0.9 select_reduce_fusion.2
  17.6 13.1 %all-to-all-done = bf16[8,256,128]{2,1,0:T(8,128)(2,1)S(1)} async-done(((bf16[8,256,128]{2,1,0:T(8,128)(2,1)}), bf16[8,256,128]{2,1,0:T(8,128)(2,1)S(1)}, u32[]{:S(2)}, u32[]{:S(2)}) %all-to-all-start) | async-done | bytes 524320 | tf_op jit(solution)/shard_map/all_to_all | solution.py:379
  30.7 3.0 %collective-permute-start.3 = (bf16[1024,128]{1,0:T(8,128)(2,1)S(1)}, bf16[1024,128]{1,0:T(8,128)(2,1)S(1)}, u32[]{:S(2)}, u32[]{:S(2)}) collective-permute-start(bf16[1024,128]{1,0:T(8,128)(2,1)S(1)} %bitcast.15), channel_id=1, source_target_pairs={{0,128},{4,132},{8,136},{12,140},{16,144},{20,148},{24,152},{28,15... | collective-permute-start | bytes 786440 | tf_op jit(solution)/shard_map/ppermute | solution.py:385
  34.4 0.7 copy-done.5
  35.2 4.6 %stats.2 = (f32[24,256]{1,0:T(8,128)}, bf16[4096,128]{1,0:T(8,128)(2,1)}) custom-call(s32[92]{0:T(128)} %get-tuple-element.54.meta.refs_0_, bf16[1024,128]{1,0:T(8,128)(2,1)} %bitcast.16, bf16[512,256]{1,0:T(8,128)(2,1)} %get-tuple-element.24.b0.refs_3_, bf16[512,256]{1,0:T(8,128)(2,1)} %copy-done.7, bf16[512,256]{1,0:T(8,128)(2,1)} %copy-done.6, ...), custom_call_target="tpu_custom_call" | custom-call | flops 1073741824 | bytes 4194304 | tf_op jit(solution)/shard_map/stats/pallas_call | solution.py:407
  40.0 0.7 copy-done.8
  40.7 4.6 %stats.3.refs_7_ = f32[24,256]{1,0:T(8,128)} custom-call(s32[92]{0:T(128)} %get-tuple-element.53.meta.refs_0_, bf16[1024,128]{1,0:T(8,128)(2,1)} %copy-done.8, bf16[512,256]{1,0:T(8,128)(2,1)} %get-tuple-element.24.b0.refs_3_, bf16[512,256]{1,0:T(8,128)(2,1)} %copy-done.7, bf16[512,256]{1,0:T(8,128)(2,1)} %copy-done.6, bf16[512,256]{1,0:T(8,128)(2,1)} %copy-done.5, ...), custom_call_target="tpu_custom_call" | custom-call | flops 1073741824 | bytes 4194304 | tf_op jit(solution)/shard_map/stats/pallas_call | solution.py:407
  45.3 2.2 %collective-permute-start.6 = (f32[24,256]{1,0:T(8,128)}, f32[24,256]{1,0:T(8,128)S(1)}, u32[]{:S(2)}, u32[]{:S(2)}) collective-permute-start(f32[24,256]{1,0:T(8,128)} %stats.3.refs_7_), channel_id=1, source_target_pairs={{0,12},{4,0},{8,4},{12,8},{16,28},{20,16},{24,20},{28,24},{32,44},... | collective-permute-start | bytes 73736 | tf_op jit(solution)/shard_map/ppermute | solution.py:382
  47.5 1.2 %collective-permute-start.5 = (f32[24,256]{1,0:T(8,128)}, f32[24,256]{1,0:T(8,128)S(1)}, u32[]{:S(2)}, u32[]{:S(2)}) collective-permute-start(f32[24,256]{1,0:T(8,128)} %stats.3.refs_7_), channel_id=1, source_target_pairs={{0,8},{4,12},{8,0},{12,4},{16,24},{20,28},{24,16},{28,20},{32,40},... | collective-permute-start | bytes 73736 | tf_op jit(solution)/shard_map/ppermute | solution.py:382
  48.7 3.1 %collective-permute-done.5.refs_9_ = f32[24,256]{1,0:T(8,128)S(1)} collective-permute-done((f32[24,256]{1,0:T(8,128)}, f32[24,256]{1,0:T(8,128)S(1)}, u32[]{:S(2)}, u32[]{:S(2)}) %collective-permute-start.5) | collective-permute-done | bytes 24608 | tf_op jit(solution)/shard_map/ppermute | solution.py:382
  51.9 0.9 collective-permute-done.4.refs_8_
  53.4 7.1 %grads.2 = (bf16[2048,128]{1,0:T(8,128)(2,1)}, f32[1024,256]{1,0:T(8,128)}) custom-call(s32[92]{0:T(128)} %get-tuple-element.53.meta.refs_0_, bf16[1024,128]{1,0:T(8,128)(2,1)} %copy-done.8, bf16[1024,128]{1,0:T(8,128)(2,1)} %copy-done.9, bf16[512,256]{1,0:T(8,128)(2,1)} %get-tuple-element.24.b0.refs_3_, bf16[512,256]{1,0:T(8,128)(2,1)} %copy-done.7, ...), custom_call_target="tpu_custom_call" | custom-call | flops 2147483648 | bytes 8388608 | tf_op jit(solution)/shard_map/grads/pallas_call | solution.py:436
  60.5 3.0 %collective-permute-start.11 = (bf16[2048,128]{1,0:T(8,128)(2,1)}, bf16[2048,128]{1,0:T(8,128)(2,1)S(1)}, u32[]{:S(2)}, u32[]{:S(2)}) collective-permute-start(bf16[2048,128]{1,0:T(8,128)(2,1)} %get-tuple-element.35), channel_id=1, source_target_pairs={{0,128},{4,132},{8,136},{12,140},{16,144},{20,148},{24,152},{28,15... | collective-permute-start | bytes 1572872 | tf_op jit(solution)/shard_map/ppermute | solution.py:385
  63.4 7.8 %grads.3 = (bf16[2048,128]{1,0:T(8,128)(2,1)}, f32[128,512]{1,0:T(8,128)}, bf16[128,512]{1,0:T(8,128)(2,1)}, bf16[128,512]{1,0:T(8,128)(2,1)}, bf16[128,512]{1,0:T(8,128)(2,1)}) custom-call(s32[92]{0:T(128)} %get-tuple-element.54.meta.refs_0_, bf16[1024,128]{1,0:T(8,128)(2,1)} %bitcast.17, bf16[1024,128]{1,0:T(8,128)(2,1)} %bitcast.14, ...), custom_call_target="tpu_custom_call" | custom-call | flops 2147483648 | bytes 8388608 | tf_op jit(solution)/shard_map/grads/pallas_call | solution.py:436
  71.3 2.1 %add_convert_fusion = bf16[2048,128]{1,0:T(8,128)(2,1)} fusion(bf16[2048,128]{1,0:T(8,128)(2,1)S(1)} %collective-permute-done.11, bf16[2048,128]{1,0:T(8,128)(2,1)} %get-tuple-element.34), kind=kLoop, calls=%fused_computation | loop fusion | flops 1048576 | bytes 1572864 | tf_op jit(solution)/shard_map/convert_element_type | solution.py:486
  73.4 4.0 %all-to-all-start.1 = ((bf16[8,256,128]{2,1,0:T(8,128)(2,1)}), bf16[8,256,128]{2,1,0:T(8,128)(2,1)S(1)}, u32[]{:S(2)}, u32[]{:S(2)}) async-start(bf16[8,256,128]{2,1,0:T(8,128)(2,1)} %bitcast.6), calls=%async_computation.1 | async-start | bytes 1048576 | tf_op jit(solution)/shard_map/all_to_all | solution.py:379
  77.4 0.6 collective-permute-start.8
  78.0 1.0 collective-permute-start.9
  79.2 2.2 %collective-permute-done.8.d1 = bf16[128,512]{1,0:T(8,128)(2,1)S(1)} collective-permute-done((bf16[128,512]{1,0:T(8,128)(2,1)}, bf16[128,512]{1,0:T(8,128)(2,1)S(1)}, u32[]{:S(2)}, u32[]{:S(2)}) %collective-permute-start.8) | collective-permute-done | bytes 131104 | tf_op jit(solution)/shard_map/ppermute | solution.py:382
  81.4 2.0 %collective-permute-done.9.d2 = bf16[128,512]{1,0:T(8,128)(2,1)S(1)} collective-permute-done((bf16[128,512]{1,0:T(8,128)(2,1)S(1)}, bf16[128,512]{1,0:T(8,128)(2,1)S(1)}, u32[]{:S(2)}, u32[]{:S(2)}) %collective-permute-start.9) | collective-permute-done | bytes 131104 | tf_op jit(solution)/shard_map/ppermute | solution.py:382
  83.4 1.6 %collective-permute-done.10.d3 = bf16[128,512]{1,0:T(8,128)(2,1)S(1)} collective-permute-done((bf16[128,512]{1,0:T(8,128)(2,1)S(1)}, bf16[128,512]{1,0:T(8,128)(2,1)S(1)}, u32[]{:S(2)}, u32[]{:S(2)}) %collective-permute-start.10) | collective-permute-done | bytes 131104 | tf_op jit(solution)/shard_map/ppermute | solution.py:382
  85.1 1.2 %copy-done.1 = bf16[4096,128]{1,0:T(8,128)(2,1)S(1)} copy-done((bf16[4096,128]{1,0:T(8,128)(2,1)S(1)}, bf16[4096,128]{1,0:T(8,128)(2,1)}, u32[]{:S(2)}) %copy-start.1) | copy-done | bytes 1048600
  86.3 2.6 %project.1 = (f32[128,512]{1,0:T(8,128)S(1)}, bf16[128,512]{1,0:T(8,128)(2,1)S(1)}, bf16[128,512]{1,0:T(8,128)(2,1)S(1)}, bf16[128,512]{1,0:T(8,128)(2,1)S(1)}) custom-call(s32[4]{0:T(128)S(1)} %and_select_fusion.3.peers, f32[128,512]{1,0:T(8,128)S(1)} %copy-done.2, bf16[128,512]{1,0:T(8,128)(2,1)S(1)} %collective-permute-done.8.d1, ...), custom_call_target="tpu_custom_call" | custom-call | tf_op jit(solution)/shard_map/project/pallas_call | solution.py:490
  88.9 9.2 %collective-permute-start.12 = (bf16[128,512]{1,0:T(8,128)(2,1)S(1)}, bf16[128,512]{1,0:T(8,128)(2,1)S(1)}, u32[]{:S(2)}, u32[]{:S(2)}) collective-permute-start(bf16[128,512]{1,0:T(8,128)(2,1)S(1)} %get-tuple-element.38), channel_id=1, source_target_pairs={{0,1},{1,2},{2,3},{3,0},{4,5},{5,6},{6,7},{7,4},{8,9},{9,10},{10,1... | collective-permute-start | bytes 393224 | tf_op jit(solution)/shard_map/ppermute | solution.py:507
  98.6 2.2 %collective-permute-done.12 = bf16[128,512]{1,0:T(8,128)(2,1)S(1)} collective-permute-done((bf16[128,512]{1,0:T(8,128)(2,1)S(1)}, bf16[128,512]{1,0:T(8,128)(2,1)S(1)}, u32[]{:S(2)}, u32[]{:S(2)}) %collective-permute-start.12) | collective-permute-done | bytes 131104 | tf_op jit(solution)/shard_map/ppermute | solution.py:507
  100.8 3.7 %collective-permute-done.13 = bf16[128,512]{1,0:T(8,128)(2,1)S(1)} collective-permute-done((bf16[128,512]{1,0:T(8,128)(2,1)S(1)}, bf16[128,512]{1,0:T(8,128)(2,1)S(1)}, u32[]{:S(2)}, u32[]{:S(2)}) %collective-permute-start.13) | collective-permute-done | bytes 131104 | tf_op jit(solution)/shard_map/ppermute | solution.py:507
  104.5 0.6 collective-permute-done.14
  105.2 0.7 add_convert_fusion.1
  (60 shorter events, 4.6 us)
Async XLA Ops:
  2.1 32.2 %collective-permute-start.2 = (bf16[512,256]{1,0:T(8,128)(2,1)}, bf16[512,256]{1,0:T(8,128)(2,1)S(1)}, u32[]{:S(2)}, u32[]{:S(2)}) collective-permute-start(bf16[512,256]{1,0:T(8,128)(2,1)} %get-tuple-element.24.b0.refs_3_), channel_id=1, source_target_pairs={{0,12},{4,0},{8,4},{12,8},{16,28},{20,16},{24,20},{28,24},{32,44},... | collective-permute-start | bytes 786440 | tf_op jit(solution)/shard_map/ppermute | solution.py:382
  5.4 28.9 %collective-permute-start.1 = (bf16[512,256]{1,0:T(8,128)(2,1)}, bf16[512,256]{1,0:T(8,128)(2,1)S(1)}, u32[]{:S(2)}, u32[]{:S(2)}) collective-permute-start(bf16[512,256]{1,0:T(8,128)(2,1)} %get-tuple-element.24.b0.refs_3_), channel_id=1, source_target_pairs={{0,8},{4,12},{8,0},{12,4},{16,24},{20,28},{24,16},{28,20},{32,40},... | collective-permute-start | bytes 786440 | tf_op jit(solution)/shard_map/ppermute | solution.py:382
  5.9 28.4 %collective-permute-start = (bf16[512,256]{1,0:T(8,128)(2,1)}, bf16[512,256]{1,0:T(8,128)(2,1)S(1)}, u32[]{:S(2)}, u32[]{:S(2)}) collective-permute-start(bf16[512,256]{1,0:T(8,128)(2,1)} %get-tuple-element.24.b0.refs_3_), channel_id=1, source_target_pairs={{0,4},{4,8},{8,12},{12,0},{16,20},{20,24},{24,28},{28,16},{32,36},... | collective-permute-start | bytes 786440 | tf_op jit(solution)/shard_map/ppermute | solution.py:382
  6.5 24.1 %all-to-all-start = ((bf16[8,256,128]{2,1,0:T(8,128)(2,1)}), bf16[8,256,128]{2,1,0:T(8,128)(2,1)S(1)}, u32[]{:S(2)}, u32[]{:S(2)}) async-start(bf16[8,256,128]{2,1,0:T(8,128)(2,1)} %bitcast.12), calls=%async_computation | async-start | bytes 1048576 | tf_op jit(solution)/shard_map/all_to_all | solution.py:379
  30.7 3.7 %copy-start.4 = (bf16[8,1,128,128]{3,2,1,0:T(8,128)(2,1)}, bf16[8,1,128,128]{3,2,1,0:T(8,128)(2,1)S(1)}, u32[]{:S(2)}) copy-start(bf16[8,1,128,128]{3,2,1,0:T(8,128)(2,1)S(1)} %get-tuple-element.50) | copy-start | bytes 786436
  30.7 9.1 %copy-start.3 = (bf16[8,1,128,128]{3,2,1,0:T(8,128)(2,1)}, bf16[8,1,128,128]{3,2,1,0:T(8,128)(2,1)S(1)}, u32[]{:S(2)}) copy-start(bf16[8,1,128,128]{3,2,1,0:T(8,128)(2,1)S(1)} %get-tuple-element.49) | copy-start | bytes 786436
  30.7 9.3 %collective-permute-start.3 = (bf16[1024,128]{1,0:T(8,128)(2,1)S(1)}, bf16[1024,128]{1,0:T(8,128)(2,1)S(1)}, u32[]{:S(2)}, u32[]{:S(2)}) collective-permute-start(bf16[1024,128]{1,0:T(8,128)(2,1)S(1)} %bitcast.15), channel_id=1, source_target_pairs={{0,128},{4,132},{8,136},{12,140},{16,144},{20,148},{24,152},{28,15... | collective-permute-start | bytes 786440 | tf_op jit(solution)/shard_map/ppermute | solution.py:385
  34.3 0.7 copy-start.5
  34.3 0.8 copy-start.6
  34.4 0.9 copy-start.7
  39.8 8.9 %collective-permute-start.7 = (bf16[1024,128]{1,0:T(8,128)(2,1)S(1)}, bf16[1024,128]{1,0:T(8,128)(2,1)S(1)}, u32[]{:S(2)}, u32[]{:S(2)}) collective-permute-start(bf16[1024,128]{1,0:T(8,128)(2,1)S(1)} %bitcast.13), channel_id=1, source_target_pairs={{0,128},{4,132},{8,136},{12,140},{16,144},{20,148},{24,152},{28,15... | collective-permute-start | bytes 786440 | tf_op jit(solution)/shard_map/ppermute | solution.py:385
  40.0 0.7 copy-start.8
  45.3 3.4 %collective-permute-start.6 = (f32[24,256]{1,0:T(8,128)}, f32[24,256]{1,0:T(8,128)S(1)}, u32[]{:S(2)}, u32[]{:S(2)}) collective-permute-start(f32[24,256]{1,0:T(8,128)} %stats.3.refs_7_), channel_id=1, source_target_pairs={{0,12},{4,0},{8,4},{12,8},{16,28},{20,16},{24,20},{28,24},{32,44},... | collective-permute-start | bytes 73736 | tf_op jit(solution)/shard_map/ppermute | solution.py:382
  47.5 4.4 %collective-permute-start.5 = (f32[24,256]{1,0:T(8,128)}, f32[24,256]{1,0:T(8,128)S(1)}, u32[]{:S(2)}, u32[]{:S(2)}) collective-permute-start(f32[24,256]{1,0:T(8,128)} %stats.3.refs_7_), channel_id=1, source_target_pairs={{0,8},{4,12},{8,0},{12,4},{16,24},{20,28},{24,16},{28,20},{32,40},... | collective-permute-start | bytes 73736 | tf_op jit(solution)/shard_map/ppermute | solution.py:382
  48.7 4.1 %collective-permute-start.4 = (f32[24,256]{1,0:T(8,128)}, f32[24,256]{1,0:T(8,128)S(1)}, u32[]{:S(2)}, u32[]{:S(2)}) collective-permute-start(f32[24,256]{1,0:T(8,128)} %stats.3.refs_7_), channel_id=1, source_target_pairs={{0,4},{4,8},{8,12},{12,0},{16,20},{20,24},{24,28},{28,16},{32,36},... | collective-permute-start | bytes 73736 | tf_op jit(solution)/shard_map/ppermute | solution.py:382
  48.7 4.1 %copy-start.9 = (bf16[1024,128]{1,0:T(8,128)(2,1)}, bf16[1024,128]{1,0:T(8,128)(2,1)S(1)}, u32[]{:S(2)}) copy-start(bf16[1024,128]{1,0:T(8,128)(2,1)S(1)} %collective-permute-done.7.refs_2_) | copy-start | bytes 786436
  48.7 4.1 %copy-start.12 = (f32[24,256]{1,0:T(8,128)}, f32[24,256]{1,0:T(8,128)S(1)}, u32[]{:S(2)}) copy-start(f32[24,256]{1,0:T(8,128)S(1)} %collective-permute-done.6.refs_10_) | copy-start | bytes 73732
  51.9 1.0 copy-start.13
  52.8 0.6 copy-start.14
  60.5 10.8 %collective-permute-start.11 = (bf16[2048,128]{1,0:T(8,128)(2,1)}, bf16[2048,128]{1,0:T(8,128)(2,1)S(1)}, u32[]{:S(2)}, u32[]{:S(2)}) collective-permute-start(bf16[2048,128]{1,0:T(8,128)(2,1)} %get-tuple-element.35), channel_id=1, source_target_pairs={{0,128},{4,132},{8,136},{12,140},{16,144},{20,148},{24,152},{28,15... | collective-permute-start | bytes 1572872 | tf_op jit(solution)/shard_map/ppermute | solution.py:385
  71.2 6.8 %copy-start.11 = (bf16[128,512]{1,0:T(8,128)(2,1)S(1)}, bf16[128,512]{1,0:T(8,128)(2,1)}, u32[]{:S(2)}) copy-start(bf16[128,512]{1,0:T(8,128)(2,1)} %get-tuple-element.32) | copy-start | bytes 393220
  71.2 7.7 %copy-start.10 = (bf16[128,512]{1,0:T(8,128)(2,1)S(1)}, bf16[128,512]{1,0:T(8,128)(2,1)}, u32[]{:S(2)}) copy-start(bf16[128,512]{1,0:T(8,128)(2,1)} %get-tuple-element.33) | copy-start | bytes 393220
  71.3 13.8 %copy-start = (bf16[2048,512]{1,0:T(8,128)(2,1)S(1)}, bf16[2048,512]{1,0:T(8,128)(2,1)}, u32[]{:S(2)}) copy-start(bf16[2048,512]{1,0:T(8,128)(2,1)} %wq_ref.1) | copy-start | bytes 6291460
  71.3 13.8 %copy-start.2 = (f32[128,512]{1,0:T(8,128)S(1)}, f32[128,512]{1,0:T(8,128)}, u32[]{:S(2)}) copy-start(f32[128,512]{1,0:T(8,128)} %get-tuple-element.30.d0) | copy-start | bytes 786436
  73.4 11.6 %all-to-all-start.1 = ((bf16[8,256,128]{2,1,0:T(8,128)(2,1)}), bf16[8,256,128]{2,1,0:T(8,128)(2,1)S(1)}, u32[]{:S(2)}, u32[]{:S(2)}) async-start(bf16[8,256,128]{2,1,0:T(8,128)(2,1)} %bitcast.6), calls=%async_computation.1 | async-start | bytes 1048576 | tf_op jit(solution)/shard_map/all_to_all | solution.py:379
  77.4 4.0 %collective-permute-start.8 = (bf16[128,512]{1,0:T(8,128)(2,1)}, bf16[128,512]{1,0:T(8,128)(2,1)S(1)}, u32[]{:S(2)}, u32[]{:S(2)}) collective-permute-start(bf16[128,512]{1,0:T(8,128)(2,1)} %get-tuple-element.31), channel_id=1, source_target_pairs={{0,12},{4,0},{8,4},{12,8},{16,28},{20,16},{24,20},{28,24},{32,44},... | collective-permute-start | bytes 393224 | tf_op jit(solution)/shard_map/ppermute | solution.py:382
  78.0 5.4 %collective-permute-start.9 = (bf16[128,512]{1,0:T(8,128)(2,1)S(1)}, bf16[128,512]{1,0:T(8,128)(2,1)S(1)}, u32[]{:S(2)}, u32[]{:S(2)}) collective-permute-start(bf16[128,512]{1,0:T(8,128)(2,1)S(1)} %copy-done.11), channel_id=1, source_target_pairs={{0,8},{4,12},{8,0},{12,4},{16,24},{20,28},{24,16},{28,20},{32,40},... | collective-permute-start | bytes 393224 | tf_op jit(solution)/shard_map/ppermute | solution.py:382
  79.0 6.1 %collective-permute-start.10 = (bf16[128,512]{1,0:T(8,128)(2,1)S(1)}, bf16[128,512]{1,0:T(8,128)(2,1)S(1)}, u32[]{:S(2)}, u32[]{:S(2)}) collective-permute-start(bf16[128,512]{1,0:T(8,128)(2,1)S(1)} %copy-done.10), channel_id=1, source_target_pairs={{0,4},{4,8},{8,12},{12,0},{16,20},{20,24},{24,28},{28,16},{32,36},... | collective-permute-start | bytes 393224 | tf_op jit(solution)/shard_map/ppermute | solution.py:382
  85.1 1.2 %copy-start.1 = (bf16[4096,128]{1,0:T(8,128)(2,1)S(1)}, bf16[4096,128]{1,0:T(8,128)(2,1)}, u32[]{:S(2)}) copy-start(bf16[4096,128]{1,0:T(8,128)(2,1)} %get-tuple-element.36.narrow_ref) | copy-start | bytes 3145732
  88.9 11.9 %collective-permute-start.12 = (bf16[128,512]{1,0:T(8,128)(2,1)S(1)}, bf16[128,512]{1,0:T(8,128)(2,1)S(1)}, u32[]{:S(2)}, u32[]{:S(2)}) collective-permute-start(bf16[128,512]{1,0:T(8,128)(2,1)S(1)} %get-tuple-element.38), channel_id=1, source_target_pairs={{0,1},{1,2},{2,3},{3,0},{4,5},{5,6},{6,7},{7,4},{8,9},{9,10},{10,1... | collective-permute-start | bytes 393224 | tf_op jit(solution)/shard_map/ppermute | solution.py:507
  98.1 6.4 %collective-permute-start.13 = (bf16[128,512]{1,0:T(8,128)(2,1)S(1)}, bf16[128,512]{1,0:T(8,128)(2,1)S(1)}, u32[]{:S(2)}, u32[]{:S(2)}) collective-permute-start(bf16[128,512]{1,0:T(8,128)(2,1)S(1)} %get-tuple-element.39), channel_id=1, source_target_pairs={{0,2},{1,3},{2,0},{3,1},{4,6},{5,7},{6,4},{7,5},{8,10},{9,11},{10,... | collective-permute-start | bytes 393224 | tf_op jit(solution)/shard_map/ppermute | solution.py:507
  98.6 6.6 %collective-permute-start.14 = (bf16[128,512]{1,0:T(8,128)(2,1)S(1)}, bf16[128,512]{1,0:T(8,128)(2,1)S(1)}, u32[]{:S(2)}, u32[]{:S(2)}) collective-permute-start(bf16[128,512]{1,0:T(8,128)(2,1)S(1)} %get-tuple-element.40), channel_id=1, source_target_pairs={{0,3},{1,0},{2,1},{3,2},{4,7},{5,4},{6,5},{7,6},{8,11},{9,8},{10,9... | collective-permute-start | bytes 393224 | tf_op jit(solution)/shard_map/ppermute | solution.py:507

commit v6 on v5

--- a/solution.py
+++ b/solution.py
@@ -419,7 +419,7 @@
                 pltpu.VMEM((QSPANS * 8, COLS), F32),
                 pltpu.SemaphoreType.DMA((8,)),
             ],
-            compiler_params=LARGE,
+            compiler_params=SMALL,
             cost_estimate=pl.CostEstimate(
                 flops=1 << 30, bytes_accessed=1 << 22, transcendentals=1 << 22
             ),

time: 107 us -> 103 us (0.963)
  Pallas kernels: 28.7 us -> 26.1 us
  local copies, waits for them, and re-layouts: 5.23 us -> 3.13 us
  starting transfers between devices: 37.6 us -> 39.5 us
    pallas_call x2, Pallas kernels: 9.15 us -> 6.05 us  [stats_of(): pl.pallas_call(functools.partial(stats_kernel, spans, steps), out_shape=[...]
    unnamed x30 -> x44, local copies, waits for them, and re-layouts: 3.42 us -> 1.91 us
    ppermute x3, starting transfers between devices: 9.7 us -> 10.9 us  [local(): own = own + lax.ppermute(pieces[s - 1], 'tp', pairs).astype(F32)]
  transfers between devices with their start and end apart: 17 -> 17, of which waited for: 9 -> 10; matrix products, arithmetic and copies ran while one was open for 3% -> 3% of each run, Pallas kernels for 16% -> 14%
where the time goes in v6:
time: 103 us
  starting transfers between devices  39.5 us (38%)
  waiting for transfers between devices  29.1 us (28%)
  Pallas kernels  26.1 us (25%)
  other arithmetic  4.52 us (4%)
  local copies, waits for them, and re-layouts  3.13 us (3%)
    pallas_call x2, Pallas kernels, grads_of(): pl.pallas_call(functools.partial(grads_kernel, spans, steps, last), out_s...  15.2 us
    all_to_all x2, waiting for transfers between devices, exchanged(): lax.all_to_all(array, 'ctx', 0, 0, tiled=True, axis_index_groups=groups)  13.1 us
    all_to_all x2, starting transfers between devices, exchanged(): lax.all_to_all(array, 'ctx', 0, 0, tiled=True, axis_index_groups=groups)  12.1 us
    ppermute x3, starting transfers between devices, local(): own = own + lax.ppermute(pieces[s - 1], 'tp', pairs).astype(F32)  10.9 us
    ppermute x9, starting transfers between devices, shifted(): lax.ppermute(array, 'ctx', [(device(a, b, c), device(a, b, c + by)) for a...  10.2 us
    ppermute x9, waiting for transfers between devices, shifted(): lax.ppermute(array, 'ctx', [(device(a, b, c), device(a, b, c + by)) for a...  9.07 us
    ppermute x3, waiting for transfers between devices, local(): own = own + lax.ppermute(pieces[s - 1], 'tp', pairs).astype(F32)  6.51 us
    ppermute x3, starting transfers between devices, crossed(): lax.ppermute(array, 'ctx', [(device(a, b, c), device(a + 1, b, c)) for a,...  6.15 us
  transfers between devices with their start and end apart: 17, of which 10 were waited for; matrix products, arithmetic and copies ran while one was open for 3% of the time, Pallas kernels for 14%

profile of v6, /device:TPU:1, one launch (start us, length us, event | category | flops | bytes accessed | tf_op | source)
XLA Modules:
  0.0 102.7 jit_solution(9300089760113242001)
XLA Ops:
  0.0 2.2 %pack.1 = (bf16[2048,128]{1,0:T(8,128)(2,1)}, bf16[512,256]{1,0:T(8,128)(2,1)}, f32[24,256]{1,0:T(8,128)}) custom-call(bf16[128,128]{1,0:T(8,128)(2,1)} %k_ref.1, bf16[128,128]{1,0:T(8,128)(2,1)} %v_ref.1, bf16[128,512]{1,0:T(8,128)(2,1)} %q_ref.1, bf16[128,512]{1,0:T(8,128)(2,1)} %g_ref.1, bf16[128,512]{1,0:T(8,128)(2,1)} %o_ref.1), custom_call_target="tpu_custom_call" | custom-call | tf_op jit(solution)/shard_map/pack/pallas_call | solution.py:387
  2.2 3.3 %collective-permute-start.2 = (bf16[512,256]{1,0:T(8,128)(2,1)}, bf16[512,256]{1,0:T(8,128)(2,1)S(1)}, u32[]{:S(2)}, u32[]{:S(2)}) collective-permute-start(bf16[512,256]{1,0:T(8,128)(2,1)} %get-tuple-element.24.b0.refs_3_), channel_id=1, source_target_pairs={{0,12},{4,0},{8,4},{12,8},{16,28},{20,16},{24,20},{28,24},{32,44},... | collective-permute-start | bytes 786440 | tf_op jit(solution)/shard_map/ppermute | solution.py:382
  6.1 0.6 collective-permute-start
  6.7 8.2 %all-to-all-start = ((bf16[8,256,128]{2,1,0:T(8,128)(2,1)}), bf16[8,256,128]{2,1,0:T(8,128)(2,1)S(1)}, u32[]{:S(2)}, u32[]{:S(2)}) async-start(bf16[8,256,128]{2,1,0:T(8,128)(2,1)} %bitcast.15), calls=%async_computation | async-start | bytes 1048576 | tf_op jit(solution)/shard_map/all_to_all | solution.py:379
  14.9 0.8 reshape.127
  15.8 0.9 select_reduce_fusion.2
  17.7 13.1 %all-to-all-done = bf16[8,256,128]{2,1,0:T(8,128)(2,1)S(1)} async-done(((bf16[8,256,128]{2,1,0:T(8,128)(2,1)}), bf16[8,256,128]{2,1,0:T(8,128)(2,1)S(1)}, u32[]{:S(2)}, u32[]{:S(2)}) %all-to-all-start) | async-done | bytes 524320 | tf_op jit(solution)/shard_map/all_to_all | solution.py:379
  30.9 3.0 %collective-permute-start.3 = (bf16[1024,128]{1,0:T(8,128)(2,1)S(1)}, bf16[1024,128]{1,0:T(8,128)(2,1)S(1)}, u32[]{:S(2)}, u32[]{:S(2)}) collective-permute-start(bf16[1024,128]{1,0:T(8,128)(2,1)S(1)} %bitcast.11), channel_id=1, source_target_pairs={{0,128},{4,132},{8,136},{12,140},{16,144},{20,148},{24,152},{28,15... | collective-permute-start | bytes 786440 | tf_op jit(solution)/shard_map/ppermute | solution.py:385
  34.0 3.1 %stats.2 = (f32[24,256]{1,0:T(8,128)S(1)}, bf16[4096,128]{1,0:T(8,128)(2,1)S(1)}) custom-call(s32[92]{0:T(128)S(1)} %get-tuple-element.54.meta.refs_0_, bf16[1024,128]{1,0:T(8,128)(2,1)S(1)} %bitcast.12, bf16[512,256]{1,0:T(8,128)(2,1)S(1)} %copy-done.9, bf16[512,256]{1,0:T(8,128)(2,1)S(1)} %collective-permute-done.b1.refs_4_, ...), custom_call_target="tpu_custom_call" | custom-call | flops 1073741824 | bytes 4194304 | tf_op jit(solution)/shard_map/stats/pallas_call | solution.py:407
  37.7 3.0 %stats.3.refs_7_ = f32[24,256]{1,0:T(8,128)S(1)} custom-call(s32[92]{0:T(128)S(1)} %get-tuple-element.53.meta.refs_0_, bf16[1024,128]{1,0:T(8,128)(2,1)S(1)} %collective-permute-done.3.k_ref.refs_1_, bf16[512,256]{1,0:T(8,128)(2,1)S(1)} %copy-done.9, bf16[512,256]{1,0:T(8,128)(2,1)S(1)} %collective-permute-done.b1.refs_4_, ...), custom_call_target="tpu_custom_call" | custom-call | flops 1073741824 | bytes 4194304 | tf_op jit(solution)/shard_map/stats/pallas_call | solution.py:407
  40.7 2.2 %collective-permute-start.6 = (f32[24,256]{1,0:T(8,128)S(1)}, f32[24,256]{1,0:T(8,128)S(1)}, u32[]{:S(2)}, u32[]{:S(2)}) collective-permute-start(f32[24,256]{1,0:T(8,128)S(1)} %stats.3.refs_7_), channel_id=1, source_target_pairs={{0,12},{4,0},{8,4},{12,8},{16,28},{20,16},{24,20},{28,24},{32,44},... | collective-permute-start | bytes 73736 | tf_op jit(solution)/shard_map/ppermute | solution.py:382
  42.9 1.2 %collective-permute-start.5 = (f32[24,256]{1,0:T(8,128)S(1)}, f32[24,256]{1,0:T(8,128)S(1)}, u32[]{:S(2)}, u32[]{:S(2)}) collective-permute-start(f32[24,256]{1,0:T(8,128)S(1)} %stats.3.refs_7_), channel_id=1, source_target_pairs={{0,8},{4,12},{8,0},{12,4},{16,24},{20,28},{24,16},{28,20},{32,40},... | collective-permute-start | bytes 73736 | tf_op jit(solution)/shard_map/ppermute | solution.py:382
  44.5 2.8 %collective-permute-done.5.refs_9_ = f32[24,256]{1,0:T(8,128)S(1)} collective-permute-done((f32[24,256]{1,0:T(8,128)S(1)}, f32[24,256]{1,0:T(8,128)S(1)}, u32[]{:S(2)}, u32[]{:S(2)}) %collective-permute-start.5) | collective-permute-done | bytes 24608 | tf_op jit(solution)/shard_map/ppermute | solution.py:382
  47.3 0.7 collective-permute-done.4.refs_8_
  48.0 0.6 copy-done.21
  48.6 7.2 %grads.2 = (bf16[2048,128]{1,0:T(8,128)(2,1)}, f32[1024,256]{1,0:T(8,128)}) custom-call(s32[92]{0:T(128)} %copy-done.6, bf16[1024,128]{1,0:T(8,128)(2,1)} %copy-done.13, bf16[1024,128]{1,0:T(8,128)(2,1)} %copy-done.17, bf16[512,256]{1,0:T(8,128)(2,1)} %get-tuple-element.24.b0.refs_3_, bf16[512,256]{1,0:T(8,128)(2,1)} %copy-done.12, ...), custom_call_target="tpu_custom_call" | custom-call | flops 2147483648 | bytes 8388608 | tf_op jit(solution)/shard_map/grads/pallas_call | solution.py:436
  55.9 3.0 %collective-permute-start.11 = (bf16[2048,128]{1,0:T(8,128)(2,1)}, bf16[2048,128]{1,0:T(8,128)(2,1)S(1)}, u32[]{:S(2)}, u32[]{:S(2)}) collective-permute-start(bf16[2048,128]{1,0:T(8,128)(2,1)} %get-tuple-element.35), channel_id=1, source_target_pairs={{0,128},{4,132},{8,136},{12,140},{16,144},{20,148},{24,152},{28,15... | collective-permute-start | bytes 1572872 | tf_op jit(solution)/shard_map/ppermute | solution.py:385
  58.9 7.9 %grads.3 = (bf16[2048,128]{1,0:T(8,128)(2,1)}, f32[128,512]{1,0:T(8,128)}, bf16[128,512]{1,0:T(8,128)(2,1)}, bf16[128,512]{1,0:T(8,128)(2,1)}, bf16[128,512]{1,0:T(8,128)(2,1)}) custom-call(s32[92]{0:T(128)} %copy-done.5, bf16[1024,128]{1,0:T(8,128)(2,1)} %bitcast.13, bf16[1024,128]{1,0:T(8,128)(2,1)} %bitcast.17, ...), custom_call_target="tpu_custom_call" | custom-call | flops 2147483648 | bytes 8388608 | tf_op jit(solution)/shard_map/grads/pallas_call | solution.py:436
  66.9 2.2 %add_convert_fusion = bf16[2048,128]{1,0:T(8,128)(2,1)} fusion(bf16[2048,128]{1,0:T(8,128)(2,1)S(1)} %collective-permute-done.11, bf16[2048,128]{1,0:T(8,128)(2,1)} %get-tuple-element.34), kind=kLoop, calls=%fused_computation | loop fusion | flops 1048576 | bytes 1572864 | tf_op jit(solution)/shard_map/convert_element_type | solution.py:486
  69.0 4.0 %all-to-all-start.1 = ((bf16[8,256,128]{2,1,0:T(8,128)(2,1)}), bf16[8,256,128]{2,1,0:T(8,128)(2,1)S(1)}, u32[]{:S(2)}, u32[]{:S(2)}) async-start(bf16[8,256,128]{2,1,0:T(8,128)(2,1)} %bitcast.6), calls=%async_computation.1 | async-start | bytes 1048576 | tf_op jit(solution)/shard_map/all_to_all | solution.py:379
  73.0 0.7 collective-permute-start.8
  74.3 0.8 collective-permute-start.10
  75.0 2.0 %collective-permute-done.8.d1 = bf16[128,512]{1,0:T(8,128)(2,1)S(1)} collective-permute-done((bf16[128,512]{1,0:T(8,128)(2,1)}, bf16[128,512]{1,0:T(8,128)(2,1)S(1)}, u32[]{:S(2)}, u32[]{:S(2)}) %collective-permute-start.8) | collective-permute-done | bytes 131104 | tf_op jit(solution)/shard_map/ppermute | solution.py:382
  77.0 2.3 %collective-permute-done.9.d2 = bf16[128,512]{1,0:T(8,128)(2,1)S(1)} collective-permute-done((bf16[128,512]{1,0:T(8,128)(2,1)}, bf16[128,512]{1,0:T(8,128)(2,1)S(1)}, u32[]{:S(2)}, u32[]{:S(2)}) %collective-permute-start.9) | collective-permute-done | bytes 131104 | tf_op jit(solution)/shard_map/ppermute | solution.py:382
  79.3 1.3 %collective-permute-done.10.d3 = bf16[128,512]{1,0:T(8,128)(2,1)S(1)} collective-permute-done((bf16[128,512]{1,0:T(8,128)(2,1)S(1)}, bf16[128,512]{1,0:T(8,128)(2,1)S(1)}, u32[]{:S(2)}, u32[]{:S(2)}) %collective-permute-start.10) | collective-permute-done | bytes 131104 | tf_op jit(solution)/shard_map/ppermute | solution.py:382
  80.6 1.2 %copy-done.2 = bf16[4096,128]{1,0:T(8,128)(2,1)S(1)} copy-done((bf16[4096,128]{1,0:T(8,128)(2,1)S(1)}, bf16[4096,128]{1,0:T(8,128)(2,1)}, u32[]{:S(2)}) %copy-start.2) | copy-done | bytes 1048600
  81.8 2.6 %project.1 = (f32[128,512]{1,0:T(8,128)S(1)}, bf16[128,512]{1,0:T(8,128)(2,1)S(1)}, bf16[128,512]{1,0:T(8,128)(2,1)S(1)}, bf16[128,512]{1,0:T(8,128)(2,1)S(1)}) custom-call(s32[4]{0:T(128)S(1)} %and_select_fusion.3.peers, f32[128,512]{1,0:T(8,128)S(1)} %copy-done.3, bf16[128,512]{1,0:T(8,128)(2,1)S(1)} %collective-permute-done.8.d1, ...), custom_call_target="tpu_custom_call" | custom-call | tf_op jit(solution)/shard_map/project/pallas_call | solution.py:490
  84.5 10.4 %collective-permute-start.12 = (bf16[128,512]{1,0:T(8,128)(2,1)S(1)}, bf16[128,512]{1,0:T(8,128)(2,1)S(1)}, u32[]{:S(2)}, u32[]{:S(2)}) collective-permute-start(bf16[128,512]{1,0:T(8,128)(2,1)S(1)} %get-tuple-element.38), channel_id=1, source_target_pairs={{0,1},{1,2},{2,3},{3,0},{4,5},{5,6},{6,7},{7,4},{8,9},{9,10},{10,1... | collective-permute-start | bytes 393224 | tf_op jit(solution)/shard_map/ppermute | solution.py:507
  95.4 2.2 %collective-permute-done.12 = bf16[128,512]{1,0:T(8,128)(2,1)S(1)} collective-permute-done((bf16[128,512]{1,0:T(8,128)(2,1)S(1)}, bf16[128,512]{1,0:T(8,128)(2,1)S(1)}, u32[]{:S(2)}, u32[]{:S(2)}) %collective-permute-start.12) | collective-permute-done | bytes 131104 | tf_op jit(solution)/shard_map/ppermute | solution.py:507
  97.6 3.7 %collective-permute-done.13 = bf16[128,512]{1,0:T(8,128)(2,1)S(1)} collective-permute-done((bf16[128,512]{1,0:T(8,128)(2,1)S(1)}, bf16[128,512]{1,0:T(8,128)(2,1)S(1)}, u32[]{:S(2)}, u32[]{:S(2)}) %collective-permute-start.13) | collective-permute-done | bytes 131104 | tf_op jit(solution)/shard_map/ppermute | solution.py:507
  101.3 0.6 collective-permute-done.14
  101.9 0.7 add_convert_fusion.1
  (74 shorter events, 3.8 us)
Async XLA Ops:
  0.0 33.9 %copy-start.8 = (bf16[2048,128]{1,0:T(8,128)(2,1)S(1)}, bf16[2048,128]{1,0:T(8,128)(2,1)}, u32[]{:S(2)}) copy-start(bf16[2048,128]{1,0:T(8,128)(2,1)} %refs_1_.1) | copy-start | bytes 1572868
  0.0 33.9 %copy-start.7 = (bf16[2048,128]{1,0:T(8,128)(2,1)S(1)}, bf16[2048,128]{1,0:T(8,128)(2,1)}, u32[]{:S(2)}) copy-start(bf16[2048,128]{1,0:T(8,128)(2,1)} %refs_0_.1) | copy-start | bytes 1572868
  2.2 31.7 %copy-start.9 = (bf16[512,256]{1,0:T(8,128)(2,1)S(1)}, bf16[512,256]{1,0:T(8,128)(2,1)}, u32[]{:S(2)}) copy-start(bf16[512,256]{1,0:T(8,128)(2,1)} %get-tuple-element.24.b0.refs_3_) | copy-start | bytes 786436
  2.2 31.7 %copy-start.14 = (f32[24,256]{1,0:T(8,128)S(1)}, f32[24,256]{1,0:T(8,128)}, u32[]{:S(2)}) copy-start(f32[24,256]{1,0:T(8,128)} %get-tuple-element.25.before) | copy-start | bytes 73732
  2.2 31.6 %collective-permute-start.2 = (bf16[512,256]{1,0:T(8,128)(2,1)}, bf16[512,256]{1,0:T(8,128)(2,1)S(1)}, u32[]{:S(2)}, u32[]{:S(2)}) collective-permute-start(bf16[512,256]{1,0:T(8,128)(2,1)} %get-tuple-element.24.b0.refs_3_), channel_id=1, source_target_pairs={{0,12},{4,0},{8,4},{12,8},{16,28},{20,16},{24,20},{28,24},{32,44},... | collective-permute-start | bytes 786440 | tf_op jit(solution)/shard_map/ppermute | solution.py:382
  5.5 28.4 %collective-permute-start.1 = (bf16[512,256]{1,0:T(8,128)(2,1)}, bf16[512,256]{1,0:T(8,128)(2,1)S(1)}, u32[]{:S(2)}, u32[]{:S(2)}) collective-permute-start(bf16[512,256]{1,0:T(8,128)(2,1)} %get-tuple-element.24.b0.refs_3_), channel_id=1, source_target_pairs={{0,8},{4,12},{8,0},{12,4},{16,24},{20,28},{24,16},{28,20},{32,40},... | collective-permute-start | bytes 786440 | tf_op jit(solution)/shard_map/ppermute | solution.py:382
  6.1 27.9 %collective-permute-start = (bf16[512,256]{1,0:T(8,128)(2,1)}, bf16[512,256]{1,0:T(8,128)(2,1)S(1)}, u32[]{:S(2)}, u32[]{:S(2)}) collective-permute-start(bf16[512,256]{1,0:T(8,128)(2,1)} %get-tuple-element.24.b0.refs_3_), channel_id=1, source_target_pairs={{0,4},{4,8},{8,12},{12,0},{16,20},{20,24},{24,28},{28,16},{32,36},... | collective-permute-start | bytes 786440 | tf_op jit(solution)/shard_map/ppermute | solution.py:382
  6.7 24.1 %all-to-all-start = ((bf16[8,256,128]{2,1,0:T(8,128)(2,1)}), bf16[8,256,128]{2,1,0:T(8,128)(2,1)S(1)}, u32[]{:S(2)}, u32[]{:S(2)}) async-start(bf16[8,256,128]{2,1,0:T(8,128)(2,1)} %bitcast.15), calls=%async_computation | async-start | bytes 1048576 | tf_op jit(solution)/shard_map/all_to_all | solution.py:379
  30.9 6.2 %copy-start.4 = (bf16[8,1,128,128]{3,2,1,0:T(8,128)(2,1)}, bf16[8,1,128,128]{3,2,1,0:T(8,128)(2,1)S(1)}, u32[]{:S(2)}) copy-start(bf16[8,1,128,128]{3,2,1,0:T(8,128)(2,1)S(1)} %get-tuple-element.50) | copy-start | bytes 786436
  30.9 6.3 %copy-start.16 = (bf16[8,1,128,128]{3,2,1,0:T(8,128)(2,1)}, bf16[8,1,128,128]{3,2,1,0:T(8,128)(2,1)S(1)}, u32[]{:S(2)}) copy-start(bf16[8,1,128,128]{3,2,1,0:T(8,128)(2,1)S(1)} %get-tuple-element.49) | copy-start | bytes 786436
  30.9 6.8 %collective-permute-start.3 = (bf16[1024,128]{1,0:T(8,128)(2,1)S(1)}, bf16[1024,128]{1,0:T(8,128)(2,1)S(1)}, u32[]{:S(2)}, u32[]{:S(2)}) collective-permute-start(bf16[1024,128]{1,0:T(8,128)(2,1)S(1)} %bitcast.11), channel_id=1, source_target_pairs={{0,128},{4,132},{8,136},{12,140},{16,144},{20,148},{24,152},{28,15... | collective-permute-start | bytes 786440 | tf_op jit(solution)/shard_map/ppermute | solution.py:385
  33.9 3.8 %copy-start.6 = (s32[92]{0:T(128)}, s32[92]{0:T(128)S(1)}, u32[]{:S(2)}) copy-start(s32[92]{0:T(128)S(1)} %get-tuple-element.53.meta.refs_0_) | copy-start | bytes 1108
  33.9 3.8 %copy-start.10 = (bf16[512,256]{1,0:T(8,128)(2,1)}, bf16[512,256]{1,0:T(8,128)(2,1)S(1)}, u32[]{:S(2)}) copy-start(bf16[512,256]{1,0:T(8,128)(2,1)S(1)} %collective-permute-done.2.b3.refs_6_) | copy-start | bytes 786436
  33.9 3.8 %copy-start.11 = (bf16[512,256]{1,0:T(8,128)(2,1)}, bf16[512,256]{1,0:T(8,128)(2,1)S(1)}, u32[]{:S(2)}) copy-start(bf16[512,256]{1,0:T(8,128)(2,1)S(1)} %collective-permute-done.1.b2.refs_5_) | copy-start | bytes 786436
  33.9 3.8 %copy-start.12 = (bf16[512,256]{1,0:T(8,128)(2,1)}, bf16[512,256]{1,0:T(8,128)(2,1)S(1)}, u32[]{:S(2)}) copy-start(bf16[512,256]{1,0:T(8,128)(2,1)S(1)} %collective-permute-done.b1.refs_4_) | copy-start | bytes 786436
  37.1 3.6 %copy-start.1 = (bf16[4096,128]{1,0:T(8,128)(2,1)}, bf16[4096,128]{1,0:T(8,128)(2,1)S(1)}, u32[]{:S(2)}) copy-start(bf16[4096,128]{1,0:T(8,128)(2,1)S(1)} %get-tuple-element.36.narrow_ref) | copy-start | bytes 3145732
  37.1 7.4 %collective-permute-start.7 = (bf16[1024,128]{1,0:T(8,128)(2,1)S(1)}, bf16[1024,128]{1,0:T(8,128)(2,1)S(1)}, u32[]{:S(2)}, u32[]{:S(2)}) collective-permute-start(bf16[1024,128]{1,0:T(8,128)(2,1)S(1)} %bitcast.16), channel_id=1, source_target_pairs={{0,128},{4,132},{8,136},{12,140},{16,144},{20,148},{24,152},{28,15... | collective-permute-start | bytes 786440 | tf_op jit(solution)/shard_map/ppermute | solution.py:385
  40.7 7.3 %copy-start.15 = (f32[24,256]{1,0:T(8,128)}, f32[24,256]{1,0:T(8,128)S(1)}, u32[]{:S(2)}) copy-start(f32[24,256]{1,0:T(8,128)S(1)} %stats.3.refs_7_) | copy-start | bytes 73732
  40.7 3.8 %collective-permute-start.6 = (f32[24,256]{1,0:T(8,128)S(1)}, f32[24,256]{1,0:T(8,128)S(1)}, u32[]{:S(2)}, u32[]{:S(2)}) collective-permute-start(f32[24,256]{1,0:T(8,128)S(1)} %stats.3.refs_7_), channel_id=1, source_target_pairs={{0,12},{4,0},{8,4},{12,8},{16,28},{20,16},{24,20},{28,24},{32,44},... | collective-permute-start | bytes 73736 | tf_op jit(solution)/shard_map/ppermute | solution.py:382
  42.9 4.5 %collective-permute-start.5 = (f32[24,256]{1,0:T(8,128)S(1)}, f32[24,256]{1,0:T(8,128)S(1)}, u32[]{:S(2)}, u32[]{:S(2)}) collective-permute-start(f32[24,256]{1,0:T(8,128)S(1)} %stats.3.refs_7_), channel_id=1, source_target_pairs={{0,8},{4,12},{8,0},{12,4},{16,24},{20,28},{24,16},{28,20},{32,40},... | collective-permute-start | bytes 73736 | tf_op jit(solution)/shard_map/ppermute | solution.py:382
  44.1 3.9 %collective-permute-start.4 = (f32[24,256]{1,0:T(8,128)S(1)}, f32[24,256]{1,0:T(8,128)S(1)}, u32[]{:S(2)}, u32[]{:S(2)}) collective-permute-start(f32[24,256]{1,0:T(8,128)S(1)} %stats.3.refs_7_), channel_id=1, source_target_pairs={{0,4},{4,8},{8,12},{12,0},{16,20},{20,24},{24,28},{28,16},{32,36},... | collective-permute-start | bytes 73736 | tf_op jit(solution)/shard_map/ppermute | solution.py:382
  55.9 11.0 %collective-permute-start.11 = (bf16[2048,128]{1,0:T(8,128)(2,1)}, bf16[2048,128]{1,0:T(8,128)(2,1)S(1)}, u32[]{:S(2)}, u32[]{:S(2)}) collective-permute-start(bf16[2048,128]{1,0:T(8,128)(2,1)} %get-tuple-element.35), channel_id=1, source_target_pairs={{0,128},{4,132},{8,136},{12,140},{16,144},{20,148},{24,152},{28,15... | collective-permute-start | bytes 1572872 | tf_op jit(solution)/shard_map/ppermute | solution.py:385
  66.8 7.5 %copy-start.18 = (bf16[128,512]{1,0:T(8,128)(2,1)S(1)}, bf16[128,512]{1,0:T(8,128)(2,1)}, u32[]{:S(2)}) copy-start(bf16[128,512]{1,0:T(8,128)(2,1)} %get-tuple-element.33) | copy-start | bytes 393220
  66.8 13.8 %copy-start = (bf16[2048,512]{1,0:T(8,128)(2,1)S(1)}, bf16[2048,512]{1,0:T(8,128)(2,1)}, u32[]{:S(2)}) copy-start(bf16[2048,512]{1,0:T(8,128)(2,1)} %wq_ref.1) | copy-start | bytes 6291460
  66.8 13.8 %copy-start.3 = (f32[128,512]{1,0:T(8,128)S(1)}, f32[128,512]{1,0:T(8,128)}, u32[]{:S(2)}) copy-start(f32[128,512]{1,0:T(8,128)} %get-tuple-element.30.d0) | copy-start | bytes 786436
  69.0 11.6 %all-to-all-start.1 = ((bf16[8,256,128]{2,1,0:T(8,128)(2,1)}), bf16[8,256,128]{2,1,0:T(8,128)(2,1)S(1)}, u32[]{:S(2)}, u32[]{:S(2)}) async-start(bf16[8,256,128]{2,1,0:T(8,128)(2,1)} %bitcast.6), calls=%async_computation.1 | async-start | bytes 1048576 | tf_op jit(solution)/shard_map/all_to_all | solution.py:379
  73.0 4.0 %collective-permute-start.8 = (bf16[128,512]{1,0:T(8,128)(2,1)}, bf16[128,512]{1,0:T(8,128)(2,1)S(1)}, u32[]{:S(2)}, u32[]{:S(2)}) collective-permute-start(bf16[128,512]{1,0:T(8,128)(2,1)} %get-tuple-element.31), channel_id=1, source_target_pairs={{0,12},{4,0},{8,4},{12,8},{16,28},{20,16},{24,20},{28,24},{32,44},... | collective-permute-start | bytes 393224 | tf_op jit(solution)/shard_map/ppermute | solution.py:382
  73.7 5.6 %collective-permute-start.9 = (bf16[128,512]{1,0:T(8,128)(2,1)}, bf16[128,512]{1,0:T(8,128)(2,1)S(1)}, u32[]{:S(2)}, u32[]{:S(2)}) collective-permute-start(bf16[128,512]{1,0:T(8,128)(2,1)} %get-tuple-element.32), channel_id=1, source_target_pairs={{0,8},{4,12},{8,0},{12,4},{16,24},{20,28},{24,16},{28,20},{32,40},... | collective-permute-start | bytes 393224 | tf_op jit(solution)/shard_map/ppermute | solution.py:382
  74.3 6.3 %collective-permute-start.10 = (bf16[128,512]{1,0:T(8,128)(2,1)S(1)}, bf16[128,512]{1,0:T(8,128)(2,1)S(1)}, u32[]{:S(2)}, u32[]{:S(2)}) collective-permute-start(bf16[128,512]{1,0:T(8,128)(2,1)S(1)} %copy-done.18), channel_id=1, source_target_pairs={{0,4},{4,8},{8,12},{12,0},{16,20},{20,24},{24,28},{28,16},{32,36},... | collective-permute-start | bytes 393224 | tf_op jit(solution)/shard_map/ppermute | solution.py:382
  84.5 13.1 %collective-permute-start.12 = (bf16[128,512]{1,0:T(8,128)(2,1)S(1)}, bf16[128,512]{1,0:T(8,128)(2,1)S(1)}, u32[]{:S(2)}, u32[]{:S(2)}) collective-permute-start(bf16[128,512]{1,0:T(8,128)(2,1)S(1)} %get-tuple-element.38), channel_id=1, source_target_pairs={{0,1},{1,2},{2,3},{3,0},{4,5},{5,6},{6,7},{7,4},{8,9},{9,10},{10,1... | collective-permute-start | bytes 393224 | tf_op jit(solution)/shard_map/ppermute | solution.py:507
  94.9 6.4 %collective-permute-start.13 = (bf16[128,512]{1,0:T(8,128)(2,1)S(1)}, bf16[128,512]{1,0:T(8,128)(2,1)S(1)}, u32[]{:S(2)}, u32[]{:S(2)}) collective-permute-start(bf16[128,512]{1,0:T(8,128)(2,1)S(1)} %get-tuple-element.39), channel_id=1, source_target_pairs={{0,2},{1,3},{2,0},{3,1},{4,6},{5,7},{6,4},{7,5},{8,10},{9,11},{10,... | collective-permute-start | bytes 393224 | tf_op jit(solution)/shard_map/ppermute | solution.py:507
  95.4 6.6 %collective-permute-start.14 = (bf16[128,512]{1,0:T(8,128)(2,1)S(1)}, bf16[128,512]{1,0:T(8,128)(2,1)S(1)}, u32[]{:S(2)}, u32[]{:S(2)}) collective-permute-start(bf16[128,512]{1,0:T(8,128)(2,1)S(1)} %get-tuple-element.40), channel_id=1, source_target_pairs={{0,3},{1,0},{2,1},{3,2},{4,7},{5,4},{6,5},{7,6},{8,11},{9,8},{10,9... | collective-permute-start | bytes 393224 | tf_op jit(solution)/shard_map/ppermute | solution.py:507
  (7 other events, 15.7 us)
